TPU v7x, 32 devices: a whole 2x2x4 slice. The times are simulated.
32 devices in a mesh: seq: 4 (over x, core), blk: 8 (over z, y).
Axes of the slice: x: 2, y: 2, z: 4, core: 2. Of those that a mesh axis runs over, the one named last changes fastest.
Arguments:
- inputs: bfloat16 [32768, 1024], P(('seq', 'blk')), may hold values from -11 to 11
- cotangent: bfloat16 [32768, 1024], P(('seq', 'blk')), may hold values from -6 to 6
- timestep: int32 [4], P('seq'), may hold values from 0 to 4999
- lengths: int32 [4, 32], P('seq'), may hold values from 1 to 512, 8192 in all within a row
- padding: int32 [32768], P(('seq', 'blk')), may hold values 0 or 1
- time_weight: bfloat16 [1024], P(('seq', 'blk')), may hold values from -6 to 6
- time_bias: bfloat16 [1024], P(('seq', 'blk')), may hold values from -3 to 3
- inproj_weight: bfloat16 [1024, 3072], P(('seq', 'blk')), may hold values from -0.1875 to 0.1875
- query_bias: bfloat16 [1024], P(('seq', 'blk')), may hold values from -1.75 to 1.75
- value_bias: bfloat16 [1024], P(('seq', 'blk')), may hold values from -3 to 3
- outproj_weight: bfloat16 [1024, 1024], P(('seq', 'blk')), may hold values from -0.5 to 0.5
- outproj_bias: bfloat16 [1024], P(('seq', 'blk')), may hold values from -3 to 3
- first_gain: bfloat16 [1024], P(('seq', 'blk')), may hold values from 0.25 to 1.75
- first_shift: bfloat16 [1024], P(('seq', 'blk')), may hold values from -1.75 to 1.75
- upward_weight: bfloat16 [1024, 4096], P(('seq', 'blk')), may hold values from -0.1875 to 0.1875
- upward_bias: bfloat16 [4096], P(('seq', 'blk')), may hold values from -3 to 3
- downward_weight: bfloat16 [4096, 1024], P(('seq', 'blk')), may hold values from -0.09375 to 0.09375
- downward_bias: bfloat16 [1024], P(('seq', 'blk')), may hold values from -3 to 3
- second_gain: bfloat16 [1024], P(('seq', 'blk')), may hold values from 0.25 to 1.75
- second_shift: bfloat16 [1024], P(('seq', 'blk')), may hold values from -1.75 to 1.75
Outputs:
- layer_out: bfloat16 [32768, 1024], P(('seq', 'blk'))
- input_grad: bfloat16 [32768, 1024], P(('seq', 'blk'))
- time_weight_grad: float32 [1024], P(('seq', 'blk'))
- time_bias_grad: float32 [1024], P(('seq', 'blk'))
- inproj_weight_grad: float32 [1024, 3072], P(('seq', 'blk'))
- query_bias_grad: float32 [1024], P(('seq', 'blk'))
- value_bias_grad: float32 [1024], P(('seq', 'blk'))
- outproj_weight_grad: float32 [1024, 1024], P(('seq', 'blk'))
- outproj_bias_grad: float32 [1024], P(('seq', 'blk'))
- first_gain_grad: float32 [1024], P(('seq', 'blk'))
- first_shift_grad: float32 [1024], P(('seq', 'blk'))
- upward_weight_grad: float32 [1024, 4096], P(('seq', 'blk'))
- upward_bias_grad: float32 [4096], P(('seq', 'blk'))
- downward_weight_grad: float32 [4096, 1024], P(('seq', 'blk'))
- downward_bias_grad: float32 [1024], P(('seq', 'blk'))
- second_gain_grad: float32 [1024], P(('seq', 'blk'))
- second_shift_grad: float32 [1024], P(('seq', 'blk'))
- branch_rms: float32 [3], replicated
Inputs may be any that keep to these rules, and one draw needn't show every extreme that they name: `lengths`: each row sums to 8192, and its longest item has exactly 512 tokens.
All inputs are finite; a program needn't handle non-finite values. No bound on the sum of `padding` on one device may be relied on, other than what follows from the above.
Results may differ from a plain program's by a relative error of at most 0.014.
The roundings to bfloat16 on the way count: a program that leaves them out, or rounds other values in their place, can miss the bound.
Values may be sent and summed in bfloat16 or wider, within the bound.
A program may use at most 384 MiB of HBM per device.

v0:
```python
import jax
import jax.numpy as jnp
from jax import lax
from jax.sharding import PartitionSpec as P

H = 16
HD = 64
MAXLEN = 512
TSTEPS = 5000


NEG_FILL = -1e30
WEIGHT_NAMES = (
    "time_weight",
    "time_bias",
    "inproj_weight",
    "query_bias",
    "value_bias",
    "outproj_weight",
    "outproj_bias",
    "first_gain",
    "first_shift",
    "upward_weight",
    "upward_bias",
    "downward_weight",
    "downward_bias",
    "second_gain",
    "second_shift",
)


def extended(block, sides, width):
    for axis, dim in sides:
        count = lax.axis_size(axis)
        forward = [(i, i + 1) for i in range(count - 1)]
        backward = [(target, source) for source, target in forward]
        low = lax.ppermute(
            lax.slice_in_dim(block, block.shape[dim] - width, None, axis=dim), axis, forward
        )
        high = lax.ppermute(lax.slice_in_dim(block, 0, width, axis=dim), axis, backward)
        block = jnp.concatenate([low, block, high], axis=dim)
    return block


def layer_norm(values, gain, shift):
    mean_val = jnp.mean(values, axis=-1, keepdims=True)
    centered = values - mean_val
    spread_val = jnp.mean(centered * centered, axis=-1, keepdims=True)
    return centered * lax.rsqrt(spread_val + 1e-05) * gain + shift


def exact_gelu(values):
    return jax.nn.gelu(values, approximate=False)


def item_of(ends, places):
    return jnp.sum((ends[None, :] <= places[:, None]).astype(jnp.int32), axis=1)


def row_dot(left, right):
    return lax.dot_general(
        left, right, (((0,), (0,)), ((), ())), preferred_element_type=jnp.float32
    )


def back_dot(left, right):
    return lax.dot_general(
        left, right, (((1,), (1,)), ((), ())), preferred_element_type=jnp.float32
    )


def as_float(value):
    return value.astype(jnp.float32)


def per_device(
    inputs,
    cotangent,
    timestep,
    lengths,
    padding,
    time_weight,
    time_bias,
    inproj_weight,
    query_bias,
    value_bias,
    outproj_weight,
    outproj_bias,
    first_gain,
    first_shift,
    upward_weight,
    upward_bias,
    downward_weight,
    downward_bias,
    second_gain,
    second_shift,
):
    shards = (
        time_weight,
        time_bias,
        inproj_weight,
        query_bias,
        value_bias,
        outproj_weight,
        outproj_bias,
        first_gain,
        first_shift,
        upward_weight,
        upward_bias,
        downward_weight,
        downward_bias,
        second_gain,
        second_shift,
    )
    full = dict(
        zip(
            WEIGHT_NAMES,
            (
                lax.all_gather(shards[0], ("seq", "blk"), axis=0, tiled=True),
                lax.all_gather(shards[1], ("seq", "blk"), axis=0, tiled=True),
                lax.all_gather(shards[2], ("seq", "blk"), axis=0, tiled=True),
                lax.all_gather(shards[3], ("seq", "blk"), axis=0, tiled=True),
                lax.all_gather(shards[4], ("seq", "blk"), axis=0, tiled=True),
                lax.all_gather(shards[5], ("seq", "blk"), axis=0, tiled=True),
                lax.all_gather(shards[6], ("seq", "blk"), axis=0, tiled=True),
                lax.all_gather(shards[7], ("seq", "blk"), axis=0, tiled=True),
                lax.all_gather(shards[8], ("seq", "blk"), axis=0, tiled=True),
                lax.all_gather(shards[9], ("seq", "blk"), axis=0, tiled=True),
                lax.all_gather(shards[10], ("seq", "blk"), axis=0, tiled=True),
                lax.all_gather(shards[11], ("seq", "blk"), axis=0, tiled=True),
                lax.all_gather(shards[12], ("seq", "blk"), axis=0, tiled=True),
                lax.all_gather(shards[13], ("seq", "blk"), axis=0, tiled=True),
                lax.all_gather(shards[14], ("seq", "blk"), axis=0, tiled=True),
            ),
        )
    )
    tok_rows = inputs.shape[0]
    width = inputs.shape[1]
    span = MAXLEN
    blocks = tok_rows // span
    scale = HD ** (-0.5)
    offset = lax.axis_index("blk") * tok_rows
    ends = jnp.cumsum(lengths[0])
    query_place = offset + jnp.arange(tok_rows, dtype=jnp.int32)
    key_place = offset - span + jnp.arange(tok_rows + 2 * span, dtype=jnp.int32)
    query_item = item_of(ends, query_place)
    key_item = jnp.where(key_place >= 0, item_of(ends, key_place), -1)
    time_value = as_float(timestep[0]) / TSTEPS
    start_vec = (
        as_float(inputs) + time_value * as_float(full["time_weight"]) + as_float(full["time_bias"])
    )
    start_low = start_vec.astype(jnp.bfloat16)
    zero_bias = jnp.zeros((width,), jnp.float32)
    proj_bias = jnp.concatenate(
        [as_float(full["query_bias"]), zero_bias, as_float(full["value_bias"])]
    )
    projected = (
        jnp.dot(start_low, full["inproj_weight"], preferred_element_type=jnp.float32) + proj_bias
    ).astype(jnp.bfloat16)
    query_low = projected[:, :width].reshape(tok_rows, H, HD)
    pair_low = projected[:, width:]
    pair_ext, keep_ext = (
        extended(pair_low, (("blk", 0),), MAXLEN),
        extended(padding.astype(jnp.bfloat16), (("blk", 0),), MAXLEN),
    )
    key_ext = pair_ext[:, :width].reshape(tok_rows + 2 * span, H, HD)
    value_ext = pair_ext[:, width:].reshape(tok_rows + 2 * span, H, HD)

    def block_inputs(index):
        begin = index * span
        query_blk = lax.dynamic_slice_in_dim(query_low, begin, span, 0)
        key_win = lax.dynamic_slice_in_dim(key_ext, begin, 3 * span, 0)
        value_win = lax.dynamic_slice_in_dim(value_ext, begin, 3 * span, 0)
        q_item = lax.dynamic_slice_in_dim(query_item, begin, span, 0)
        k_item = lax.dynamic_slice_in_dim(key_item, begin, 3 * span, 0)
        k_keep = lax.dynamic_slice_in_dim(keep_ext, begin, 3 * span, 0)
        q_place = lax.dynamic_slice_in_dim(query_place, begin, span, 0)
        k_place = lax.dynamic_slice_in_dim(key_place, begin, 3 * span, 0)
        allowed = (q_item[:, None] == k_item[None, :]) & (
            (k_keep[None, :] > 0.5) | (q_place[:, None] == k_place[None, :])
        )
        score = (
            jnp.einsum("qhd,khd->hqk", query_blk, key_win, preferred_element_type=jnp.float32)
            * scale
        )
        masked = jnp.where(allowed[None], score, NEG_FILL)
        return (query_blk, key_win, value_win, masked)

    def forward_block(index):
        query_blk, key_win, value_win, masked = block_inputs(index)
        row_top = jnp.max(masked, axis=-1, keepdims=True)
        expo_vals = jnp.exp(masked - row_top)
        denom = jnp.sum(expo_vals, axis=-1, keepdims=True)
        probs_low = (expo_vals / denom).astype(jnp.bfloat16)
        result = jnp.einsum(
            "hqk,khd->qhd", probs_low, value_win, preferred_element_type=jnp.float32
        )
        return (result.reshape(span, width).astype(jnp.bfloat16), row_top + jnp.log(denom))

    attended_blocks, log_totals = lax.map(forward_block, jnp.arange(blocks, dtype=jnp.int32))
    attended_low = attended_blocks.reshape(tok_rows, width)
    attn_branch = jnp.dot(
        attended_low, full["outproj_weight"], preferred_element_type=jnp.float32
    ) + as_float(full["outproj_bias"])
    first_in = start_vec + attn_branch
    first_gain_f = as_float(full["first_gain"])
    first_shift_f = as_float(full["first_shift"])
    first_out = layer_norm(first_in, first_gain_f, first_shift_f)
    first_low = first_out.astype(jnp.bfloat16)
    upward = jnp.dot(
        first_low, full["upward_weight"], preferred_element_type=jnp.float32
    ) + as_float(full["upward_bias"])
    hidden_low = exact_gelu(upward).astype(jnp.bfloat16)
    ffn_branch = jnp.dot(
        hidden_low, full["downward_weight"], preferred_element_type=jnp.float32
    ) + as_float(full["downward_bias"])
    second_in = first_out + ffn_branch
    second_gain_f = as_float(full["second_gain"])
    second_shift_f = as_float(full["second_shift"])
    layer_out = layer_norm(second_in, second_gain_f, second_shift_f).astype(jnp.bfloat16)
    local_sums = jnp.stack(
        [
            jnp.sum(start_vec * start_vec),
            jnp.sum(attn_branch * attn_branch),
            jnp.sum(ffn_branch * ffn_branch),
        ]
    )
    total_sums = lax.psum(local_sums, ("seq", "blk"))
    branch_rms = jnp.sqrt(total_sums / (tok_rows * width * lax.axis_size(("seq", "blk"))))
    grad_cot = as_float(cotangent)
    grad_second_in, grad_second_gain, grad_second_shift = jax.vjp(
        layer_norm, second_in, second_gain_f, second_shift_f
    )[1](grad_cot)
    grad_ffn_low = grad_second_in.astype(jnp.bfloat16)
    grad_down_weight = row_dot(hidden_low, grad_ffn_low)
    grad_down_bias = jnp.sum(as_float(grad_ffn_low), axis=0)
    grad_hidden = back_dot(grad_ffn_low, full["downward_weight"])
    grad_upward = jax.vjp(exact_gelu, upward)[1](grad_hidden)[0]
    grad_up_low = grad_upward.astype(jnp.bfloat16)
    grad_up_weight = row_dot(first_low, grad_up_low)
    grad_up_bias = jnp.sum(as_float(grad_up_low), axis=0)
    grad_first = grad_second_in + back_dot(grad_up_low, full["upward_weight"])
    ffn_grads = (
        grad_up_weight,
        grad_up_bias,
        grad_down_weight,
        grad_down_bias,
        grad_second_gain,
        grad_second_shift,
    )
    grad_first_in, grad_first_gain, grad_first_shift = jax.vjp(
        layer_norm, first_in, first_gain_f, first_shift_f
    )[1](grad_first)
    grad_branch_low = grad_first_in.astype(jnp.bfloat16)
    grad_out_weight = row_dot(attended_low, grad_branch_low)
    grad_out_bias = jnp.sum(as_float(grad_branch_low), axis=0)
    grad_attended = (
        back_dot(grad_branch_low, full["outproj_weight"])
        .astype(jnp.bfloat16)
        .reshape(tok_rows, H, HD)
    )

    def backward_block(index):
        query_blk, key_win, value_win, masked = block_inputs(index)
        grad_out_blk = lax.dynamic_slice_in_dim(grad_attended, index * span, span, 0)
        probs = jnp.exp(masked - log_totals[index])
        probs_low = probs.astype(jnp.bfloat16)
        grad_probs = jnp.einsum(
            "qhd,khd->hqk", grad_out_blk, value_win, preferred_element_type=jnp.float32
        )
        delta_sum = jnp.sum(probs * grad_probs, axis=-1, keepdims=True)
        grad_score = (probs * (grad_probs - delta_sum)).astype(jnp.bfloat16)
        grad_query = (
            jnp.einsum("hqk,khd->qhd", grad_score, key_win, preferred_element_type=jnp.float32)
            * scale
        )
        grad_key = (
            jnp.einsum("hqk,qhd->khd", grad_score, query_blk, preferred_element_type=jnp.float32)
            * scale
        )
        grad_value = jnp.einsum(
            "hqk,qhd->khd", probs_low, grad_out_blk, preferred_element_type=jnp.float32
        )
        grad_pair = jnp.concatenate(
            [grad_key.reshape(3 * span, width), grad_value.reshape(3 * span, width)], axis=1
        )
        return (grad_query.reshape(span, width), grad_pair)

    grad_query_blocks, grad_pair_wins = lax.map(backward_block, jnp.arange(blocks, dtype=jnp.int32))
    parts = grad_pair_wins.reshape(blocks, 3, span, 2 * width)
    pieces = jnp.zeros((blocks + 2, span, 2 * width), jnp.float32)
    pieces = (
        pieces.at[:blocks]
        .add(parts[:, 0])
        .at[1 : blocks + 1]
        .add(parts[:, 1])
        .at[2:]
        .add(parts[:, 2])
    )
    pieces = pieces.reshape((blocks + 2) * span, 2 * width)
    outward = jnp.concatenate([pieces[:span], pieces[-span:]], axis=0)
    returned = extended(outward.astype(jnp.bfloat16), (("blk", 0),), MAXLEN).astype(outward.dtype)
    grad_pair_own = pieces[span : span + tok_rows]
    grad_pair_own = (
        grad_pair_own.at[:span].add(returned[:span]).at[tok_rows - span :].add(returned[3 * span :])
    )
    grad_proj_low = jnp.concatenate(
        [grad_query_blocks.reshape(tok_rows, width), grad_pair_own], axis=1
    ).astype(jnp.bfloat16)
    grad_in_weight = row_dot(start_low, grad_proj_low)
    grad_proj_sums = jnp.sum(as_float(grad_proj_low), axis=0)
    grad_query_bias = grad_proj_sums[:width]
    grad_value_bias = grad_proj_sums[2 * width :]
    grad_start = grad_first_in + back_dot(grad_proj_low, full["inproj_weight"])
    grad_time_bias = jnp.sum(grad_start, axis=0)
    grad_time_weight = time_value * grad_time_bias
    input_grad = grad_start.astype(jnp.bfloat16)
    attn_grads = (
        grad_time_weight,
        grad_time_bias,
        grad_in_weight,
        grad_query_bias,
        grad_value_bias,
        grad_out_weight,
        grad_out_bias,
        grad_first_gain,
        grad_first_shift,
    )
    shares = lax.psum_scatter(
        attn_grads + ffn_grads, ("seq", "blk"), scatter_dimension=0, tiled=True
    )
    return (
        layer_out,
        input_grad,
        shares[0],
        shares[1],
        shares[2],
        shares[3],
        shares[4],
        shares[5],
        shares[6],
        shares[7],
        shares[8],
        shares[9],
        shares[10],
        shares[11],
        shares[12],
        shares[13],
        shares[14],
        branch_rms,
    )


def solution(mesh):
    in_specs = (
        P(("seq", "blk"), None),
        P(("seq", "blk"), None),
        P("seq"),
        P("seq", None),
        P(("seq", "blk")),
        P(("seq", "blk")),
        P(("seq", "blk")),
        P(("seq", "blk"), None),
        P(("seq", "blk")),
        P(("seq", "blk")),
        P(("seq", "blk"), None),
        P(("seq", "blk")),
        P(("seq", "blk")),
        P(("seq", "blk")),
        P(("seq", "blk"), None),
        P(("seq", "blk")),
        P(("seq", "blk"), None),
        P(("seq", "blk")),
        P(("seq", "blk")),
        P(("seq", "blk")),
    )
    out_specs = (
        P(("seq", "blk"), None),
        P(("seq", "blk"), None),
        P(("seq", "blk")),
        P(("seq", "blk")),
        P(("seq", "blk"), None),
        P(("seq", "blk")),
        P(("seq", "blk")),
        P(("seq", "blk"), None),
        P(("seq", "blk")),
        P(("seq", "blk")),
        P(("seq", "blk")),
        P(("seq", "blk"), None),
        P(("seq", "blk")),
        P(("seq", "blk"), None),
        P(("seq", "blk")),
        P(("seq", "blk")),
        P(("seq", "blk")),
        P(),
    )
    return jax.shard_map(
        per_device, mesh=mesh, in_specs=in_specs, out_specs=out_specs, check_vma=False
    )
```

profile of v0, /device:TPU:0, one launch (start us, length us, event | category | flops | bytes accessed | tf_op | source)
XLA Modules:
  0.0 2091.6 jit_solution(13179972312955816410)
XLA Ops:
  17.8 42.6 %all-reduce.23 = (bf16[1024]{0:T(1024)(128)(2,1)S(1)}, bf16[1024]{0:T(1024)(128)(2,1)S(1)}, bf16[1024]{0:T(1024)(128)(2,1)S(1)}, bf16[1024]{0:T(1024)(128)(2,1)S...) all-reduce(bf16[1024]{0:T(1024)(128)(2,1)S(1)} %dynamic-update-slic, ...), channel_id=1, replica_groups=mesh['seq'=4,'blk'=8] {'seq','blk'}, use_global_device_ids=true, to_apply=%add.4 | all-reduce | flops 10240 | bytes 40960
  64.1 19.2 all-gather.6.cloned.1.call-done
  83.3 10.1 add_convert_fusion.1
  97.6 4.7 collective-permute-start
  103.6 4.5 collective-permute-start.2
  109.8 147.2 %all-gather = bf16[32,1,128]{2,1,0:T(2,128)(2,1)S(1)} all-gather(bf16[1,1,128]{2,1,0:T(2,128)(2,1)S(1)} %bitcast.121), channel_id=1, replica_groups=mesh['seq'=4,'blk'=8] {'seq','blk'}, dimensions={0}, use_global_device_ids=true | all-gather | bytes 8448 | tf_op jit(solution)/shard_map/all_gather | solution.py:129
  264.0 4.8 slice.205
  274.7 4.4 pad_maximum_fusion
  283.0 6.5 copy.87
  289.5 6.7 copy.90
  296.2 144.8 %while.29 = (s32[]{:T(128)}, bf16[2,512,1024]{2,1,0:T(8,128)(2,1)}, f32[2,16,512,1]{2,1,3,0:T(8,128)S(1)}, s32[2]{0:T(128)S(1)}, bf16[2048,16,64]{0,2,1:T(8,128)...) while((s32[]{:T(128)}, bf16[2,512,1024]{2,1,0:T(8,128)(2,1)}, ...), condition=%wide.region_6.7_spmd, body=%wide.region_3.6_spmd.sunk | while | flops 3375886848 | bytes 167041808 | solution.py:200
  298.7 20.9 fusion.120
  319.6 22.4 %fusion.121 = f32[16,512]{1,0:T(8,128)S(1)} fusion(f32[16,512,1536]{2,1,0:T(8,128)} %get-tuple-element.584, f32[16,512]{1,0:T(8,128)S(1)} %get-tuple-element.585, pred[512,1536]{1,0:T(8,128)(4,1)S(1)} %or_and_fusion.4), kind=kLoop, calls=%fused_computation.4.clone.1 | loop fusion | flops 50323456 | bytes 51183616 | tf_op jit(solution)/shard_map/while/body/eval_jaxpr/reduce_sum | solution.py:193
  342.0 22.5 %fusion.122 = bf16[16,64,512]{2,1,0:T(8,128)(2,1)} fusion(f32[16,512,1536]{2,1,0:T(8,128)} %get-tuple-element.584, f32[16,512]{1,0:T(8,128)S(1)} %fusion.121, f32[16,512]{1,0:T(8,128)S(1)} %get-tuple-element.585, pred[512,1536]{1,0:T(8,128)(4,1)S(1)} %or_and_fusion.4, bf16[2048,16,64]{0,2,1:T(8,128)(2,1)} %get-tuple-element.640, s32[]{:T(128)S(6)} %select_n.75), kind=kOutput, calls=%fused_computation.10.clone.1 | convolution fusion | flops 1674051584 | bytes 55377924 | tf_op jit(solution)/shard_map/while/body/eval_jaxpr/hqk,khd->qhd/dot_general | solution.py:195
  371.6 20.0 fusion.120
  391.6 22.0 %fusion.121 = f32[16,512]{1,0:T(8,128)S(1)} fusion(f32[16,512,1536]{2,1,0:T(8,128)} %get-tuple-element.584, f32[16,512]{1,0:T(8,128)S(1)} %get-tuple-element.585, pred[512,1536]{1,0:T(8,128)(4,1)S(1)} %or_and_fusion.4), kind=kLoop, calls=%fused_computation.4.clone.1 | loop fusion | flops 50323456 | bytes 51183616 | tf_op jit(solution)/shard_map/while/body/eval_jaxpr/reduce_sum | solution.py:193
  413.7 22.4 %fusion.122 = bf16[16,64,512]{2,1,0:T(8,128)(2,1)} fusion(f32[16,512,1536]{2,1,0:T(8,128)} %get-tuple-element.584, f32[16,512]{1,0:T(8,128)S(1)} %fusion.121, f32[16,512]{1,0:T(8,128)S(1)} %get-tuple-element.585, pred[512,1536]{1,0:T(8,128)(4,1)S(1)} %or_and_fusion.4, bf16[2048,16,64]{0,2,1:T(8,128)(2,1)} %get-tuple-element.640, s32[]{:T(128)S(6)} %select_n.75), kind=kOutput, calls=%fused_computation.10.clone.1 | convolution fusion | flops 1674051584 | bytes 55377924 | tf_op jit(solution)/shard_map/while/body/eval_jaxpr/hqk,khd->qhd/dot_general | solution.py:195
  441.1 7.7 fusion.73
  451.6 47.9 %multiply_convert_fusion.1 = (bf16[1024,4096]{1,0:T(8,128)(2,1)}, f32[1024,4096]{1,0:T(8,128)}, f32[1024,4096]{1,0:T(8,128)}) fusion(f32[4096]{0:T(1024)S(1)} %bitcast.118, bf16[1024,4096]{1,0:T(8,128)(2,1)} %all-gather.10.cloned.1.call-done, bf16[1024,1024]{0,1:T(8,128)(2,1)S(1)} %fusion.68.clone.4), kind=kOutput, calls=%fused_computation.54 | convolution fusion | flops 8866758656 | bytes 52445184 | tf_op jit(solution)/shard_map/dot_general | solution.py:210
  499.5 16.3 fusion.71
  515.8 5.2 fusion.49
  524.2 4.3 convert_reduce_fusion.3
  528.4 24.8 %convert_reduce_fusion = (f32[4096]{0:T(1024)}, bf16[1024,4096]{1,0:T(8,128)(2,1)}) fusion(f32[1024,4096]{1,0:T(8,128)} %get-tuple-element.409, f32[1024,4096]{1,0:T(8,128)} %get-tuple-element.432, f32[4096]{0:T(1024)S(1)} %bitcast.119, bf16[1024,1024]{0,1:T(8,128)(2,1)} %get-tuple-element.399, bf16[4096,1024]{1,0:T(8,128)(2,1)} %all-gather.12.cloned.1.call-done), kind=kOutput, calls=%fused_computation.52 | convolution fusion | flops 8661233664 | bytes 52461568 | tf_op jit(solution)/shard_map/dot_general | solution.py:67
  553.2 17.2 multiply_reduce_fusion.4
  576.0 4.4 fusion.80
  580.4 6.0 convolution_convert_fusion
  586.5 390.7 %while.30 = (s32[]{:T(128)}, bf16[2,512,1024]{2,1,0:T(8,128)(2,1)}, f32[2,1536,2048]{2,1,0:T(8,128)}, s32[2]{0:T(128)S(1)}, bf16[2048,16,64]{0,2,1:T(8,128)(2,1)...) while((s32[]{:T(128)}, bf16[2,512,1024]{2,1,0:T(8,128)(2,1)}, ...), condition=%wide.region_17.18_spmd, body=%wide.region_15.17_spmd.sunk | while | flops 8250716672 | bytes 496262624 | solution.py:289
  588.0 21.2 %fusion.131 = f32[16,512,1536]{2,1,0:T(8,128)} fusion(bf16[2048,16,64]{0,2,1:T(8,128)(2,1)} %get-tuple-element.697, s32[]{:T(128)S(6)} %select_n.80, bf16[1024,16,64]{0,2,1:T(8,128)(2,1)S(1)} %get-tuple-element.703, s32[]{:T(128)S(6)} %select_n.81), kind=kOutput, calls=%fused_computation.32.clone.1 | convolution fusion | flops 1610612736 | bytes 54525960 | tf_op jit(solution)/shard_map/while/body/eval_jaxpr/qhd,khd->hqk/dot_general | solution.py:183
  612.4 37.2 %multiply_reduce_fusion.9 = (f32[16,512]{1,0:T(8,128)S(1)}, f32[16,512,1536]{2,1,0:T(8,128)}) fusion(f32[16,512,1536]{2,1,0:T(8,128)} %fusion.131, f32[16,512]{1,0:T(8,128)S(1)} %dynamic-slice_bitcast_fusion.2, pred[512,1536]{1,0:T(8,128)(4,1)S(1)} %or_and_fusion.5, bf16[2048,16,64]{0,2,1:T(8,128)(2,1)} %get-tuple-element.706, s32[]{:T(128)S(6)} %select_n.80, ...), kind=kOutput, calls=%fused_computation.20.clone.1 | convolution fusion | flops 1673519104 | bytes 105709576 | tf_op jit(solution)/shard_map/while/body/eval_jaxpr/qhd,khd->hqk/dot_general | solution.py:268
  649.6 41.1 %multiply_convert_fusion.3 = bf16[16,512,1536]{2,1,0:T(8,128)(2,1)} fusion(f32[16,512,1536]{2,1,0:T(8,128)} %get-tuple-element.600, f32[16,512,1536]{2,1,0:T(8,128)} %fusion.131, f32[16,512]{1,0:T(8,128)S(1)} %get-tuple-element.601, f32[16,512]{1,0:T(8,128)S(1)} %dynamic-slice_bitcast_fusion.2, pred[512,1536]{1,0:T(8,128)(4,1)S(1)} %or_and_fusion.5), kind=kLoop, calls=%fused_computation.19.clone.1 | loop fusion | flops 75497472 | bytes 126681088 | tf_op jit(solution)/shard_map/while/body/eval_jaxpr/convert_element_type | solution.py:272
  690.7 15.2 convolution_multiply_fusion.2
  705.9 23.0 %fusion.133 = f32[16,64,1536]{2,1,0:T(8,128)} fusion(f32[16,512,1536]{2,1,0:T(8,128)} %fusion.131, f32[16,512]{1,0:T(8,128)S(1)} %dynamic-slice_bitcast_fusion.2, pred[512,1536]{1,0:T(8,128)(4,1)S(1)} %or_and_fusion.5, bf16[1024,16,64]{0,2,1:T(8,128)(2,1)S(1)} %copy-done.11, s32[]{:T(128)S(6)} %select_n.81), kind=kOutput, calls=%fused_computation.23.clone.1 | convolution fusion | flops 1660944384 | bytes 58490884 | tf_op jit(solution)/shard_map/while/body/eval_jaxpr/hqk,qhd->khd/dot_general | solution.py:281
  728.8 10.4 maximum_bitcast_fusion.2
  739.2 12.7 copy.139
  751.9 11.2 constant_dynamic-update-slice_fusion.9
  763.1 14.1 fusion.132
  783.0 21.2 %fusion.131 = f32[16,512,1536]{2,1,0:T(8,128)} fusion(bf16[2048,16,64]{0,2,1:T(8,128)(2,1)} %get-tuple-element.697, s32[]{:T(128)S(6)} %select_n.80, bf16[1024,16,64]{0,2,1:T(8,128)(2,1)S(1)} %get-tuple-element.703, s32[]{:T(128)S(6)} %select_n.81), kind=kOutput, calls=%fused_computation.32.clone.1 | convolution fusion | flops 1610612736 | bytes 54525960 | tf_op jit(solution)/shard_map/while/body/eval_jaxpr/qhd,khd->hqk/dot_general | solution.py:183
  807.5 37.1 %multiply_reduce_fusion.9 = (f32[16,512]{1,0:T(8,128)S(1)}, f32[16,512,1536]{2,1,0:T(8,128)}) fusion(f32[16,512,1536]{2,1,0:T(8,128)} %fusion.131, f32[16,512]{1,0:T(8,128)S(1)} %dynamic-slice_bitcast_fusion.2, pred[512,1536]{1,0:T(8,128)(4,1)S(1)} %or_and_fusion.5, bf16[2048,16,64]{0,2,1:T(8,128)(2,1)} %get-tuple-element.706, s32[]{:T(128)S(6)} %select_n.80, ...), kind=kOutput, calls=%fused_computation.20.clone.1 | convolution fusion | flops 1673519104 | bytes 105709576 | tf_op jit(solution)/shard_map/while/body/eval_jaxpr/qhd,khd->hqk/dot_general | solution.py:268
  844.6 41.1 %multiply_convert_fusion.3 = bf16[16,512,1536]{2,1,0:T(8,128)(2,1)} fusion(f32[16,512,1536]{2,1,0:T(8,128)} %get-tuple-element.600, f32[16,512,1536]{2,1,0:T(8,128)} %fusion.131, f32[16,512]{1,0:T(8,128)S(1)} %get-tuple-element.601, f32[16,512]{1,0:T(8,128)S(1)} %dynamic-slice_bitcast_fusion.2, pred[512,1536]{1,0:T(8,128)(4,1)S(1)} %or_and_fusion.5), kind=kLoop, calls=%fused_computation.19.clone.1 | loop fusion | flops 75497472 | bytes 126681088 | tf_op jit(solution)/shard_map/while/body/eval_jaxpr/convert_element_type | solution.py:272
  885.7 15.2 convolution_multiply_fusion.2
  900.8 23.0 %fusion.133 = f32[16,64,1536]{2,1,0:T(8,128)} fusion(f32[16,512,1536]{2,1,0:T(8,128)} %fusion.131, f32[16,512]{1,0:T(8,128)S(1)} %dynamic-slice_bitcast_fusion.2, pred[512,1536]{1,0:T(8,128)(4,1)S(1)} %or_and_fusion.5, bf16[1024,16,64]{0,2,1:T(8,128)(2,1)S(1)} %copy-done.11, s32[]{:T(128)S(6)} %select_n.81), kind=kOutput, calls=%fused_computation.23.clone.1 | convolution fusion | flops 1660944384 | bytes 58490884 | tf_op jit(solution)/shard_map/while/body/eval_jaxpr/hqk,qhd->khd/dot_general | solution.py:281
  923.8 10.4 maximum_bitcast_fusion.2
  934.2 12.7 copy.139
  946.9 11.3 constant_dynamic-update-slice_fusion.9
  958.2 14.1 fusion.132
  977.2 7.7 slice_bitcast_fusion.2
  984.9 11.3 scatter-add.16
  996.3 11.8 fusion.46
  1008.2 11.7 fusion.44
  1019.9 7.7 constant_dynamic-update-slice_fusion.3
  1033.9 4.7 collective-permute-start.4
  1038.6 4.0 slice.214
  1042.6 37.9 %collective-permute-done.5 = bf16[512,2048]{1,0:T(8,128)(2,1)S(1)} collective-permute-done((bf16[512,2048]{1,0:T(8,128)(2,1)S(1)}, bf16[512,2048]{1,0:T(8,128)(2,1)S(1)}, u32[]{:S(2)}, u32[]{:S(2)}) %collective-permute-start.5) | collective-permute-done | bytes 2097184 | tf_op jit(solution)/shard_map/ppermute | solution.py:40
  1080.5 104.1 %collective-permute-done.4 = bf16[512,2048]{1,0:T(8,128)(2,1)S(1)} collective-permute-done((bf16[512,2048]{1,0:T(8,128)(2,1)S(1)}, bf16[512,2048]{1,0:T(8,128)(2,1)S(1)}, u32[]{:S(2)}, u32[]{:S(2)}) %collective-permute-start.4) | collective-permute-done | bytes 2097184 | tf_op jit(solution)/shard_map/ppermute | solution.py:37
  1184.6 5.2 fusion.52
  1196.9 9.9 fusion.58
  1207.5 16.7 fusion.65
  1225.9 15.1 fusion.81
  1248.3 4.1 convert_reduce_fusion.1
  1252.5 10.3 fusion.77
  1263.0 45.5 %all-reduce.22 = (f32[1024]{0:T(1024)S(1)}, f32[1024]{0:T(1024)S(1)}, f32[1024]{0:T(1024)S(1)}, f32[1024]{0:T(1024)S(1)}, f32[1024]{0:T(1024)S(1)}, /*index=5*/f...) all-reduce(f32[1024]{0:T(1024)S(1)} %get-tuple-element.435, ...), channel_id=2, replica_groups=mesh['seq'=4,'blk'=8] {'seq','blk'}, use_global_device_ids=true, to_apply=%region_19.20.clone | all-reduce | flops 14339 | bytes 114712
  1317.9 46.1 %reduce-scatter.5.cloned.1.call-done = f32[32,3072]{1,0:T(8,128)} async-done(((f32[1024,3072]{1,0:T(8,128)}), f32[32,3072]{1,0:T(8,128)}) %reduce-scatter.5.cloned.1.call-update) | async-done | bytes 393232 | tf_op jit(solution)/shard_map/reduce_scatter | solution.py:329
  1364.0 360.2 %reduce-scatter.9.cloned.1.call-done = f32[32,4096]{1,0:T(8,128)} async-done(((f32[1024,4096]{1,0:T(8,128)}), f32[32,4096]{1,0:T(8,128)}) %reduce-scatter.9.cloned.1.call-update) | async-done | bytes 524304 | tf_op jit(solution)/shard_map/reduce_scatter | solution.py:329
  1724.2 360.4 %reduce-scatter.11.cloned.1.call-done = f32[128,1024]{1,0:T(8,128)} async-done(((f32[4096,1024]{1,0:T(8,128)}), f32[128,1024]{1,0:T(8,128)}) %reduce-scatter.11.cloned.1.call-update) | async-done | bytes 524304 | tf_op jit(solution)/shard_map/reduce_scatter | solution.py:329
  (297 shorter events, 107.0 us)
Async XLA Ops:
  7.2 76.1 %all-gather.6.cloned.1.call-start = ((), (), s32[]{:S(2)}) async-start(), calls=%async_computation.4 | async-start | bytes 6488064 | tf_op jit(solution)/shard_map/all_gather | solution.py:121
  7.9 433.2 %all-gather.8.cloned.1.call-start = ((), (), s32[]{:S(2)}) async-start(), calls=%async_computation.5 | async-start | bytes 2162688 | tf_op jit(solution)/shard_map/all_gather | solution.py:124
  8.7 442.9 %all-gather.10.cloned.1.call-start = ((), (), s32[]{:S(2)}) async-start(), calls=%async_computation.6 | async-start | bytes 8650752 | tf_op jit(solution)/shard_map/all_gather | solution.py:128
  9.4 490.1 %all-gather.12.cloned.1.call-start = ((), (), s32[]{:S(2)}) async-start(), calls=%async_computation.7 | async-start | bytes 8650752 | tf_op jit(solution)/shard_map/all_gather | solution.py:130
  61.1 32.3 %copy-start.55 = (f32[1024]{0:T(1024)}, f32[1024]{0:T(1024)S(1)}, u32[]{:S(2)}) copy-start(f32[1024]{0:T(1024)S(1)} %convert_element_type.127) | copy-start | bytes 12292
  64.0 19.3 copy-start.14
  64.0 19.2 copy-start.60
  93.4 10.1 copy-start.54
  93.4 16.1 copy-start.63
  93.4 16.4 copy-start.64
  93.4 167.4 %copy-start.13 = (bf16[1024,1024]{1,0:T(8,128)(2,1)S(1)}, bf16[1024,1024]{1,0:T(8,128)(2,1)}, u32[]{:S(2)}) copy-start(bf16[1024,1024]{1,0:T(8,128)(2,1)} %param.35) | copy-start | bytes 6291460
  97.6 177.2 %collective-permute-start = (bf16[512,2048]{1,0:T(8,128)(2,1)}, bf16[512,2048]{1,0:T(8,128)(2,1)}, u32[]{:S(2)}, u32[]{:S(2)}) collective-permute-start(bf16[512,2048]{1,0:T(8,128)(2,1)} %get-tuple-element.418), channel_id=1, source_target_pairs={{0,1},{1,2},{2,3},{3,4},{4,5},{5,6},{6,7},{8,9},{9,10},{10,11},{11... | collective-permute-start | bytes 6291464 | tf_op jit(solution)/shard_map/ppermute | solution.py:37
  102.3 172.5 %collective-permute-start.1 = (bf16[512,2048]{1,0:T(8,128)(2,1)}, bf16[512,2048]{1,0:T(8,128)(2,1)}, u32[]{:S(2)}, u32[]{:S(2)}) collective-permute-start(bf16[512,2048]{1,0:T(8,128)(2,1)} %get-tuple-element.419), channel_id=1, source_target_pairs={{1,0},{2,1},{3,2},{4,3},{5,4},{6,5},{7,6},{9,8},{10,9},{11,10},{12... | collective-permute-start | bytes 6291464 | tf_op jit(solution)/shard_map/ppermute | solution.py:40
  103.6 160.4 %collective-permute-start.2 = (bf16[512]{0:T(512)(128)(2,1)S(1)}, bf16[512]{0:T(512)(128)(2,1)S(1)}, u32[]{:S(2)}, u32[]{:S(2)}) collective-permute-start(bf16[512]{0:T(512)(128)(2,1)S(1)} %get-tuple-element.430), channel_id=1, source_target_pairs={{0,1},{1,2},{2,3},{3,4},{4,5},{5,6},{6,7},{8,9},{9,10},{10,11},{11... | collective-permute-start | bytes 3080 | tf_op jit(solution)/shard_map/ppermute | solution.py:37
  108.1 155.8 %collective-permute-start.3 = (bf16[512]{0:T(512)(128)(2,1)S(1)}, bf16[512]{0:T(512)(128)(2,1)S(1)}, u32[]{:S(2)}, u32[]{:S(2)}) collective-permute-start(bf16[512]{0:T(512)(128)(2,1)S(1)} %get-tuple-element.431), channel_id=1, source_target_pairs={{1,0},{2,1},{3,2},{4,3},{5,4},{6,5},{7,6},{9,8},{10,9},{11,10},{12... | collective-permute-start | bytes 3080 | tf_op jit(solution)/shard_map/ppermute | solution.py:40
  109.5 1208.5 %reduce-scatter.7.cloned.1.call-start = ((), (), s32[]{:S(2)}) async-start(), calls=%async_computation.9 | async-start | bytes 4325376 | tf_op jit(solution)/shard_map/reduce_scatter | solution.py:329
  296.2 145.0 %copy-start.56 = (f32[1024]{0:T(1024)S(1)}, f32[1024]{0:T(1024)}, u32[]{:S(2)}) copy-start(f32[1024]{0:T(1024)} %copy-done.55) | copy-start | bytes 12292
  296.2 145.0 %copy-start.59 = (f32[1024]{0:T(1024)S(1)}, f32[1024]{0:T(1024)}, u32[]{:S(2)}) copy-start(f32[1024]{0:T(1024)} %convert_element_type.135) | copy-start | bytes 12292
  296.2 145.0 %copy-start.61 = (f32[1024]{0:T(1024)S(1)}, f32[1024]{0:T(1024)}, u32[]{:S(2)}) copy-start(f32[1024]{0:T(1024)} %copy-done.60) | copy-start | bytes 12292
  441.0 7.8 copy-start
  441.0 7.8 copy-start.20
  441.0 7.8 copy-start.22
  441.0 7.8 copy-start.24
  441.1 7.8 copy-start.26
  441.1 7.8 copy-start.28
  441.1 7.8 copy-start.30
  448.9 121.5 %copy-start.32 = (f32[1024]{0:T(1024)}, f32[1024]{0:T(1024)S(1)}, u32[]{:S(2)}) copy-start(f32[1024]{0:T(1024)S(1)} %broadcast_multiply_fusion.1) | copy-start | bytes 12292
  449.4 50.1 %copy-start.39 = (f32[1024]{0:T(1024)}, f32[1024]{0:T(1024)S(1)}, u32[]{:S(2)}) copy-start(f32[1024]{0:T(1024)S(1)} %multiply_reduce_fusion.7) | copy-start | bytes 12292
  450.9 119.5 %copy-start.37 = (f32[1024]{0:T(1024)}, f32[1024]{0:T(1024)S(1)}, u32[]{:S(2)}) copy-start(f32[1024]{0:T(1024)S(1)} %fusion.59) | copy-start | bytes 12292
  451.6 47.9 %copy-start.58 = (f32[1024]{0:T(1024)S(1)}, f32[1024]{0:T(1024)}, u32[]{:S(2)}) copy-start(f32[1024]{0:T(1024)} %convert_element_type.141) | copy-start | bytes 12292
  499.5 16.3 copy-start.34
  515.8 8.4 copy-start.4
  515.8 5.2 copy-start.5
  528.4 24.8 %copy-start.3 = (f32[1024,1024]{0,1:T(8,128)S(1)}, f32[1024,1024]{0,1:T(8,128)}, u32[]{:S(2)}) copy-start(f32[1024,1024]{0,1:T(8,128)} %copy-done.2) | copy-start | bytes 12582916
  528.4 24.8 %copy-start.6 = (bf16[1024,1024]{0,1:T(8,128)(2,1)S(1)}, bf16[1024,1024]{0,1:T(8,128)(2,1)}, u32[]{:S(2)}) copy-start(bf16[1024,1024]{0,1:T(8,128)(2,1)} %copy.93) | copy-start | bytes 6291460
  553.2 17.2 copy-start.40
  580.4 6.1 copy-start.1
  580.4 6.1 copy-start.21
  580.4 6.1 copy-start.23
  580.4 6.1 copy-start.25
  580.4 6.1 copy-start.27
  580.4 6.1 copy-start.29
  580.4 6.1 copy-start.31
  586.7 22.5 %copy-start.66 = (s32[2]{0:T(128)}, s32[2]{0:T(128)S(1)}, u32[]{:S(2)}) copy-start(s32[2]{0:T(128)S(1)} %get-tuple-element.696) | copy-start | bytes 28 | tf_op jit(solution)/shard_map/while
  690.7 15.2 copy-start.11
  777.2 4.5 copy-start.67
  781.8 22.5 %copy-start.66 = (s32[2]{0:T(128)}, s32[2]{0:T(128)S(1)}, u32[]{:S(2)}) copy-start(s32[2]{0:T(128)S(1)} %get-tuple-element.696) | copy-start | bytes 28 | tf_op jit(solution)/shard_map/while
  885.7 15.2 copy-start.11
  972.3 4.6 copy-start.67
  996.3 367.8 %reduce-scatter.5.cloned.1.call-start = ((), (), s32[]{:S(2)}) async-start(), calls=%async_computation.8 | async-start | bytes 12976128 | tf_op jit(solution)/shard_map/reduce_scatter | solution.py:329
  1032.6 47.9 %collective-permute-start.5 = (bf16[512,2048]{1,0:T(8,128)(2,1)S(1)}, bf16[512,2048]{1,0:T(8,128)(2,1)S(1)}, u32[]{:S(2)}, u32[]{:S(2)}) collective-permute-start(bf16[512,2048]{1,0:T(8,128)(2,1)S(1)} %fusion.57), channel_id=1, source_target_pairs={{1,0},{2,1},{3,2},{4,3},{5,4},{6,5},{7,6},{9,8},{10,9},{11,10},{12... | collective-permute-start | bytes 6291464 | tf_op jit(solution)/shard_map/ppermute | solution.py:40
  1033.9 150.7 %collective-permute-start.4 = (bf16[512,2048]{1,0:T(8,128)(2,1)S(1)}, bf16[512,2048]{1,0:T(8,128)(2,1)S(1)}, u32[]{:S(2)}, u32[]{:S(2)}) collective-permute-start(bf16[512,2048]{1,0:T(8,128)(2,1)S(1)} %fusion.56), channel_id=1, source_target_pairs={{0,1},{1,2},{2,3},{3,4},{4,5},{5,6},{6,7},{8,9},{9,10},{10,11},{11... | collective-permute-start | bytes 6291464 | tf_op jit(solution)/shard_map/ppermute | solution.py:37
  1206.8 517.4 %reduce-scatter.9.cloned.1.call-start = ((), (), s32[]{:S(2)}) async-start(), calls=%async_computation.10 | async-start | bytes 17301504 | tf_op jit(solution)/shard_map/reduce_scatter | solution.py:329
  1224.2 860.3 %reduce-scatter.11.cloned.1.call-start = ((), (), s32[]{:S(2)}) async-start(), calls=%async_computation.11 | async-start | bytes 17301504 | tf_op jit(solution)/shard_map/reduce_scatter | solution.py:329
  1245.3 7.1 copy-start.9
  1245.3 7.1 copy-start.17
  1245.3 7.1 copy-start.47
  1252.5 10.4 copy-start.41
  1252.5 10.4 copy-start.42
  1252.5 10.4 copy-start.43
  1252.5 10.4 copy-start.49
  1252.5 10.4 copy-start.51
  1252.5 10.4 copy-start.52
  1252.5 10.4 copy-start.53
  (21 other events, 48.4 us)
Sparse Core Ops, SparseCore 0:
  10.9 72.3 all-gather.5
  86.2 96.7 all-gather.7
  186.1 76.3 all-gather.9
  265.3 76.0 all-gather.11
  996.4 182.4 reduce-scatter.6
  1207.0 157.0 reduce-scatter.4
  1367.0 357.1 reduce-scatter.8
  1727.2 357.3 reduce-scatter.10
where the time goes:
time: 2100 us; the launch traced here: 2090 us
  waiting for transfers between devices  930 us (44%)
  matrix products  493 us (23%)
  blocking collectives  235 us (11%)
  other arithmetic  217 us (10%)
  local copies, waits for them, and re-layouts  175 us (8%)
    reduce_scatter x4, waiting for transfers between devices, per_device(): lax.psum_scatter(attn_grads + ffn_grads, ('seq', 'blk'), scatter_dimensio...  767 us
    all_gather x1, blocking collectives, per_device(): lax.all_gather(shards[10], ('seq', 'blk'), axis=0, tiled=True)  147 us
    ppermute x3, waiting for transfers between devices, extended(): lax.ppermute(lax.slice_in_dim(block, block.shape[dim] - width, None, axis...  104 us
    unnamed x2, blocking collectives  88.1 us
    dot_general x4, matrix products, block_inputs(): jnp.einsum('qhd,khd->hqk', query_blk, key_win, preferred_element_type=jnp...  83.4 us
    convert_element_type x2, other arithmetic, backward_block(): grad_score = (probs * (grad_probs - delta_sum)).astype(jnp.bfloat16)  82.1 us
    dot_general x2, matrix products, backward_block(): jnp.einsum('qhd,khd->hqk', grad_out_blk, value_win, preferred_element_typ...  74.3 us
    dot_general x4, matrix products, back_dot(): lax.dot_general(left, right, (((1,), (1,)), ((), ())), preferred_element_...  58.3 us
  transfers between devices with their start and end apart: 14, of which 6 were waited for; matrix products, arithmetic and copies ran while one was open for 18% of the time, Pallas kernels for 0%

commit v1 on v0

v1 whole, which is shorter than its diff:
```python
import functools

import jax
import jax.numpy as jnp
from jax import lax
from jax.experimental import pallas as pl
from jax.experimental.pallas import tpu as pltpu
from jax.sharding import PartitionSpec as P

HD=64
TQ = 256
NEG = -(2.0 ** 100)

def nt(a, b):
    return lax.dot_general(a, b, (((1,), (1,)), ((), ())), preferred_element_type=jnp.float32)

def nn(a, b):
    return jnp.dot(a, b, preferred_element_type=jnp.float32)

def fwd_kernel(tiles, lse_lane, lo_ref, n_ref, q_ref, k_ref, v_ref, qf_ref, kf_ref, o_ref, f_ref, ka, va, qa, sb, acc):
    step = pl.program_id(0)
    ext = k_ref.shape[0]
    half = (ext - tiles * TQ) // 2

    @pl.when(step == 0)
    def _():
        ka[:, 128:] = kf_ref[...]
        va[:, 128:] = jnp.ones((ext, 128), jnp.bfloat16)
        f_ref[...] = qf_ref[half : half + tiles * TQ, :]

    ka[:, :128] = k_ref[...]
    va[:, :128] = v_ref[...]
    lane = lax.broadcasted_iota(jnp.int32, (TQ, 128), 1)
    left = lane < HD
    for t in range(tiles):
        rows = slice(half + t * TQ, half + (t + 1) * TQ)
        q = q_ref[rows, :] * jnp.bfloat16(HD ** -0.5)
        zero = jnp.zeros_like(q)
        qa[:TQ, :128] = jnp.where(left, q, zero)
        qa[TQ:, :128] = jnp.where(left, zero, q)
        qa[:TQ, 128:] = qf_ref[rows, :]
        qa[TQ:, 128:] = qf_ref[rows, :]
        lo = lo_ref[t]
        count = n_ref[t]

        def scores(j, top):
            start = pl.multiple_of((lo + j) * TQ, TQ)
            s = nt(qa[...], ka[pl.ds(start, TQ), :])
            sb[j] = s
            return jnp.maximum(top, jnp.maximum(s[:, :128], s[:, 128:]))

        top = lax.fori_loop(0, count, scores, jnp.full((2 * TQ, 128), -jnp.inf, jnp.float32))
        top = jnp.max(top, axis=1, keepdims=True)
        acc[...] = jnp.zeros_like(acc)

        def weigh(j, carry):
            start = pl.multiple_of((lo + j) * TQ, TQ)
            p = jnp.exp(sb[j] - top).astype(jnp.bfloat16)
            acc[...] += nn(p, va[pl.ds(start, TQ), :])
            return carry

        lax.fori_loop(0, count, weigh, 0)
        total = acc[:, 128:]
        o = acc[:, :128] / total
        own = slice(t * TQ, (t + 1) * TQ)
        o_ref[own, :] = jnp.where(left, o[:TQ], o[TQ:]).astype(jnp.bfloat16)
        lse = top + jnp.log(total)
        feat = f_ref[own, :]
        for side in range(2):
            rest = lse[side * TQ : (side + 1) * TQ]
            for part in range(3):
                piece = rest.astype(jnp.bfloat16)
                rest = rest - piece.astype(jnp.float32)
                at = lse_lane + part * 16 + 2 * step + side
                feat = jnp.where(lane == at, piece, feat)
        f_ref[own, :] = feat


def attn_fwd(proj, qf, kf, lo, n, lse_lane, tok):
    ext, wide = proj.shape
    width = wide // 3
    pairs = width // 128
    tiles = tok // TQ
    col = lambda base: pl.BlockSpec((ext, 128), lambda i, *_: (0, base + i))
    fix = pl.BlockSpec((ext, 128), lambda i, *_: (0, 0))
    return pl.pallas_call(
        functools.partial(fwd_kernel, tiles, lse_lane),
        grid_spec=pltpu.PrefetchScalarGridSpec(
            num_scalar_prefetch=2,
            grid=(pairs,),
            in_specs=[col(0), col(pairs), col(2 * pairs), fix, fix],
            out_specs=[pl.BlockSpec((tok, 128), lambda i, *_: (0, i)), pl.BlockSpec((tok, 128), lambda i, *_: (0, 0))],
            scratch_shapes=[
                pltpu.VMEM((ext, 256), jnp.bfloat16),
                pltpu.VMEM((ext, 256), jnp.bfloat16),
                pltpu.VMEM((2 * TQ, 256), jnp.bfloat16),
                pltpu.VMEM((6, 2 * TQ, TQ), jnp.float32),
                pltpu.VMEM((2 * TQ, 256), jnp.float32),
            ],
        ),
        out_shape=[jax.ShapeDtypeStruct((tok, width), jnp.bfloat16), jax.ShapeDtypeStruct((tok, 128), jnp.bfloat16)],
        compiler_params=pltpu.CompilerParams(vmem_limit_bytes=48 << 20, dimension_semantics=("arbitrary",)),
        cost_estimate=pl.CostEstimate(flops=2 * 2 * tok * 768 * width * 2, bytes_accessed=8 << 20, transcendentals=tok * 768 * 16),
        name="attn_fwd",
    )(lo, n, proj, proj, proj, qf, kf)


def bwd_kernel(tiles, lse_lane, lo_ref, n_ref, q_ref, k_ref, v_ref, d_ref, qf_ref, kf_ref, df_ref, vf_ref, g_ref,
               ka, va, qa, da, acc, acc2):
    step = pl.program_id(0)
    ext = k_ref.shape[0]
    half = (ext - tiles * TQ) // 2

    @pl.when(step == 0)
    def _():
        ka[:, 128:] = kf_ref[...]
        va[:, 128:] = vf_ref[...]

    ka[:, :128] = k_ref[...]
    va[:, :128] = v_ref[...]
    lane = lax.broadcasted_iota(jnp.int32, (TQ, 128), 1)
    left = lane < HD
    for side in range(2):
        mine = left if side == 0 else ~left
        own_lane = (lane - lse_lane) % 16 == 2 * step + side
        for t in range(ext // TQ):
            rows = slice(t * TQ, (t + 1) * TQ)
            zero = jnp.zeros((TQ, 128), jnp.bfloat16)
            qa[t, side * TQ : (side + 1) * TQ, :128] = jnp.where(mine, q_ref[rows, :] * jnp.bfloat16(HD ** -0.5), zero)
            qa[t, side * TQ : (side + 1) * TQ, 128:] = jnp.where((lane < lse_lane) | own_lane, qf_ref[rows, :], zero)
            da[t, side * TQ : (side + 1) * TQ, :128] = jnp.where(mine, d_ref[rows, :], zero)
            da[t, side * TQ : (side + 1) * TQ, 128:] = jnp.where(own_lane, df_ref[rows, :], zero)
    first = half // TQ
    for t in range(tiles):
        rows = slice(half + t * TQ, half + (t + 1) * TQ)
        own = slice(t * TQ, (t + 1) * TQ)
        lo = lo_ref[t]
        count = n_ref[t]
        acc[...] = jnp.zeros_like(acc)
        acc2[...] = jnp.zeros_like(acc2)

        def query_pass(j, carry):
            start = pl.multiple_of((lo + j) * TQ, TQ)
            p = jnp.exp(nt(qa[first + t], ka[pl.ds(start, TQ), :]))
            g = (p * nt(da[first + t], va[pl.ds(start, TQ), :])).astype(jnp.bfloat16)
            acc[...] += nn(g, k_ref[pl.ds(start, TQ), :])
            return carry

        lax.fori_loop(0, count, query_pass, 0)
        g_ref[0, own, :] = (jnp.where(left, acc[:TQ], acc[TQ:]) * HD ** -0.5).astype(jnp.bfloat16)

        def key_pass(j, carry):
            at = lo + j
            p = jnp.exp(nt(ka[rows, :], qa[at]))
            g = (p * nt(va[rows, :], da[at])).astype(jnp.bfloat16)
            acc2[:, :128] += nn(g, qa[at, :, :128])
            acc2[:, 128:] += nn(p.astype(jnp.bfloat16), da[at, :, :128])
            return carry

        lax.fori_loop(0, count, key_pass, 0)
        g_ref[1, own, :] = acc2[:, :128].astype(jnp.bfloat16)
        g_ref[2, own, :] = acc2[:, 128:].astype(jnp.bfloat16)


def attn_bwd(proj, grad_ext, qf, kf, df, vf, lo, n, lse_lane, tok):
    ext, wide = proj.shape
    width = wide // 3
    pairs = width // 128
    tiles = tok // TQ
    col = lambda base: pl.BlockSpec((ext, 128), lambda i, *_: (0, base + i))
    fix = pl.BlockSpec((ext, 128), lambda i, *_: (0, 0))
    return pl.pallas_call(
        functools.partial(bwd_kernel, tiles, lse_lane),
        grid_spec=pltpu.PrefetchScalarGridSpec(
            num_scalar_prefetch=2,
            grid=(pairs,),
            in_specs=[col(0), col(pairs), col(2 * pairs), col(0), fix, fix, fix, fix],
            out_specs=pl.BlockSpec((3, tok, 128), lambda i, *_: (0, 0, i)),
            scratch_shapes=[
                pltpu.VMEM((ext, 256), jnp.bfloat16),
                pltpu.VMEM((ext, 256), jnp.bfloat16),
                pltpu.VMEM((ext // TQ, 2 * TQ, 256), jnp.bfloat16),
                pltpu.VMEM((ext // TQ, 2 * TQ, 256), jnp.bfloat16),
                pltpu.VMEM((2 * TQ, 128), jnp.float32),
                pltpu.VMEM((TQ, 256), jnp.float32),
            ],
        ),
        out_shape=jax.ShapeDtypeStruct((3, tok, width), jnp.bfloat16),
        compiler_params=pltpu.CompilerParams(vmem_limit_bytes=48 << 20, dimension_semantics=("arbitrary",)),
        cost_estimate=pl.CostEstimate(flops=2 * 4 * tok * 768 * width * 2, bytes_accessed=16 << 20, transcendentals=tok * 768 * 32),
        name="attn_bwd",
    )(lo, n, proj, proj, proj, grad_ext, qf, kf, df, vf)


def bits(values, count):
    planes = (values[:, None] >> jnp.arange(count, dtype=jnp.int32)[None, :]) & 1
    return planes.astype(jnp.float32)


def features(item, keep, tok, n_items):
    ext = item.shape[0]
    nb = (n_items + 1).bit_length()
    pb = (ext - 1).bit_length()
    lse_lane = 2 * (nb + pb)
    assert lse_lane + 48 <= 128
    ib = bits(item + 1, nb)
    ps = bits(jnp.arange(ext, dtype=jnp.int32), pb)
    kept = keep.astype(jnp.float32)[:, None]
    qf = jnp.concatenate([ib, 1 - ib, ps, 1 - ps, jnp.zeros((ext, 128 - lse_lane), jnp.float32)], axis=1)
    kf = jnp.concatenate([NEG * kept * (1 - ib), NEG * kept * ib, NEG * (1 - kept) * (1 - ps), NEG * (1 - kept) * ps,
                          -jnp.ones((ext, 48), jnp.float32), jnp.zeros((ext, 80 - lse_lane), jnp.float32)], axis=1)
    return qf.astype(jnp.bfloat16), kf.astype(jnp.bfloat16), lse_lane


def stat_lanes(ext, lse_lane):
    lane = jnp.arange(128)
    vf = jnp.where((lane >= lse_lane) & (lane < lse_lane + 48), -1.0, 0.0)
    return jnp.broadcast_to(vf[None], (ext, 128)).astype(jnp.bfloat16)


def delta_features(delta, lse_lane):
    parts = []
    rest = delta
    for _ in range(3):
        piece = rest.astype(jnp.bfloat16)
        parts.append(piece)
        rest = rest - piece.astype(jnp.float32)
    return jnp.pad(jnp.concatenate(parts, axis=1), ((0, 0), (lse_lane, 80 - lse_lane)))


def key_range(ends, offset, tok, half):
    tiles = tok // TQ
    ext = tok + 2 * half
    starts = jnp.concatenate([jnp.zeros((1,), ends.dtype), ends[:-1]])
    first = offset + jnp.arange(tiles, dtype=jnp.int32) * TQ
    last = first + TQ - 1
    begin = jnp.max(jnp.where(starts[None, :] <= first[:, None], starts[None, :], 0), axis=1)
    big = jnp.int32(1 << 30)
    stop = jnp.min(jnp.where(ends[None, :] > last[:, None], ends[None, :], big), axis=1)
    begin = jnp.maximum(begin - offset + half, 0)
    stop = jnp.minimum(stop - offset + half, ext)
    lo = begin // TQ
    return lo.astype(jnp.int32), ((stop + TQ - 1) // TQ - lo).astype(jnp.int32)


H = 16
MAXLEN = 512
TSTEPS = 5000
AXES = ("seq", "blk")
SMALL = 10


def as_float(value):
    return value.astype(jnp.float32)


def low(value):
    return value.astype(jnp.bfloat16)


def row_dot(left, right):
    return lax.dot_general(left, right, (((0,), (0,)), ((), ())), preferred_element_type=jnp.float32)


def place():
    seq, blk = lax.axis_index("seq"), lax.axis_index("blk")
    return seq // 2, seq % 2, blk // 2, blk % 2


def swap(value, dx=0, dc=0, dz=0, dy=0):
    pairs = []
    for i in range(32):
        seq, blk = i // 8, i % 8
        seq, blk = seq ^ (2 * dx + dc), blk ^ (2 * dz + dy)
        pairs.append((i, seq * 8 + blk))
    return lax.ppermute(value, AXES, pairs)


def ordered(bit, own, other, axis):
    return jnp.where(bit == 0, jnp.stack([own, other], axis), jnp.stack([other, own], axis))


def cut(columns):
    return columns // 256 * 128


def gather_rows(shard):
    x, c, z, y = place()
    parts = [shard] + [swap(shard, dz=k) for k in (1, 2, 3)]
    parts = [jnp.where(z % 2 == 0, parts[i], parts[i ^ 1]) for i in range(4)]
    line = jnp.stack([jnp.where(z < 2, parts[i], parts[i ^ 2]) for i in range(4)])
    at = cut(shard.shape[1])
    one, two = line[..., :at], line[..., at:]
    one = ordered(x, one, swap(one, dx=1), 0)
    two = ordered(y, two, swap(two, dy=1), 1)
    one = ordered(y, one, swap(one, dy=1), 2)
    two = ordered(x, two, swap(two, dx=1), 0)
    mine = jnp.concatenate([one, two], axis=-1)
    return mine, swap(mine, dc=1)


def gather(shard):
    mine, other = gather_rows(shard)
    full = ordered(place()[1], mine, other, 1)
    return full.reshape(-1, shard.shape[1])


def pick(value, index, axis):
    return lax.dynamic_index_in_dim(value, index, axis, keepdims=False)


def scatter_sum(value):
    x, c, z, y = place()
    value = value.reshape(2, 2, 4, 2, value.shape[0] // 32, value.shape[1])
    total = as_float(pick(value, c, 1)) + as_float(swap(pick(value, 1 - c, 1), dc=1))
    at = cut(value.shape[-1])
    one, two = low(total[..., :at]), low(total[..., at:])
    one = low(as_float(pick(one, y, 2)) + as_float(swap(pick(one, 1 - y, 2), dy=1)))
    two = low(as_float(pick(two, x, 0)) + as_float(swap(pick(two, 1 - x, 0), dx=1)))
    one = low(as_float(pick(one, x, 0)) + as_float(swap(pick(one, 1 - x, 0), dx=1)))
    two = low(as_float(pick(two, y, 1)) + as_float(swap(pick(two, 1 - y, 1), dy=1)))
    line = jnp.concatenate([one, two], axis=-1)
    total = as_float(pick(line, z, 0))
    for k in (1, 2, 3):
        total = total + as_float(swap(pick(line, z ^ k, 0), dz=k))
    return total


def total_of(values):
    for step in (dict(dc=1), dict(dx=1), dict(dy=1), dict(dz=1), dict(dz=2)):
        values = values + swap(values, **step)
    return values


def neighbours(low_part, high_part):
    count = lax.axis_size("blk")
    up = [(i, i + 1) for i in range(count - 1)]
    down = [(i + 1, i) for i in range(count - 1)]
    return lax.ppermute(high_part, "blk", up), lax.ppermute(low_part, "blk", down)


def norm_forward(values):
    mean_val = jnp.mean(values, axis=-1, keepdims=True)
    centered = values - mean_val
    inv = lax.rsqrt(jnp.mean(centered * centered, axis=-1, keepdims=True) + 1e-05)
    return centered * inv, inv


def norm_backward(grad, normal, inv, gain):
    scaled = grad * gain
    grad_in = inv * (
        scaled
        - jnp.mean(scaled, axis=-1, keepdims=True)
        - normal * jnp.mean(scaled * normal, axis=-1, keepdims=True)
    )
    return grad_in, jnp.sum(grad * normal, axis=0), jnp.sum(grad, axis=0)


def item_of(ends, places):
    return jnp.sum((ends[None, :] <= places[:, None]).astype(jnp.int32), axis=1)


def per_device(fast, inputs, cotangent, timestep, lengths, padding, *shards):
    (time_weight, time_bias, inproj, query_bias, value_bias, outproj, outproj_bias, first_gain, first_shift,
     upward_w, upward_bias, downward_w, downward_bias, second_gain, second_shift) = shards
    small = (time_weight, time_bias, query_bias, value_bias, outproj_bias, first_gain, first_shift,
             downward_bias, second_gain, second_shift)
    tok, width = inputs.shape
    half = MAXLEN
    ext = tok + 2 * half
    hidden = upward_w.shape[1]

    mark = jnp.zeros((16, width), jnp.bfloat16)
    keep_own = low(padding)
    edge_low = jnp.concatenate([inputs[:half], mark.at[0, :half].set(keep_own[:half])])
    edge_high = jnp.concatenate([inputs[tok - half :], mark.at[0, :half].set(keep_own[tok - half :])])
    from_low, from_high = neighbours(edge_low, edge_high)

    if fast:
        rows = time_weight.shape[0]
        cols = [v[:, None] for v in small] + [upward_bias.reshape(-1, rows).T]
        cols = jnp.concatenate(cols, axis=1)
        cols = jnp.pad(cols, ((0, 0), (0, 128 - cols.shape[1])))
        first = gather(jnp.concatenate([inproj, cols], axis=1))
        second = gather(jnp.concatenate([outproj, upward_w], axis=1))
        downward_f = gather(downward_w)
        inproj_f = first[:, : 3 * width]
        small_f = as_float(first[:, 3 * width :].T)
        upward_bias_f = small_f[SMALL : SMALL + hidden // width]
        upward_bias_f = upward_bias_f.reshape(-1, width // rows, rows).transpose(1, 0, 2).reshape(hidden)
        outproj_f, upward_f = second[:, :width], second[:, width:]
    else:
        whole = lambda v: lax.all_gather(v, AXES, axis=0, tiled=True)
        inproj_f, outproj_f, upward_f, downward_f = map(whole, (inproj, outproj, upward_w, downward_w))
        small_f = [as_float(whole(v)) for v in small]
        upward_bias_f = as_float(whole(upward_bias))
    (time_weight_f, time_bias_f, query_bias_f, value_bias_f, outproj_bias_f, first_gain_f, first_shift_f,
     downward_bias_f, second_gain_f, second_shift_f) = [small_f[i] for i in range(SMALL)]

    offset = lax.axis_index("blk") * tok
    ends = jnp.cumsum(lengths[0]).astype(jnp.int32)
    places = offset - half + jnp.arange(ext, dtype=jnp.int32)
    item = jnp.where(places >= 0, item_of(ends, places), -1)
    keep = jnp.concatenate([from_low[half, :half], keep_own, from_high[half, :half]])
    query_feat, key_feat, lane = features(item, as_float(keep) > 0.5, tok, lengths.shape[1])
    lo, count = key_range(ends, offset, tok, half)

    time_value = as_float(timestep[0]) / TSTEPS
    shift = time_value * time_weight_f + time_bias_f
    start_of = lambda v: as_float(v) + time_value * time_weight_f + time_bias_f
    start_vec = start_of(inputs)
    start_low = low(start_vec)
    start_ext = jnp.concatenate([low(start_of(from_low[:half])), start_low, low(start_of(from_high[:half]))])
    proj_bias = jnp.concatenate([query_bias_f, jnp.zeros_like(query_bias_f), value_bias_f])
    projected = low(jnp.dot(start_ext, inproj_f, preferred_element_type=jnp.float32) + proj_bias)

    attended, query_feat_own = attn_fwd(projected, query_feat, key_feat, lo, count, lane, tok)
    attn_branch = jnp.dot(attended, outproj_f, preferred_element_type=jnp.float32) + outproj_bias_f
    first_normal, first_inv = norm_forward(start_vec + attn_branch)
    first_out = first_normal * first_gain_f + first_shift_f
    first_low = low(first_out)
    upward = jnp.dot(first_low, upward_f, preferred_element_type=jnp.float32) + upward_bias_f
    phi = 0.5 * (1.0 + lax.erf(upward * 2.0**-0.5))
    hidden_low = low(upward * phi)
    slope = phi + upward * (jnp.exp(-0.5 * upward * upward) * 0.3989422804014327)
    ffn_branch = jnp.dot(hidden_low, downward_f, preferred_element_type=jnp.float32) + downward_bias_f
    second_normal, second_inv = norm_forward(first_out + ffn_branch)
    layer_out = low(second_normal * second_gain_f + second_shift_f)
    sums = jnp.stack([jnp.sum(v * v) for v in (start_vec, attn_branch, ffn_branch)])
    sums = total_of(sums) if fast else lax.psum(sums, AXES)
    branch_rms = jnp.sqrt(sums / (tok * width * lax.axis_size(AXES)))

    grad_second_in, grad_second_gain, grad_second_shift = norm_backward(
        as_float(cotangent), second_normal, second_inv, second_gain_f
    )
    grad_ffn_low = low(grad_second_in)
    grad_down_weight = row_dot(hidden_low, grad_ffn_low)
    grad_down_bias = jnp.sum(as_float(grad_ffn_low), axis=0)
    grad_up_low = low(nt(grad_ffn_low, downward_f) * slope)
    grad_up_weight = row_dot(first_low, grad_up_low)
    grad_up_bias = jnp.sum(as_float(grad_up_low), axis=0)
    grad_first = grad_second_in + nt(grad_up_low, upward_f)
    grad_first_in, grad_first_gain, grad_first_shift = norm_backward(grad_first, first_normal, first_inv, first_gain_f)
    grad_branch_low = low(grad_first_in)
    grad_out_weight = row_dot(attended, grad_branch_low)
    grad_out_bias = jnp.sum(as_float(grad_branch_low), axis=0)
    grad_attended = low(nt(grad_branch_low, outproj_f))

    head = jnp.arange(width)[:, None] // HD == jnp.arange(H)[None, :]
    delta = jnp.dot(
        as_float(grad_attended) * as_float(attended), as_float(head), precision=lax.Precision.HIGHEST
    )
    stats = jnp.concatenate(
        [query_feat_own[:, lane : lane + 48], delta_features(delta, 0)[:, :48], jnp.zeros((tok, 32), jnp.bfloat16)], axis=1
    )
    packed = jnp.concatenate([grad_attended, stats], axis=1)
    back_low, back_high = neighbours(packed[:half], packed[tok - half :])
    packed = jnp.concatenate([back_low, packed, back_high])
    grad_ext = packed[:, :width]
    query_feat = jnp.concatenate([query_feat[:, :lane], packed[:, width : width + 48], query_feat[:, lane + 48 :]], axis=1)
    delta_feat = jnp.pad(packed[:, width + 48 : width + 96], ((0, 0), (lane, 80 - lane)))
    grad_proj = attn_bwd(projected, grad_ext, query_feat, key_feat, delta_feat, stat_lanes(ext, lane), lo, count, lane, tok)

    grad_proj_low = jnp.concatenate([grad_proj[0], grad_proj[1], grad_proj[2]], axis=1)
    grad_in_weight = row_dot(start_low, grad_proj_low)
    grad_query_bias = jnp.sum(as_float(grad_proj[0]), axis=0)
    grad_value_bias = jnp.sum(as_float(grad_proj[2]), axis=0)
    grad_start = grad_first_in + nt(grad_proj_low, inproj_f)
    grad_time_bias = jnp.sum(grad_start, axis=0)
    grad_time_weight = time_value * grad_time_bias
    input_grad = low(grad_start)

    small_grads = (grad_time_weight, grad_time_bias, grad_query_bias, grad_value_bias, grad_out_bias, grad_first_gain,
                   grad_first_shift, grad_down_bias, grad_second_gain, grad_second_shift)
    if fast:
        down_share = scatter_sum(low(grad_down_weight))
        up_share = scatter_sum(low(grad_up_weight))
        out_share = scatter_sum(low(grad_out_weight))
        cols = grad_up_bias.reshape(width // rows, -1, rows).transpose(1, 0, 2).reshape(-1, width)
        cols = jnp.concatenate([jnp.stack(small_grads), cols]).T
        cols = jnp.pad(cols, ((0, 0), (0, 128 - cols.shape[1])))
        last = scatter_sum(low(jnp.concatenate([grad_in_weight, cols], axis=1)))
        in_share = last[:, : 3 * width]
        small_shares = [last[:, 3 * width + i] for i in range(SMALL)]
        up_bias_share = last[:, 3 * width + SMALL : 3 * width + SMALL + hidden // width].T.reshape(-1)
    else:
        share = lambda v: lax.psum_scatter(v, AXES, scatter_dimension=0, tiled=True)
        down_share, up_share, out_share, in_share, up_bias_share = map(
            share, (grad_down_weight, grad_up_weight, grad_out_weight, grad_in_weight, grad_up_bias)
        )
        small_shares = [share(v) for v in small_grads]
    (time_weight_s, time_bias_s, query_bias_s, value_bias_s, out_bias_s, first_gain_s, first_shift_s,
     down_bias_s, second_gain_s, second_shift_s) = small_shares
    return (layer_out, input_grad, time_weight_s, time_bias_s, in_share, query_bias_s, value_bias_s, out_share,
            out_bias_s, first_gain_s, first_shift_s, up_share, up_bias_share, down_share, down_bias_s,
            second_gain_s, second_shift_s, branch_rms)


def solution(mesh):
    both = P(AXES)
    matrix = P(AXES, None)
    in_specs = (matrix, matrix, P("seq"), P("seq", None), both,
                both, both, matrix, both, both, matrix, both, both, both, matrix, both, matrix, both, both, both)
    out_specs = (matrix, matrix, both, both, matrix, both, both, matrix, both, both, both, matrix, both, matrix,
                 both, both, both, P())
    fast = dict(mesh.shape) == {"seq": 4, "blk": 8}
    return jax.shard_map(
        functools.partial(per_device, fast), mesh=mesh, in_specs=in_specs, out_specs=out_specs, check_vma=False
    )
```

time: 2100 us -> 981 us (0.47)
  waiting for transfers between devices: 930 us -> 232 us
  matrix products: 493 us -> 159 us
  blocking collectives: 235 us -> 0 us
  Pallas kernels: 0 us -> 171 us
  starting transfers between devices: 18.1 us -> 179 us
  local copies, waits for them, and re-layouts: 175 us -> 90.9 us
  other arithmetic: 217 us -> 138 us
    reduce_scatter x4 -> x0, waiting for transfers between devices: 767 us -> none  [per_device(): lax.psum_scatter(attn_grads + ffn_grads, ('seq', 'blk'), scatter_dimensio...]
    dot_general x22 -> x9, matrix products: 447 us -> 114 us  [the longest x4 50 us: nt(): lax.dot_general(a, b, (((1,), (1,)), ((), ())), preferred_element_type=jn...]
    pallas_call x0 -> x2, Pallas kernels: none -> 171 us  [the longest x1 110 us: attn_bwd(): pl.pallas_call(functools.partial(bwd_kernel, tiles, lse_lane), grid_spec=...]
    ppermute x6 -> x65, starting transfers between devices: 17.8 us -> 179 us  [the longest x61 163 us: swap(): return lax.ppermute(value, AXES, pairs)]
    all_gather x1 -> x0, blocking collectives: 147 us -> none  [per_device(): lax.all_gather(shards[10], ('seq', 'blk'), axis=0, tiled=True)]
    ppermute x6 -> x65, waiting for transfers between devices: 142 us -> 232 us  [the longest x61 232 us: swap(): return lax.ppermute(value, AXES, pairs)]
    unnamed x2 -> x0, blocking collectives: 88.1 us -> none
    convert_element_type x4 -> x21, other arithmetic: 82.8 us -> 13.7 us  [the longest x19 12.3 us: low(): return value.astype(jnp.bfloat16)]
  transfers between devices with their start and end apart: 14 -> 65, of which waited for: 6 -> 23; matrix products, arithmetic and copies ran while one was open for 18% -> 25% of each run, Pallas kernels for 0% -> 18%
where the time goes in v1:
time: 981 us; the launch traced here: 973 us
  waiting for transfers between devices  232 us (24%)
  starting transfers between devices  179 us (18%)
  Pallas kernels  171 us (17%)
  matrix products  159 us (16%)
  other arithmetic  138 us (14%)
  local copies, waits for them, and re-layouts  90.9 us (9%)
    ppermute x61, waiting for transfers between devices, swap(): return lax.ppermute(value, AXES, pairs)  232 us
    ppermute x61, starting transfers between devices, swap(): return lax.ppermute(value, AXES, pairs)  163 us
    pallas_call x1, Pallas kernels, attn_bwd(): pl.pallas_call(functools.partial(bwd_kernel, tiles, lse_lane), grid_spec=...  110 us
    pallas_call x1, Pallas kernels, attn_fwd(): pl.pallas_call(functools.partial(fwd_kernel, tiles, lse_lane), grid_spec=...  61 us
    dot_general x4, matrix products, nt(): lax.dot_general(a, b, (((1,), (1,)), ((), ())), preferred_element_type=jn...  50 us
    dot_general x4, matrix products, row_dot(): lax.dot_general(left, right, (((0,), (0,)), ((), ())), preferred_element_...  44.8 us
    select_n x18, other arithmetic, ordered(): jnp.where(bit == 0, jnp.stack([own, other], axis), jnp.stack([other, own]...  34.2 us
    unnamed x116, local copies, waits for them, and re-layouts  25.6 us
  transfers between devices with their start and end apart: 65, of which 23 were waited for; matrix products, arithmetic and copies ran while one was open for 25% of the time, Pallas kernels for 18%

profile of v1, /device:TPU:0, one launch (start us, length us, event | category | flops | bytes accessed | tf_op | source)
XLA Modules:
  0.0 972.6 jit_solution(4661564866351858646)
XLA Ops:
  0.7 3.1 collective-permute-start.18
  10.3 3.8 collective-permute-start.2
  14.1 4.0 copy.203
  41.6 4.3 collective-permute-start.11
  47.6 3.6 collective-permute-start.8
  55.7 6.1 collective-permute-done.10
  63.2 13.4 %collective-permute-done.11 = bf16[32,5120]{1,0:T(8,128)(2,1)S(1)} collective-permute-done((bf16[32,5120]{1,0:T(8,128)(2,1)}, bf16[32,5120]{1,0:T(8,128)(2,1)S(1)}, u32[]{:S(2)}, u32[]{:S(2)}) %collective-permute-start.11) | collective-permute-done | bytes 327712 | tf_op jit(solution)/shard_map/ppermute | solution.py:276
  82.1 25.7 %collective-permute-done.5 = bf16[4,32,1664]{2,1,0:T(8,128)(2,1)S(1)} collective-permute-done((bf16[4,32,1664]{2,1,0:T(8,128)(2,1)S(1)}, bf16[4,32,1664]{2,1,0:T(8,128)(2,1)S(1)}, u32[]{:S(2)}, u32[]{:S(2)}) %collective-permute-start.5) | collective-permute-done | bytes 426016 | tf_op jit(solution)/shard_map/ppermute | solution.py:276
  110.7 8.3 collective-permute-done.23
  127.7 5.4 collective-permute-done.15
  139.0 15.9 %collective-permute-done.6 = bf16[4,2,32,1664]{3,2,1,0:T(8,128)(2,1)S(1)} collective-permute-done((bf16[4,2,32,1664]{3,2,1,0:T(8,128)(2,1)S(1)}, bf16[4,2,32,1664]{3,2,1,0:T(8,128)(2,1)S(1)}, u32[]{:S(2)}, u32[]{:S(2)}) %collective-permute-start.6) | collective-permute-done | bytes 852000 | tf_op jit(solution)/shard_map/ppermute | solution.py:276
  157.7 3.3 fusion.130
  175.9 3.0 concatenate.192.qf_ref
  180.7 3.3 concatenate.196.kf_ref
  186.8 5.3 fusion.131
  192.4 6.1 collective-permute-done.16
  200.6 6.4 fusion.132
  207.1 4.7 maximum_select_fusion.2
  219.3 3.2 add_convert_fusion.3
  222.5 19.6 %add_convert_fusion.q_ref.k_ref.v_ref = bf16[2048,3072]{1,0:T(8,128)(2,1)} fusion(f32[3072]{0:T(1024)S(1)} %pad_maximum_fusion.22, bf16[1024,3200]{1,0:T(8,128)(2,1)} %bitcast.293, bf16[512,1024]{0,1:T(8,128)(2,1)} %get-tuple-element.277, bf16[1024,1024]{0,1:T(8,128)(2,1)} %fusion.33, bf16[512,1024]{0,1:T(8,128)(2,1)S(1)} %get-tuple-element.276), kind=kOutput, calls=%fused_computation.1 | convolution fusion | flops 12910067712 | bytes 23080960 | tf_op jit(solution)/shard_map/dot_general | solution.py:415
  242.1 61.0 %attn_fwd.1 = (bf16[1024,1024]{1,0:T(8,128)(2,1)S(1)}, bf16[1024,128]{1,0:T(8,128)(2,1)S(1)}) custom-call(s32[4]{0:T(128)S(1)} %get-tuple-element.192.lo_ref, s32[4]{0:T(128)S(1)} %get-tuple-element.191.n_ref, bf16[2048,3072]{1,0:T(8,128)(2,1)} %add_convert_fusion.q_ref.k_ref.v_ref, bf16[2048,3072]{1,0:T(8,128)(2,1)} %add_convert_fusion.q_ref.k_ref.v_ref, ...), custom_call_target="tpu_custom_call" | custom-call | flops 6442450944 | bytes 8388608 | tf_op jit(solution)/shard_map/attn_fwd/pallas_call | solution.py:86
  304.1 7.9 maximum_select_fusion.1
  312.0 6.5 maximum_select_fusion
  318.5 4.6 fusion.138
  323.6 20.0 %multiply_convert_fusion = (bf16[1024,4096]{1,0:T(8,128)(2,1)}, f32[1024,4096]{1,0:T(8,128)}) fusion(f32[4096]{0:T(1024)S(1)} %add.503, bf16[1024,5120]{1,0:T(8,128)(2,1)} %bitcast.283, f32[1024,1024]{0,1:T(8,128)S(1)} %get-tuple-element.190, f32[1024]{0:T(1024)S(1)} %get-tuple-element.166, f32[1024]{0:T(1024)S(1)} %get-tuple-element.167, ...), kind=kOutput, calls=%fused_computation.8 | convolution fusion | flops 8620343296 | bytes 37781504 | tf_op jit(solution)/shard_map/dot_general | solution.py:422
  343.7 17.4 %fusion.137 = (f32[1024]{0:T(1024)S(1)}, f32[1024,1024]{0,1:T(8,128)}, f32[]{:T(128)}) fusion(f32[1024]{0:T(1024)S(1)} %get-tuple-element.165, f32[1024]{0:T(1024)S(1)} %get-tuple-element.166, f32[1024]{0:T(1024)S(1)} %get-tuple-element.167, f32[1024]{0:T(1024)S(1)} %add_rsqrt_fusion.1, f32[1024,1024]{0,1:T(8,128)} %copy-done.4, ...), kind=kOutput, calls=%fused_computation.402 | convolution fusion | flops 8599370752 | bytes 25190404 | tf_op jit(solution)/shard_map/dot_general | solution.py:426
  364.5 3.1 fusion.22
  369.3 15.2 %convolution_convert_fusion = bf16[4096,1024]{1,0:T(8,128)(2,1)} fusion(bf16[1024,4096]{1,0:T(8,128)(2,1)} %get-tuple-element.284, bf16[1024,1024]{0,1:T(8,128)(2,1)S(1)} %get-tuple-element.184), kind=kOutput, calls=%fused_computation.18 | convolution fusion | flops 8594128896 | bytes 18874368 | tf_op jit(solution)/shard_map/dot_general | solution.py:262
  384.5 18.6 %fusion.149 = (bf16[4096]{0:T(1024)(128)(2,1)S(1)}, bf16[1024,4096]{1,0:T(8,128)(2,1)}) fusion(f32[1024,4096]{1,0:T(8,128)} %get-tuple-element.285, f32[4096]{0:T(1024)S(1)} %add.503, bf16[1024,1024]{0,1:T(8,128)(2,1)S(1)} %get-tuple-element.184, bf16[4096,1024]{1,0:T(8,128)(2,1)S(1)} %bitcast.289), kind=kOutput, calls=%fused_computation.413 | convolution fusion | flops 8640262144 | bytes 35676160 | tf_op jit(solution)/shard_map/dot_general | solution.py:15
  403.1 14.9 %convolution_convert_fusion.1 = bf16[1024,4096]{1,0:T(8,128)(2,1)} fusion(bf16[1024,4096]{1,0:T(8,128)(2,1)} %get-tuple-element.291, f32[1024,1024]{0,1:T(8,128)S(1)} %copy-done.5, f32[1024]{0:T(1024)S(1)} %get-tuple-element.166, f32[1024]{0:T(1024)S(1)} %get-tuple-element.167, f32[1024]{0:T(1024)S(1)} %add_rsqrt_fusion.1, ...), kind=kOutput, calls=%fused_computation.19 | convolution fusion | flops 8599371776 | bytes 20987904 | tf_op jit(solution)/shard_map/dot_general | solution.py:262
  418.0 17.3 %multiply_reduce_fusion.3 = (bf16[1024]{0:T(1024)(128)(2,1)S(1)}, f32[1024]{0:T(1024)S(1)}, f32[1024]{0:T(1024)S(1)}, bf16[1024]{0:T(1024)(128)(2,1)S(1)}, f32[1024,1024]{0,1:T(8,128)}) fusion(f32[1024,1024]{0,1:T(8,128)S(1)} %copy-done.5, f32[1024]{0:T(1024)S(1)} %add_rsqrt_fusion.1, f32[1024]{0:T(1024)S(1)} %broadcast_multiply_fusion.5, ...), kind=kOutput, calls=%fused_computation.58 | convolution fusion | flops 8608804864 | bytes 31502336 | tf_op jit(solution)/shard_map/dot_general | solution.py:15
  435.4 3.7 convert_reduce_fusion.1
  441.5 4.0 convolution_convert_fusion.4
  451.0 4.7 collective-permute-start.60
  455.7 6.9 constant_dynamic-slice_fusion.1
  465.3 6.3 constant_dynamic-slice_fusion.3
  477.7 4.5 concatenate.200
  483.7 9.6 collective-permute-start.26
  494.9 3.9 copy.239
  500.9 5.7 collective-permute-start.61
  510.1 13.6 %collective-permute-start.62 = (f32[3]{0:T(128)S(1)}, f32[3]{0:T(128)S(1)}, u32[]{:S(2)}, u32[]{:S(2)}) collective-permute-start(f32[3]{0:T(128)S(1)} %fusion.166), channel_id=1, source_target_pairs={{0,1},{1,0},{2,3},{3,2},{4,5},{5,4},{6,7},{7,6},{8,9},{9,8},{10,11... | collective-permute-start | bytes 44 | tf_op jit(solution)/shard_map/ppermute | solution.py:276
  523.7 19.6 %collective-permute-done.62 = f32[3]{0:T(128)S(1)} collective-permute-done((f32[3]{0:T(128)S(1)}, f32[3]{0:T(128)S(1)}, u32[]{:S(2)}, u32[]{:S(2)}) %collective-permute-start.62) | collective-permute-done | bytes 44 | tf_op jit(solution)/shard_map/ppermute | solution.py:276
  543.3 20.1 %collective-permute-start.63 = (f32[3]{0:T(128)S(1)}, f32[3]{0:T(128)S(1)}, u32[]{:S(2)}, u32[]{:S(2)}) collective-permute-start(f32[3]{0:T(128)S(1)} %add.563), channel_id=1, source_target_pairs={{0,2},{1,3},{2,0},{3,1},{4,6},{5,7},{6,4},{7,5},{8,10},{9,11},{10,... | collective-permute-start | bytes 44 | tf_op jit(solution)/shard_map/ppermute | solution.py:276
  565.5 3.8 collective-permute-done.64
  576.8 3.3 concatenate.202.qf_ref
  586.8 109.7 %attn_bwd.1 = bf16[3,1024,1024]{2,1,0:T(8,128)(2,1)} custom-call(s32[4]{0:T(128)S(1)} %get-tuple-element.192.lo_ref, s32[4]{0:T(128)S(1)} %get-tuple-element.191.n_ref, bf16[2048,3072]{1,0:T(8,128)(2,1)} %add_convert_fusion.q_ref.k_ref.v_ref, bf16[2048,3072]{1,0:T(8,128)(2,1)} %add_convert_fusion.q_ref.k_ref.v_ref, ...), custom_call_target="tpu_custom_call" | custom-call | flops 12884901888 | bytes 16777216 | tf_op jit(solution)/shard_map/attn_bwd/pallas_call | solution.py:172
  696.5 5.2 slice_reduce_fusion
  702.8 10.1 %fusion.142 = (f32[1024]{0:T(1024)S(1)}, bf16[1024,1024]{0,1:T(8,128)(2,1)}) fusion(f32[1024,1024]{0,1:T(8,128)S(1)} %copy-done.20, bf16[1024,3200]{1,0:T(8,128)(2,1)S(1)} %bitcast.296, bf16[1024,1024]{1,0:T(8,128)(2,1)} %get-tuple-element.199, bf16[1024,1024]{1,0:T(8,128)(2,1)} %get-tuple-element.200, bf16[1024,1024]{1,0:T(8,128)(2,1)} %get-tuple-element.201), kind=kOutput, calls=%fused_computation.406 | convolution fusion | flops 6464470016 | bytes 18878464 | tf_op jit(solution)/shard_map/dot_general | solution.py:15
  712.9 12.3 %convolution_convert_fusion.2 = bf16[1024,3072]{1,0:T(8,128)(2,1)} fusion(bf16[1024,1024]{0,1:T(8,128)(2,1)S(1)} %copy-done.22, bf16[1024,1024]{1,0:T(8,128)(2,1)} %get-tuple-element.199, bf16[1024,1024]{1,0:T(8,128)(2,1)} %get-tuple-element.200, bf16[1024,1024]{1,0:T(8,128)(2,1)} %get-tuple-element.201), kind=kOutput, calls=%fused_computation.30 | convolution fusion | flops 6464471040 | bytes 14680064 | tf_op jit(solution)/shard_map/dot_general | solution.py:262
  726.6 19.4 %collective-permute-start.40 = (bf16[4,32,512]{2,1,0:T(8,128)(2,1)S(1)}, bf16[4,32,512]{2,1,0:T(8,128)(2,1)S(1)}, u32[]{:S(2)}, u32[]{:S(2)}) collective-permute-start(bf16[4,32,512]{2,1,0:T(8,128)(2,1)S(1)} %dynamic-slice_bitcast_fusion.14), channel_id=1, source_target_pairs={{0,1},{1,0},{2,3},{3,2},{4,5},{5,4},{6,7},{7,6},{8,9},{9,8},{10,11... | collective-permute-start | bytes 393224 | tf_op jit(solution)/shard_map/ppermute | solution.py:276
  752.8 27.8 %collective-permute-start.41 = (bf16[32,1024]{1,0:T(8,128)(2,1)}, bf16[32,1024]{1,0:T(8,128)(2,1)}, u32[]{:S(2)}, u32[]{:S(2)}) collective-permute-start(bf16[32,1024]{1,0:T(8,128)(2,1)} %get-tuple-element.270), channel_id=1, source_target_pairs={{0,2},{1,3},{2,0},{3,1},{4,6},{5,7},{6,4},{7,5},{8,10},{9,11},{10,... | collective-permute-start | bytes 196616 | tf_op jit(solution)/shard_map/ppermute | solution.py:276
  782.9 3.1 fusion.36
  788.0 4.1 copy.240
  793.8 5.6 fusion.6
  802.2 3.7 fusion.7
  810.2 16.1 %collective-permute-done.55 = bf16[4,2,128,512]{3,2,0,1:T(8,128)(2,1)} collective-permute-done((bf16[4,2,128,512]{3,2,0,1:T(8,128)(2,1)S(1)}, bf16[4,2,128,512]{3,2,0,1:T(8,128)(2,1)}, u32[]{:S(2)}, u32[]{:S(2)}) %collective-permute-start.55) | collective-permute-done | bytes 1048608 | tf_op jit(solution)/shard_map/ppermute | solution.py:276
  830.4 18.2 %collective-permute-done.47 = bf16[4,2,32,2048]{3,2,0,1:T(8,128)(2,1)S(1)} collective-permute-done((bf16[4,2,32,2048]{3,2,0,1:T(8,128)(2,1)S(1)}, bf16[4,2,32,2048]{3,2,0,1:T(8,128)(2,1)S(1)}, u32[]{:S(2)}, u32[]{:S(2)}) %collective-permute-start.47) | collective-permute-done | bytes 1048608 | tf_op jit(solution)/shard_map/ppermute | solution.py:276
  850.6 15.1 %collective-permute-done.29 = bf16[2,4,32,1536]{3,2,1,0:T(8,128)(2,1)S(1)} collective-permute-done((bf16[2,4,32,1536]{3,2,1,0:T(8,128)(2,1)S(1)}, bf16[2,4,32,1536]{3,2,1,0:T(8,128)(2,1)S(1)}, u32[]{:S(2)}, u32[]{:S(2)}) %collective-permute-start.29) | collective-permute-done | bytes 786464 | tf_op jit(solution)/shard_map/ppermute | solution.py:276
  868.4 29.0 %collective-permute-done.30 = bf16[4,32,1536]{2,1,0:T(8,128)(2,1)S(1)} collective-permute-done((bf16[4,32,1536]{2,1,0:T(8,128)(2,1)S(1)}, bf16[4,32,1536]{2,1,0:T(8,128)(2,1)S(1)}, u32[]{:S(2)}, u32[]{:S(2)}) %collective-permute-start.30) | collective-permute-done | bytes 393248 | tf_op jit(solution)/shard_map/ppermute | solution.py:276
  897.5 11.3 %collective-permute-done.32 = bf16[4,32,1664]{2,1,0:T(8,128)(2,1)S(1)} collective-permute-done((bf16[4,32,1664]{2,1,0:T(8,128)(2,1)S(1)}, bf16[4,32,1664]{2,1,0:T(8,128)(2,1)S(1)}, u32[]{:S(2)}, u32[]{:S(2)}) %collective-permute-start.32) | collective-permute-done | bytes 426016 | tf_op jit(solution)/shard_map/ppermute | solution.py:276
  921.9 4.9 collective-permute-done.34
  926.8 15.5 %collective-permute-start.50 = (bf16[32,4096]{1,0:T(8,128)(2,1)}, bf16[32,4096]{1,0:T(8,128)(2,1)S(1)}, u32[]{:S(2)}, u32[]{:S(2)}) collective-permute-start(bf16[32,4096]{1,0:T(8,128)(2,1)} %get-tuple-element.242), channel_id=1, source_target_pairs={{0,4},{1,5},{2,6},{3,7},{4,0},{5,1},{6,2},{7,3},{8,12},{9,13},{10,... | collective-permute-start | bytes 786440 | tf_op jit(solution)/shard_map/ppermute | solution.py:276
  947.7 11.7 %collective-permute-done.58 = bf16[128,1024]{1,0:T(8,128)(2,1)S(1)} collective-permute-done((bf16[128,1024]{1,0:T(8,128)(2,1)}, bf16[128,1024]{1,0:T(8,128)(2,1)S(1)}, u32[]{:S(2)}, u32[]{:S(2)}) %collective-permute-start.58) | collective-permute-done | bytes 262176 | tf_op jit(solution)/shard_map/ppermute | solution.py:276
  960.3 10.3 %collective-permute-done.50 = bf16[32,4096]{1,0:T(8,128)(2,1)S(1)} collective-permute-done((bf16[32,4096]{1,0:T(8,128)(2,1)}, bf16[32,4096]{1,0:T(8,128)(2,1)S(1)}, u32[]{:S(2)}, u32[]{:S(2)}) %collective-permute-start.50) | collective-permute-done | bytes 262176 | tf_op jit(solution)/shard_map/ppermute | solution.py:276
  (399 shorter events, 191.9 us)
Async XLA Ops:
  0.7 46.8 %collective-permute-start.18 = (bf16[128,1024]{1,0:T(8,128)(2,1)}, bf16[128,1024]{1,0:T(8,128)(2,1)}, u32[]{:S(2)}, u32[]{:S(2)}) collective-permute-start(bf16[128,1024]{1,0:T(8,128)(2,1)} %param.40), channel_id=1, source_target_pairs={{0,2},{1,3},{2,0},{3,1},{4,6},{5,7},{6,4},{7,5},{8,10},{9,11},{10,... | collective-permute-start | bytes 786440 | tf_op jit(solution)/shard_map/ppermute | solution.py:276
  3.8 43.8 %collective-permute-start.19 = (bf16[128,1024]{1,0:T(8,128)(2,1)}, bf16[128,1024]{1,0:T(8,128)(2,1)}, u32[]{:S(2)}, u32[]{:S(2)}) collective-permute-start(bf16[128,1024]{1,0:T(8,128)(2,1)} %param.40), channel_id=1, source_target_pairs={{0,4},{1,5},{2,6},{3,7},{4,0},{5,1},{6,2},{7,3},{8,12},{9,13},{10,... | collective-permute-start | bytes 786440 | tf_op jit(solution)/shard_map/ppermute | solution.py:276
  9.6 31.8 %collective-permute-start = (bf16[32,3200]{1,0:T(8,128)(2,1)S(1)}, bf16[32,3200]{1,0:T(8,128)(2,1)}, u32[]{:S(2)}, u32[]{:S(2)}) collective-permute-start(bf16[32,3200]{1,0:T(8,128)(2,1)S(1)} %fusion.101), channel_id=1, source_target_pairs={{0,2},{1,3},{2,0},{3,1},{4,6},{5,7},{6,4},{7,5},{8,10},{9,11},{10,... | collective-permute-start | bytes 614408 | tf_op jit(solution)/shard_map/ppermute | solution.py:276
  10.1 31.4 %collective-permute-start.1 = (bf16[32,3200]{1,0:T(8,128)(2,1)S(1)}, bf16[32,3200]{1,0:T(8,128)(2,1)}, u32[]{:S(2)}, u32[]{:S(2)}) collective-permute-start(bf16[32,3200]{1,0:T(8,128)(2,1)S(1)} %fusion.101), channel_id=1, source_target_pairs={{0,4},{1,5},{2,6},{3,7},{4,0},{5,1},{6,2},{7,3},{8,12},{9,13},{10,... | collective-permute-start | bytes 614408 | tf_op jit(solution)/shard_map/ppermute | solution.py:276
  10.3 31.3 %collective-permute-start.2 = (bf16[32,3200]{1,0:T(8,128)(2,1)S(1)}, bf16[32,3200]{1,0:T(8,128)(2,1)}, u32[]{:S(2)}, u32[]{:S(2)}) collective-permute-start(bf16[32,3200]{1,0:T(8,128)(2,1)S(1)} %fusion.101), channel_id=1, source_target_pairs={{0,6},{1,7},{2,4},{3,5},{4,2},{5,3},{6,0},{7,1},{8,14},{9,15},{10,... | collective-permute-start | bytes 614408 | tf_op jit(solution)/shard_map/ppermute | solution.py:276
  41.4 11.3 %collective-permute-start.20 = (bf16[128,1024]{1,0:T(8,128)(2,1)}, bf16[128,1024]{1,0:T(8,128)(2,1)S(1)}, u32[]{:S(2)}, u32[]{:S(2)}) collective-permute-start(bf16[128,1024]{1,0:T(8,128)(2,1)} %param.40), channel_id=1, source_target_pairs={{0,6},{1,7},{2,4},{3,5},{4,2},{5,3},{6,0},{7,1},{8,14},{9,15},{10,... | collective-permute-start | bytes 786440 | tf_op jit(solution)/shard_map/ppermute | solution.py:276
  41.5 20.2 %collective-permute-start.10 = (bf16[32,5120]{1,0:T(8,128)(2,1)}, bf16[32,5120]{1,0:T(8,128)(2,1)S(1)}, u32[]{:S(2)}, u32[]{:S(2)}) collective-permute-start(bf16[32,5120]{1,0:T(8,128)(2,1)} %constant_dynamic-update-slice_fusion), channel_id=1, source_target_pairs={{0,2},{1,3},{2,0},{3,1},{4,6},{5,7},{6,4},{7,5},{8,10},{9,11},{10,... | collective-permute-start | bytes 983048 | tf_op jit(solution)/shard_map/ppermute | solution.py:276
  41.6 35.1 %collective-permute-start.11 = (bf16[32,5120]{1,0:T(8,128)(2,1)}, bf16[32,5120]{1,0:T(8,128)(2,1)S(1)}, u32[]{:S(2)}, u32[]{:S(2)}) collective-permute-start(bf16[32,5120]{1,0:T(8,128)(2,1)} %constant_dynamic-update-slice_fusion), channel_id=1, source_target_pairs={{0,4},{1,5},{2,6},{3,7},{4,0},{5,1},{6,2},{7,3},{8,12},{9,13},{10,... | collective-permute-start | bytes 983048 | tf_op jit(solution)/shard_map/ppermute | solution.py:276
  47.4 30.7 %collective-permute-start.12 = (bf16[32,5120]{1,0:T(8,128)(2,1)}, bf16[32,5120]{1,0:T(8,128)(2,1)S(1)}, u32[]{:S(2)}, u32[]{:S(2)}) collective-permute-start(bf16[32,5120]{1,0:T(8,128)(2,1)} %constant_dynamic-update-slice_fusion), channel_id=1, source_target_pairs={{0,6},{1,7},{2,4},{3,5},{4,2},{5,3},{6,0},{7,1},{8,14},{9,15},{10,... | collective-permute-start | bytes 983048 | tf_op jit(solution)/shard_map/ppermute | solution.py:276
  47.6 116.2 %collective-permute-start.8 = (bf16[528,1024]{1,0:T(8,128)(2,1)S(1)}, bf16[528,1024]{1,0:T(8,128)(2,1)S(1)}, u32[]{:S(2)}, u32[]{:S(2)}) collective-permute-start(bf16[528,1024]{1,0:T(8,128)(2,1)S(1)} %copy-done.27), channel_id=1, source_target_pairs={{0,1},{1,2},{2,3},{3,4},{4,5},{5,6},{6,7},{8,9},{9,10},{10,11},{11... | collective-permute-start | bytes 3244040 | tf_op jit(solution)/shard_map/ppermute | solution.py:339
  52.7 109.6 %collective-permute-start.9 = (bf16[528,1024]{1,0:T(8,128)(2,1)S(1)}, bf16[528,1024]{1,0:T(8,128)(2,1)S(1)}, u32[]{:S(2)}, u32[]{:S(2)}) collective-permute-start(bf16[528,1024]{1,0:T(8,128)(2,1)S(1)} %copy-done.28), channel_id=1, source_target_pairs={{1,0},{2,1},{3,2},{4,3},{5,4},{6,5},{7,6},{9,8},{10,9},{11,10},{12... | collective-permute-start | bytes 3244040 | tf_op jit(solution)/shard_map/ppermute | solution.py:339
  61.7 18.5 %collective-permute-start.3 = (bf16[4,32,1536]{2,1,0:T(8,128)(2,1)S(1)}, bf16[4,32,1536]{2,1,0:T(8,128)(2,1)S(1)}, u32[]{:S(2)}, u32[]{:S(2)}) collective-permute-start(bf16[4,32,1536]{2,1,0:T(8,128)(2,1)S(1)} %pad_maximum_fusion.21), channel_id=1, source_target_pairs={{0,16},{1,17},{2,18},{3,19},{4,20},{5,21},{6,22},{7,23},{8,24},{9,... | collective-permute-start | bytes 1179656 | tf_op jit(solution)/shard_map/ppermute | solution.py:276
  76.6 31.1 %collective-permute-start.5 = (bf16[4,32,1664]{2,1,0:T(8,128)(2,1)S(1)}, bf16[4,32,1664]{2,1,0:T(8,128)(2,1)S(1)}, u32[]{:S(2)}, u32[]{:S(2)}) collective-permute-start(bf16[4,32,1664]{2,1,0:T(8,128)(2,1)S(1)} %pad_maximum_fusion.18), channel_id=1, source_target_pairs={{0,1},{1,0},{2,3},{3,2},{4,5},{5,4},{6,7},{7,6},{8,9},{9,8},{10,11... | collective-permute-start | bytes 1277960 | tf_op jit(solution)/shard_map/ppermute | solution.py:276
  78.1 40.9 %collective-permute-start.23 = (bf16[4,128,512]{2,1,0:T(8,128)(2,1)S(1)}, bf16[4,128,512]{2,1,0:T(8,128)(2,1)S(1)}, u32[]{:S(2)}, u32[]{:S(2)}) collective-permute-start(bf16[4,128,512]{2,1,0:T(8,128)(2,1)S(1)} %get-tuple-element.252), channel_id=1, source_target_pairs={{0,1},{1,0},{2,3},{3,2},{4,5},{5,4},{6,7},{7,6},{8,9},{9,8},{10,11... | collective-permute-start | bytes 1572872 | tf_op jit(solution)/shard_map/ppermute | solution.py:276
  80.2 41.3 %collective-permute-start.21 = (bf16[4,128,512]{2,1,0:T(8,128)(2,1)S(1)}, bf16[4,128,512]{2,1,0:T(8,128)(2,1)S(1)}, u32[]{:S(2)}, u32[]{:S(2)}) collective-permute-start(bf16[4,128,512]{2,1,0:T(8,128)(2,1)S(1)} %get-tuple-element.253), channel_id=1, source_target_pairs={{0,16},{1,17},{2,18},{3,19},{4,20},{5,21},{6,22},{7,23},{8,24},{9,... | collective-permute-start | bytes 1572872 | tf_op jit(solution)/shard_map/ppermute | solution.py:276
  107.8 25.3 %collective-permute-start.15 = (bf16[4,32,2560]{2,1,0:T(8,128)(2,1)S(1)}, bf16[4,32,2560]{2,1,0:T(8,128)(2,1)S(1)}, u32[]{:S(2)}, u32[]{:S(2)}) collective-permute-start(bf16[4,32,2560]{2,1,0:T(8,128)(2,1)S(1)} %get-tuple-element.228), channel_id=1, source_target_pairs={{0,1},{1,0},{2,3},{3,2},{4,5},{5,4},{6,7},{7,6},{8,9},{9,8},{10,11... | collective-permute-start | bytes 1966088 | tf_op jit(solution)/shard_map/ppermute | solution.py:276
  119.0 18.2 %collective-permute-start.13 = (bf16[4,32,2560]{2,1,0:T(8,128)(2,1)S(1)}, bf16[4,32,2560]{2,1,0:T(8,128)(2,1)S(1)}, u32[]{:S(2)}, u32[]{:S(2)}) collective-permute-start(bf16[4,32,2560]{2,1,0:T(8,128)(2,1)S(1)} %get-tuple-element.229), channel_id=1, source_target_pairs={{0,16},{1,17},{2,18},{3,19},{4,20},{5,21},{6,22},{7,23},{8,24},{9,... | collective-permute-start | bytes 1966088 | tf_op jit(solution)/shard_map/ppermute | solution.py:276
  121.6 36.1 %collective-permute-start.4 = (bf16[2,4,32,1536]{3,2,1,0:T(8,128)(2,1)S(1)}, bf16[2,4,32,1536]{3,2,1,0:T(8,128)(2,1)S(1)}, u32[]{:S(2)}, u32[]{:S(2)}) collective-permute-start(bf16[2,4,32,1536]{3,2,1,0:T(8,128)(2,1)S(1)} %maximum_select_fusion.17), channel_id=1, source_target_pairs={{0,1},{1,0},{2,3},{3,2},{4,5},{5,4},{6,7},{7,6},{8,9},{9,8},{10,11... | collective-permute-start | bytes 2359304 | tf_op jit(solution)/shard_map/ppermute | solution.py:276
  133.0 21.9 %collective-permute-start.6 = (bf16[4,2,32,1664]{3,2,1,0:T(8,128)(2,1)S(1)}, bf16[4,2,32,1664]{3,2,1,0:T(8,128)(2,1)S(1)}, u32[]{:S(2)}, u32[]{:S(2)}) collective-permute-start(bf16[4,2,32,1664]{3,2,1,0:T(8,128)(2,1)S(1)} %maximum_select_fusion.15), channel_id=1, source_target_pairs={{0,16},{1,17},{2,18},{3,19},{4,20},{5,21},{6,22},{7,23},{8,24},{9,... | collective-permute-start | bytes 2555912 | tf_op jit(solution)/shard_map/ppermute | solution.py:276
  137.2 46.8 %collective-permute-start.24 = (bf16[4,2,128,512]{3,2,1,0:T(8,128)(2,1)}, bf16[4,2,128,512]{3,2,1,0:T(8,128)(2,1)}, u32[]{:S(2)}, u32[]{:S(2)}) collective-permute-start(bf16[4,2,128,512]{3,2,1,0:T(8,128)(2,1)} %maximum_select_fusion.14), channel_id=1, source_target_pairs={{0,16},{1,17},{2,18},{3,19},{4,20},{5,21},{6,22},{7,23},{8,24},{9,... | collective-permute-start | bytes 3145736 | tf_op jit(solution)/shard_map/ppermute | solution.py:276
  154.9 31.9 %collective-permute-start.22 = (bf16[2,4,128,512]{3,2,1,0:T(8,128)(2,1)}, bf16[2,4,128,512]{3,2,1,0:T(8,128)(2,1)}, u32[]{:S(2)}, u32[]{:S(2)}) collective-permute-start(bf16[2,4,128,512]{3,2,1,0:T(8,128)(2,1)} %maximum_select_fusion.13), channel_id=1, source_target_pairs={{0,1},{1,0},{2,3},{3,2},{4,5},{5,4},{6,7},{7,6},{8,9},{9,8},{10,11... | collective-permute-start | bytes 3145736 | tf_op jit(solution)/shard_map/ppermute | solution.py:276
  161.0 46.1 %collective-permute-start.7 = (bf16[2,4,2,32,3200]{4,3,2,1,0:T(8,128)(2,1)}, bf16[2,4,2,32,3200]{4,3,2,1,0:T(8,128)(2,1)}, u32[]{:S(2)}, u32[]{:S(2)}) collective-permute-start(bf16[2,4,2,32,3200]{4,3,2,1,0:T(8,128)(2,1)} %get-tuple-element.216), channel_id=1, source_target_pairs={{0,8},{1,9},{2,10},{3,11},{4,12},{5,13},{6,14},{7,15},{8,0},{9,1},... | collective-permute-start | bytes 9830408 | tf_op jit(solution)/shard_map/ppermute | solution.py:276
  162.3 36.2 %collective-permute-start.16 = (bf16[4,2,32,2560]{3,2,1,0:T(8,128)(2,1)}, bf16[4,2,32,2560]{3,2,1,0:T(8,128)(2,1)}, u32[]{:S(2)}, u32[]{:S(2)}) collective-permute-start(bf16[4,2,32,2560]{3,2,1,0:T(8,128)(2,1)} %maximum_select_fusion.11), channel_id=1, source_target_pairs={{0,16},{1,17},{2,18},{3,19},{4,20},{5,21},{6,22},{7,23},{8,24},{9,... | collective-permute-start | bytes 3932168 | tf_op jit(solution)/shard_map/ppermute | solution.py:276
  163.8 36.8 %collective-permute-start.14 = (bf16[2,4,32,2560]{3,2,1,0:T(8,128)(2,1)}, bf16[2,4,32,2560]{3,2,1,0:T(8,128)(2,1)}, u32[]{:S(2)}, u32[]{:S(2)}) collective-permute-start(bf16[2,4,32,2560]{3,2,1,0:T(8,128)(2,1)} %maximum_select_fusion.10), channel_id=1, source_target_pairs={{0,1},{1,0},{2,3},{3,2},{4,5},{5,4},{6,7},{7,6},{8,9},{9,8},{10,11... | collective-permute-start | bytes 3932168 | tf_op jit(solution)/shard_map/ppermute | solution.py:276
  192.2 111.9 %collective-permute-start.25 = (bf16[2,4,2,128,1024]{4,3,2,1,0:T(8,128)(2,1)}, bf16[2,4,2,128,1024]{4,3,2,1,0:T(8,128)(2,1)}, u32[]{:S(2)}, u32[]{:S(2)}) collective-permute-start(bf16[2,4,2,128,1024]{4,3,2,1,0:T(8,128)(2,1)} %get-tuple-element.214), channel_id=1, source_target_pairs={{0,8},{1,9},{2,10},{3,11},{4,12},{5,13},{6,14},{7,15},{8,0},{9,1},... | collective-permute-start | bytes 12582920 | tf_op jit(solution)/shard_map/ppermute | solution.py:276
  207.1 104.9 %collective-permute-start.17 = (bf16[2,4,2,32,5120]{4,3,2,1,0:T(8,128)(2,1)}, bf16[2,4,2,32,5120]{4,3,2,1,0:T(8,128)(2,1)}, u32[]{:S(2)}, u32[]{:S(2)}) collective-permute-start(bf16[2,4,2,32,5120]{4,3,2,1,0:T(8,128)(2,1)} %get-tuple-element.203), channel_id=1, source_target_pairs={{0,8},{1,9},{2,10},{3,11},{4,12},{5,13},{6,14},{7,15},{8,0},{9,1},... | collective-permute-start | bytes 15728648 | tf_op jit(solution)/shard_map/ppermute | solution.py:276
  451.0 47.9 %collective-permute-start.60 = (f32[3]{0:T(128)S(1)}, f32[3]{0:T(128)S(1)}, u32[]{:S(2)}, u32[]{:S(2)}) collective-permute-start(f32[3]{0:T(128)S(1)} %pad_maximum_fusion.23), channel_id=1, source_target_pairs={{0,8},{1,9},{2,10},{3,11},{4,12},{5,13},{6,14},{7,15},{8,0},{9,1},... | collective-permute-start | bytes 44 | tf_op jit(solution)/shard_map/ppermute | solution.py:276
  465.3 328.6 %collective-permute-start.52 = (bf16[2,4,2,128,1024]{4,3,1,2,0:T(8,128)(2,1)}, bf16[2,4,2,128,1024]{4,3,1,2,0:T(8,128)(2,1)}, u32[]{:S(2)}, u32[]{:S(2)}) collective-permute-start(bf16[2,4,2,128,1024]{4,3,1,2,0:T(8,128)(2,1)} %bitcast.276), channel_id=1, source_target_pairs={{0,8},{1,9},{2,10},{3,11},{4,12},{5,13},{6,14},{7,15},{8,0},{9,1},... | collective-permute-start | bytes 12582920 | tf_op jit(solution)/shard_map/ppermute | solution.py:276
  476.1 93.8 %collective-permute-start.36 = (bf16[2,4,2,32,1024]{4,3,1,2,0:T(8,128)(2,1)}, bf16[2,4,2,32,1024]{4,3,1,2,0:T(8,128)(2,1)}, u32[]{:S(2)}, u32[]{:S(2)}) collective-permute-start(bf16[2,4,2,32,1024]{4,3,1,2,0:T(8,128)(2,1)} %bitcast.279), channel_id=1, source_target_pairs={{0,8},{1,9},{2,10},{3,11},{4,12},{5,13},{6,14},{7,15},{8,0},{9,1},... | collective-permute-start | bytes 3145736 | tf_op jit(solution)/shard_map/ppermute | solution.py:276
  483.7 91.2 %collective-permute-start.26 = (bf16[512,1152]{1,0:T(8,128)(2,1)}, bf16[512,1152]{1,0:T(8,128)(2,1)}, u32[]{:S(2)}, u32[]{:S(2)}) collective-permute-start(bf16[512,1152]{1,0:T(8,128)(2,1)} %get-tuple-element.217), channel_id=1, source_target_pairs={{0,1},{1,2},{2,3},{3,4},{4,5},{5,6},{6,7},{8,9},{9,10},{10,11},{11... | collective-permute-start | bytes 3538952 | tf_op jit(solution)/shard_map/ppermute | solution.py:339
  493.3 81.6 %collective-permute-start.27 = (bf16[512,1152]{1,0:T(8,128)(2,1)}, bf16[512,1152]{1,0:T(8,128)(2,1)}, u32[]{:S(2)}, u32[]{:S(2)}) collective-permute-start(bf16[512,1152]{1,0:T(8,128)(2,1)} %get-tuple-element.218), channel_id=1, source_target_pairs={{1,0},{2,1},{3,2},{4,3},{5,4},{6,5},{7,6},{9,8},{10,9},{11,10},{12... | collective-permute-start | bytes 3538952 | tf_op jit(solution)/shard_map/ppermute | solution.py:339
  500.9 7.2 collective-permute-start.61
  510.1 33.2 %collective-permute-start.62 = (f32[3]{0:T(128)S(1)}, f32[3]{0:T(128)S(1)}, u32[]{:S(2)}, u32[]{:S(2)}) collective-permute-start(f32[3]{0:T(128)S(1)} %fusion.166), channel_id=1, source_target_pairs={{0,1},{1,0},{2,3},{3,2},{4,5},{5,4},{6,7},{7,6},{8,9},{9,8},{10,11... | collective-permute-start | bytes 44 | tf_op jit(solution)/shard_map/ppermute | solution.py:276
  543.3 21.6 %collective-permute-start.63 = (f32[3]{0:T(128)S(1)}, f32[3]{0:T(128)S(1)}, u32[]{:S(2)}, u32[]{:S(2)}) collective-permute-start(f32[3]{0:T(128)S(1)} %add.563), channel_id=1, source_target_pairs={{0,2},{1,3},{2,0},{3,1},{4,6},{5,7},{6,4},{7,5},{8,10},{9,11},{10,... | collective-permute-start | bytes 44 | tf_op jit(solution)/shard_map/ppermute | solution.py:276
  569.3 231.9 %collective-permute-start.44 = (bf16[2,4,2,32,4096]{4,3,1,2,0:T(8,128)(2,1)}, bf16[2,4,2,32,4096]{4,3,1,2,0:T(8,128)(2,1)}, u32[]{:S(2)}, u32[]{:S(2)}) collective-permute-start(bf16[2,4,2,32,4096]{4,3,1,2,0:T(8,128)(2,1)} %bitcast.298), channel_id=1, source_target_pairs={{0,8},{1,9},{2,10},{3,11},{4,12},{5,13},{6,14},{7,15},{8,0},{9,1},... | collective-permute-start | bytes 12582920 | tf_op jit(solution)/shard_map/ppermute | solution.py:276
  572.8 152.8 %collective-permute-start.39 = (bf16[4,2,32,512]{3,2,0,1:T(8,128)(2,1)}, bf16[4,2,32,512]{3,2,0,1:T(8,128)(2,1)}, u32[]{:S(2)}, u32[]{:S(2)}) collective-permute-start(bf16[4,2,32,512]{3,2,0,1:T(8,128)(2,1)} %dynamic-slice_bitcast_fusion.12), channel_id=1, source_target_pairs={{0,16},{1,17},{2,18},{3,19},{4,20},{5,21},{6,22},{7,23},{8,24},{9,... | collective-permute-start | bytes 786440 | tf_op jit(solution)/shard_map/ppermute | solution.py:276
  574.9 171.1 %collective-permute-start.37 = (bf16[2,4,32,512]{3,2,1,0:T(8,128)(2,1)}, bf16[2,4,32,512]{3,2,1,0:T(8,128)(2,1)}, u32[]{:S(2)}, u32[]{:S(2)}) collective-permute-start(bf16[2,4,32,512]{3,2,1,0:T(8,128)(2,1)} %dynamic-slice_bitcast_fusion.13), channel_id=1, source_target_pairs={{0,1},{1,0},{2,3},{3,2},{4,5},{5,4},{6,7},{7,6},{8,9},{9,8},{10,11... | collective-permute-start | bytes 786440 | tf_op jit(solution)/shard_map/ppermute | solution.py:276
  726.6 23.0 %collective-permute-start.40 = (bf16[4,32,512]{2,1,0:T(8,128)(2,1)S(1)}, bf16[4,32,512]{2,1,0:T(8,128)(2,1)S(1)}, u32[]{:S(2)}, u32[]{:S(2)}) collective-permute-start(bf16[4,32,512]{2,1,0:T(8,128)(2,1)S(1)} %dynamic-slice_bitcast_fusion.14), channel_id=1, source_target_pairs={{0,1},{1,0},{2,3},{3,2},{4,5},{5,4},{6,7},{7,6},{8,9},{9,8},{10,11... | collective-permute-start | bytes 393224 | tf_op jit(solution)/shard_map/ppermute | solution.py:276
  747.1 5.0 collective-permute-start.38
  752.8 39.3 %collective-permute-start.41 = (bf16[32,1024]{1,0:T(8,128)(2,1)}, bf16[32,1024]{1,0:T(8,128)(2,1)}, u32[]{:S(2)}, u32[]{:S(2)}) collective-permute-start(bf16[32,1024]{1,0:T(8,128)(2,1)} %get-tuple-element.270), channel_id=1, source_target_pairs={{0,2},{1,3},{2,0},{3,1},{4,6},{5,7},{6,4},{7,5},{8,10},{9,11},{10,... | collective-permute-start | bytes 196616 | tf_op jit(solution)/shard_map/ppermute | solution.py:276
  780.6 11.6 %collective-permute-start.42 = (bf16[32,1024]{1,0:T(8,128)(2,1)}, bf16[32,1024]{1,0:T(8,128)(2,1)}, u32[]{:S(2)}, u32[]{:S(2)}) collective-permute-start(bf16[32,1024]{1,0:T(8,128)(2,1)} %get-tuple-element.271), channel_id=1, source_target_pairs={{0,4},{1,5},{2,6},{3,7},{4,0},{5,1},{6,2},{7,3},{8,12},{9,13},{10,... | collective-permute-start | bytes 196616 | tf_op jit(solution)/shard_map/ppermute | solution.py:276
  780.6 11.6 %collective-permute-start.43 = (bf16[32,1024]{1,0:T(8,128)(2,1)}, bf16[32,1024]{1,0:T(8,128)(2,1)}, u32[]{:S(2)}, u32[]{:S(2)}) collective-permute-start(bf16[32,1024]{1,0:T(8,128)(2,1)} %get-tuple-element.272), channel_id=1, source_target_pairs={{0,6},{1,7},{2,4},{3,5},{4,2},{5,3},{6,0},{7,1},{8,14},{9,15},{10,... | collective-permute-start | bytes 196616 | tf_op jit(solution)/shard_map/ppermute | solution.py:276
  792.1 16.7 %collective-permute-start.28 = (bf16[2,4,2,32,3200]{4,3,1,2,0:T(8,128)(2,1)}, bf16[2,4,2,32,3200]{4,3,1,2,0:T(8,128)(2,1)S(1)}, u32[]{:S(2)}, u32[]{:S(2)}) collective-permute-start(bf16[2,4,2,32,3200]{4,3,1,2,0:T(8,128)(2,1)} %bitcast.299), channel_id=1, source_target_pairs={{0,8},{1,9},{2,10},{3,11},{4,12},{5,13},{6,14},{7,15},{8,0},{9,1},... | collective-permute-start | bytes 9830408 | tf_op jit(solution)/shard_map/ppermute | solution.py:276
  800.1 26.1 %collective-permute-start.55 = (bf16[4,2,128,512]{3,2,0,1:T(8,128)(2,1)S(1)}, bf16[4,2,128,512]{3,2,0,1:T(8,128)(2,1)}, u32[]{:S(2)}, u32[]{:S(2)}) collective-permute-start(bf16[4,2,128,512]{3,2,0,1:T(8,128)(2,1)S(1)} %dynamic-slice_bitcast_fusion), channel_id=1, source_target_pairs={{0,16},{1,17},{2,18},{3,19},{4,20},{5,21},{6,22},{7,23},{8,24},{9,... | collective-permute-start | bytes 3145736 | tf_op jit(solution)/shard_map/ppermute | solution.py:276
  800.3 27.6 %collective-permute-start.53 = (bf16[2,4,128,512]{3,2,1,0:T(8,128)(2,1)S(1)}, bf16[2,4,128,512]{3,2,1,0:T(8,128)(2,1)}, u32[]{:S(2)}, u32[]{:S(2)}) collective-permute-start(bf16[2,4,128,512]{3,2,1,0:T(8,128)(2,1)S(1)} %dynamic-slice_bitcast_fusion.1), channel_id=1, source_target_pairs={{0,1},{1,0},{2,3},{3,2},{4,5},{5,4},{6,7},{7,6},{8,9},{9,8},{10,11... | collective-permute-start | bytes 3145736 | tf_op jit(solution)/shard_map/ppermute | solution.py:276
  806.4 42.2 %collective-permute-start.47 = (bf16[4,2,32,2048]{3,2,0,1:T(8,128)(2,1)S(1)}, bf16[4,2,32,2048]{3,2,0,1:T(8,128)(2,1)S(1)}, u32[]{:S(2)}, u32[]{:S(2)}) collective-permute-start(bf16[4,2,32,2048]{3,2,0,1:T(8,128)(2,1)S(1)} %dynamic-slice_bitcast_fusion.2), channel_id=1, source_target_pairs={{0,16},{1,17},{2,18},{3,19},{4,20},{5,21},{6,22},{7,23},{8,24},{9,... | collective-permute-start | bytes 3145736 | tf_op jit(solution)/shard_map/ppermute | solution.py:276
  806.7 42.4 %collective-permute-start.45 = (bf16[2,4,32,2048]{3,2,1,0:T(8,128)(2,1)S(1)}, bf16[2,4,32,2048]{3,2,1,0:T(8,128)(2,1)S(1)}, u32[]{:S(2)}, u32[]{:S(2)}) collective-permute-start(bf16[2,4,32,2048]{3,2,1,0:T(8,128)(2,1)S(1)} %dynamic-slice_bitcast_fusion.3), channel_id=1, source_target_pairs={{0,1},{1,0},{2,3},{3,2},{4,5},{5,4},{6,7},{7,6},{8,9},{9,8},{10,11... | collective-permute-start | bytes 3145736 | tf_op jit(solution)/shard_map/ppermute | solution.py:276
  810.0 55.6 %collective-permute-start.29 = (bf16[2,4,32,1536]{3,2,1,0:T(8,128)(2,1)S(1)}, bf16[2,4,32,1536]{3,2,1,0:T(8,128)(2,1)S(1)}, u32[]{:S(2)}, u32[]{:S(2)}) collective-permute-start(bf16[2,4,32,1536]{3,2,1,0:T(8,128)(2,1)S(1)} %dynamic-slice_bitcast_fusion.5), channel_id=1, source_target_pairs={{0,1},{1,0},{2,3},{3,2},{4,5},{5,4},{6,7},{7,6},{8,9},{9,8},{10,11... | collective-permute-start | bytes 2359304 | tf_op jit(solution)/shard_map/ppermute | solution.py:276
  826.2 41.7 %collective-permute-start.31 = (bf16[4,2,32,1664]{3,2,0,1:T(8,128)(2,1)S(1)}, bf16[4,2,32,1664]{3,2,0,1:T(8,128)(2,1)S(1)}, u32[]{:S(2)}, u32[]{:S(2)}) collective-permute-start(bf16[4,2,32,1664]{3,2,0,1:T(8,128)(2,1)S(1)} %dynamic-slice_bitcast_fusion.4), channel_id=1, source_target_pairs={{0,16},{1,17},{2,18},{3,19},{4,20},{5,21},{6,22},{7,23},{8,24},{9,... | collective-permute-start | bytes 2555912 | tf_op jit(solution)/shard_map/ppermute | solution.py:276
  827.9 82.2 %collective-permute-start.56 = (bf16[4,128,512]{2,1,0:T(8,128)(2,1)S(1)}, bf16[4,128,512]{2,1,0:T(8,128)(2,1)S(1)}, u32[]{:S(2)}, u32[]{:S(2)}) collective-permute-start(bf16[4,128,512]{2,1,0:T(8,128)(2,1)S(1)} %dynamic-slice_bitcast_fusion.6), channel_id=1, source_target_pairs={{0,1},{1,0},{2,3},{3,2},{4,5},{5,4},{6,7},{7,6},{8,9},{9,8},{10,11... | collective-permute-start | bytes 1572872 | tf_op jit(solution)/shard_map/ppermute | solution.py:276
  848.6 62.6 %collective-permute-start.54 = (bf16[4,128,512]{2,1,0:T(8,128)(2,1)S(1)}, bf16[4,128,512]{2,1,0:T(8,128)(2,1)S(1)}, u32[]{:S(2)}, u32[]{:S(2)}) collective-permute-start(bf16[4,128,512]{2,1,0:T(8,128)(2,1)S(1)} %dynamic-slice_bitcast_fusion.7), channel_id=1, source_target_pairs={{0,16},{1,17},{2,18},{3,19},{4,20},{5,21},{6,22},{7,23},{8,24},{9,... | collective-permute-start | bytes 1572872 | tf_op jit(solution)/shard_map/ppermute | solution.py:276
  849.2 65.5 %collective-permute-start.48 = (bf16[4,32,2048]{2,1,0:T(8,128)(2,1)S(1)}, bf16[4,32,2048]{2,1,0:T(8,128)(2,1)S(1)}, u32[]{:S(2)}, u32[]{:S(2)}) collective-permute-start(bf16[4,32,2048]{2,1,0:T(8,128)(2,1)S(1)} %dynamic-slice_bitcast_fusion.8), channel_id=1, source_target_pairs={{0,1},{1,0},{2,3},{3,2},{4,5},{5,4},{6,7},{7,6},{8,9},{9,8},{10,11... | collective-permute-start | bytes 1572872 | tf_op jit(solution)/shard_map/ppermute | solution.py:276
  865.6 49.4 %collective-permute-start.46 = (bf16[4,32,2048]{2,1,0:T(8,128)(2,1)S(1)}, bf16[4,32,2048]{2,1,0:T(8,128)(2,1)S(1)}, u32[]{:S(2)}, u32[]{:S(2)}) collective-permute-start(bf16[4,32,2048]{2,1,0:T(8,128)(2,1)S(1)} %dynamic-slice_bitcast_fusion.9), channel_id=1, source_target_pairs={{0,16},{1,17},{2,18},{3,19},{4,20},{5,21},{6,22},{7,23},{8,24},{9,... | collective-permute-start | bytes 1572872 | tf_op jit(solution)/shard_map/ppermute | solution.py:276
  868.0 29.4 %collective-permute-start.30 = (bf16[4,32,1536]{2,1,0:T(8,128)(2,1)S(1)}, bf16[4,32,1536]{2,1,0:T(8,128)(2,1)S(1)}, u32[]{:S(2)}, u32[]{:S(2)}) collective-permute-start(bf16[4,32,1536]{2,1,0:T(8,128)(2,1)S(1)} %dynamic-slice_bitcast_fusion.11), channel_id=1, source_target_pairs={{0,16},{1,17},{2,18},{3,19},{4,20},{5,21},{6,22},{7,23},{8,24},{9,... | collective-permute-start | bytes 1179656 | tf_op jit(solution)/shard_map/ppermute | solution.py:276
  897.3 11.4 %collective-permute-start.32 = (bf16[4,32,1664]{2,1,0:T(8,128)(2,1)S(1)}, bf16[4,32,1664]{2,1,0:T(8,128)(2,1)S(1)}, u32[]{:S(2)}, u32[]{:S(2)}) collective-permute-start(bf16[4,32,1664]{2,1,0:T(8,128)(2,1)S(1)} %dynamic-slice_bitcast_fusion.10), channel_id=1, source_target_pairs={{0,1},{1,0},{2,3},{3,2},{4,5},{5,4},{6,7},{7,6},{8,9},{9,8},{10,11... | collective-permute-start | bytes 1277960 | tf_op jit(solution)/shard_map/ppermute | solution.py:276
  908.9 11.5 %collective-permute-start.33 = (bf16[32,3200]{1,0:T(8,128)(2,1)S(1)}, bf16[32,3200]{1,0:T(8,128)(2,1)S(1)}, u32[]{:S(2)}, u32[]{:S(2)}) collective-permute-start(bf16[32,3200]{1,0:T(8,128)(2,1)S(1)} %get-tuple-element.263), channel_id=1, source_target_pairs={{0,2},{1,3},{2,0},{3,1},{4,6},{5,7},{6,4},{7,5},{8,10},{9,11},{10,... | collective-permute-start | bytes 614408 | tf_op jit(solution)/shard_map/ppermute | solution.py:276
  910.1 16.7 %collective-permute-start.34 = (bf16[32,3200]{1,0:T(8,128)(2,1)S(1)}, bf16[32,3200]{1,0:T(8,128)(2,1)S(1)}, u32[]{:S(2)}, u32[]{:S(2)}) collective-permute-start(bf16[32,3200]{1,0:T(8,128)(2,1)S(1)} %get-tuple-element.264), channel_id=1, source_target_pairs={{0,4},{1,5},{2,6},{3,7},{4,0},{5,1},{6,2},{7,3},{8,12},{9,13},{10,... | collective-permute-start | bytes 614408 | tf_op jit(solution)/shard_map/ppermute | solution.py:276
  911.2 15.6 %collective-permute-start.35 = (bf16[32,3200]{1,0:T(8,128)(2,1)S(1)}, bf16[32,3200]{1,0:T(8,128)(2,1)S(1)}, u32[]{:S(2)}, u32[]{:S(2)}) collective-permute-start(bf16[32,3200]{1,0:T(8,128)(2,1)S(1)} %get-tuple-element.265), channel_id=1, source_target_pairs={{0,6},{1,7},{2,4},{3,5},{4,2},{5,3},{6,0},{7,1},{8,14},{9,15},{10,... | collective-permute-start | bytes 614408 | tf_op jit(solution)/shard_map/ppermute | solution.py:276
  914.7 27.8 %collective-permute-start.57 = (bf16[128,1024]{1,0:T(8,128)(2,1)S(1)}, bf16[128,1024]{1,0:T(8,128)(2,1)S(1)}, u32[]{:S(2)}, u32[]{:S(2)}) collective-permute-start(bf16[128,1024]{1,0:T(8,128)(2,1)S(1)} %get-tuple-element.238), channel_id=1, source_target_pairs={{0,2},{1,3},{2,0},{3,1},{4,6},{5,7},{6,4},{7,5},{8,10},{9,11},{10,... | collective-permute-start | bytes 786440 | tf_op jit(solution)/shard_map/ppermute | solution.py:276
  915.0 44.3 %collective-permute-start.58 = (bf16[128,1024]{1,0:T(8,128)(2,1)}, bf16[128,1024]{1,0:T(8,128)(2,1)S(1)}, u32[]{:S(2)}, u32[]{:S(2)}) collective-permute-start(bf16[128,1024]{1,0:T(8,128)(2,1)} %get-tuple-element.239), channel_id=1, source_target_pairs={{0,4},{1,5},{2,6},{3,7},{4,0},{5,1},{6,2},{7,3},{8,12},{9,13},{10,... | collective-permute-start | bytes 786440 | tf_op jit(solution)/shard_map/ppermute | solution.py:276
  920.4 38.9 %collective-permute-start.59 = (bf16[128,1024]{1,0:T(8,128)(2,1)}, bf16[128,1024]{1,0:T(8,128)(2,1)S(1)}, u32[]{:S(2)}, u32[]{:S(2)}) collective-permute-start(bf16[128,1024]{1,0:T(8,128)(2,1)} %get-tuple-element.240), channel_id=1, source_target_pairs={{0,6},{1,7},{2,4},{3,5},{4,2},{5,3},{6,0},{7,1},{8,14},{9,15},{10,... | collective-permute-start | bytes 786440 | tf_op jit(solution)/shard_map/ppermute | solution.py:276
  926.8 33.5 %collective-permute-start.49 = (bf16[32,4096]{1,0:T(8,128)(2,1)}, bf16[32,4096]{1,0:T(8,128)(2,1)S(1)}, u32[]{:S(2)}, u32[]{:S(2)}) collective-permute-start(bf16[32,4096]{1,0:T(8,128)(2,1)} %get-tuple-element.241), channel_id=1, source_target_pairs={{0,2},{1,3},{2,0},{3,1},{4,6},{5,7},{6,4},{7,5},{8,10},{9,11},{10,... | collective-permute-start | bytes 786440 | tf_op jit(solution)/shard_map/ppermute | solution.py:276
  926.8 43.7 %collective-permute-start.50 = (bf16[32,4096]{1,0:T(8,128)(2,1)}, bf16[32,4096]{1,0:T(8,128)(2,1)S(1)}, u32[]{:S(2)}, u32[]{:S(2)}) collective-permute-start(bf16[32,4096]{1,0:T(8,128)(2,1)} %get-tuple-element.242), channel_id=1, source_target_pairs={{0,4},{1,5},{2,6},{3,7},{4,0},{5,1},{6,2},{7,3},{8,12},{9,13},{10,... | collective-permute-start | bytes 786440 | tf_op jit(solution)/shard_map/ppermute | solution.py:276
  942.4 28.1 %collective-permute-start.51 = (bf16[32,4096]{1,0:T(8,128)(2,1)}, bf16[32,4096]{1,0:T(8,128)(2,1)}, u32[]{:S(2)}, u32[]{:S(2)}) collective-permute-start(bf16[32,4096]{1,0:T(8,128)(2,1)} %get-tuple-element.243), channel_id=1, source_target_pairs={{0,6},{1,7},{2,4},{3,5},{4,2},{5,3},{6,0},{7,1},{8,14},{9,15},{10,... | collective-permute-start | bytes 786440 | tf_op jit(solution)/shard_map/ppermute | solution.py:276
  (54 other events, 884.6 us)

commit v2 on v1

--- a/solution.py
+++ b/solution.py
@@ -243,6 +243,373 @@
     return lo.astype(jnp.int32), ((stop + TQ - 1) // TQ - lo).astype(jnp.int32)
 
 
+MESH = pl.DeviceIdType.MESH
+
+
+def coords():
+    seq, blk = lax.axis_index("seq"), lax.axis_index("blk")
+    return seq // 2, lax.rem(seq, 2), blk // 2, lax.rem(blk, 2)
+
+
+def device_at(x, c, z, y):
+    return (x * 2 + c, z * 2 + y)
+
+
+def other_z(z, k):
+    low_bit = lax.rem(z, 2)
+    high_bit = z // 2
+    if k & 1:
+        low_bit = 1 - low_bit
+    if k & 2:
+        high_bit = 1 - high_bit
+    return high_bit * 2 + low_bit
+
+
+def partners():
+    x, c, z, y = coords()
+    return {
+        "x": device_at(1 - x, c, z, y),
+        "y": device_at(x, c, z, 1 - y),
+        "c": device_at(x, 1 - c, z, y),
+        1: device_at(x, c, other_z(z, 1), y),
+        2: device_at(x, c, other_z(z, 2), y),
+        3: device_at(x, c, other_z(z, 3), y),
+    }
+
+
+def meet(to):
+    barrier = pltpu.get_barrier_semaphore()
+    for device in to.values():
+        pl.semaphore_signal(barrier, inc=1, device_id=device, device_id_type=MESH)
+    pl.semaphore_wait(barrier, len(to))
+
+
+class Sends:
+    def __init__(self, send_sem, recv_sem, to):
+        self.send_sem, self.recv_sem, self.to, self.used, self.live = send_sem, recv_sem, to, 0, []
+
+    def start(self, src, dst, partner):
+        copy = pltpu.make_async_remote_copy(
+            src_ref=src, dst_ref=dst, send_sem=self.send_sem.at[self.used], recv_sem=self.recv_sem.at[self.used],
+            device_id=self.to[partner], device_id_type=MESH,
+        )
+        copy.start()
+        self.used += 1
+        self.live.append(copy)
+        return copy
+
+    def finish(self):
+        for copy in self.live:
+            copy.wait_send()
+
+
+def gather_plan(shard, full, sends, local, base, wide):
+    x, c, z, y = coords()
+    at = cut(wide)
+    every, one, two = pl.ds(base, wide), pl.ds(base, at), pl.ds(base + at, wide - at)
+
+    def send(partner, *index):
+        return sends.start(full.at[index], full.at[index], partner)
+
+    rows = slice(None)
+    own = pltpu.make_async_copy(shard.at[:, every], full.at[x, c, z, y, :, every], local)
+    own.start()
+    line = [sends.start(shard.at[:, every], full.at[x, c, z, y, :, every], k) for k in (1, 2, 3)]
+    yield
+    own.wait()
+    for copy in line:
+        copy.wait_recv()
+    if at:
+        a = send("x", x, c, rows, y, rows, one)
+    b = send("y", x, c, rows, y, rows, two)
+    core = [send("c", x, c, rows, y, rows, every)]
+    yield
+    if at:
+        a.wait_recv()
+        a2 = send("y", rows, c, rows, y, rows, one)
+        core.append(send("c", 1 - x, c, rows, y, rows, one))
+    b.wait_recv()
+    b2 = send("x", x, c, rows, rows, rows, two)
+    core.append(send("c", x, c, rows, 1 - y, rows, two))
+    yield
+    if at:
+        a2.wait_recv()
+        core.append(send("c", rows, c, rows, 1 - y, rows, one))
+    b2.wait_recv()
+    core.append(send("c", 1 - x, c, rows, rows, rows, two))
+    yield
+    for copy in core:
+        copy.wait_recv()
+    yield
+
+
+SENDS = 12
+
+
+def cut(columns):
+    return columns // 256 * 128
+
+
+def run_staggered(plans):
+    for turn in range(len(plans) + 4):
+        for k in reversed(range(len(plans))):
+            if 0 <= turn - k <= 4:
+                next(plans[k])
+
+
+def pieces(widths, parts):
+    return [(k, p * (w // n), w // n) for k, (w, n) in enumerate(zip(widths, parts)) for p in range(n)]
+
+
+def halo_start(edges, halo, sends, local):
+    seq, blk = lax.axis_index("seq"), lax.axis_index("blk")
+    last = lax.axis_size("blk") - 1
+    s, r = sends.send_sem, sends.recv_sem
+    at = sends.used
+    sends.used += 2
+    remote = functools.partial(pltpu.make_async_remote_copy, device_id_type=MESH)
+    down = remote(src_ref=edges.at[0], dst_ref=halo.at[1], send_sem=s.at[at], recv_sem=r.at[at],
+                  device_id=(seq, lax.max(blk - 1, 0)))
+    up = remote(src_ref=edges.at[1], dst_ref=halo.at[0], send_sem=s.at[at + 1], recv_sem=r.at[at + 1],
+                device_id=(seq, lax.min(blk + 1, last)))
+    fill = [pltpu.make_async_copy(edges.at[k], halo.at[k], local) for k in (0, 1)]
+
+    @pl.when(blk > 0)
+    def _():
+        down.start()
+
+    @pl.when(blk < last)
+    def _():
+        up.start()
+
+    @pl.when(blk == 0)
+    def _():
+        fill[0].start()
+
+    @pl.when(blk == last)
+    def _():
+        fill[1].start()
+
+    def finish():
+        @pl.when(blk > 0)
+        def _():
+            down.wait_send()
+            up.wait_recv()
+
+        @pl.when(blk < last)
+        def _():
+            up.wait_send()
+            down.wait_recv()
+
+        @pl.when(blk == 0)
+        def _():
+            fill[0].wait()
+
+        @pl.when(blk == last)
+        def _():
+            fill[1].wait()
+
+    return finish
+
+
+def meet_all(to):
+    seq, blk = lax.axis_index("seq"), lax.axis_index("blk")
+    last = lax.axis_size("blk") - 1
+    barrier = pltpu.get_barrier_semaphore()
+    for device in to.values():
+        pl.semaphore_signal(barrier, inc=1, device_id=device, device_id_type=MESH)
+
+    @pl.when(blk > 0)
+    def _():
+        pl.semaphore_signal(barrier, inc=1, device_id=(seq, lax.max(blk - 1, 0)), device_id_type=MESH)
+
+    @pl.when(blk < last)
+    def _():
+        pl.semaphore_signal(barrier, inc=1, device_id=(seq, lax.min(blk + 1, last)), device_id_type=MESH)
+
+    ends = jnp.where(blk == 0, 1, 0) + jnp.where(blk == last, 1, 0)
+    pl.semaphore_wait(barrier, len(to) + 2 - ends)
+
+
+def gather_kernel(plan, count, *refs):
+    shards, edges, fulls, halo = refs[:count], refs[count], refs[count + 1 : 2 * count + 1], refs[2 * count + 1]
+    send_sem, recv_sem, local_sem = refs[2 * count + 2 :]
+    to = partners()
+    meet_all(to)
+    sends = Sends(send_sem, recv_sem, to)
+    finish = halo_start(edges, halo, sends, local_sem.at[len(plan)])
+    run_staggered([
+        gather_plan(shards[k], fulls[k], sends, local_sem.at[i], base, wide) for i, (k, base, wide) in enumerate(plan)
+    ])
+    finish()
+    sends.finish()
+
+
+def gather_all(shards, parts, edges, collective):
+    count = len(shards)
+    plan = pieces([v.shape[1] for v in shards], parts)
+    anywhere = pl.BlockSpec(memory_space=pl.ANY)
+    shapes = [(2, 2, 4, 2) + v.shape for v in shards] + [edges.shape]
+    return pl.pallas_call(
+        functools.partial(gather_kernel, plan, count),
+        in_specs=[anywhere] * (count + 1),
+        out_specs=[anywhere] * (count + 1),
+        out_shape=[jax.ShapeDtypeStruct(s, jnp.bfloat16) for s in shapes],
+        scratch_shapes=[
+            pltpu.SemaphoreType.DMA((len(plan) * SENDS + 2,)),
+            pltpu.SemaphoreType.DMA((len(plan) * SENDS + 2,)),
+            pltpu.SemaphoreType.DMA((len(plan) + 1,)),
+        ],
+        compiler_params=pltpu.CompilerParams(collective_id=collective, has_side_effects=True),
+        name="gather_weights",
+    )(*shards, edges)
+
+
+def widen(value):
+    return value.astype(jnp.float32)
+
+
+def scatter_plan(grad, out, bufs, sends, local, base, wide):
+    x, c, z, y = coords()
+    at = cut(wide)
+    own, got, one1, two1, one2, two2, line, ends = bufs if at else bufs[:2] + (None,) + bufs[2:3] + (None,) + bufs[3:]
+    every, one, two = pl.ds(base, wide), pl.ds(0, at), pl.ds(at, wide - at)
+    low = jnp.bfloat16
+    load = pltpu.make_async_copy(grad.at[:, c, :, :, :, every], own, local)
+    load.start()
+    cross = sends.start(grad.at[:, 1 - c, :, :, :, every], got, "c")
+    yield
+    load.wait()
+    cross.wait_recv()
+
+    @pl.loop(0, 8)
+    def _(i):
+        own[i // 4, lax.rem(i, 4)] = (widen(own[i // 4, lax.rem(i, 4)]) + widen(got[i // 4, lax.rem(i, 4)])).astype(low)
+
+    if at:
+        a = sends.start(own.at[:, :, 1 - y, :, one], one1, "y")
+    b = sends.start(own.at[1 - x, :, :, :, two], two1, "x")
+    yield
+    if at:
+        a.wait_recv()
+
+        @pl.loop(0, 8)
+        def _(i):
+            one1[i // 4, lax.rem(i, 4)] = (
+                widen(own[i // 4, lax.rem(i, 4), y, :, :at]) + widen(one1[i // 4, lax.rem(i, 4)])
+            ).astype(low)
+
+        a2 = sends.start(one1.at[1 - x], one2, "x")
+    b.wait_recv()
+
+    @pl.loop(0, 4)
+    def _(i):
+        two1[i] = (widen(own[x, i, :, :, at:]) + widen(two1[i])).astype(low)
+
+    b2 = sends.start(two1.at[:, 1 - y], two2, "y")
+    yield
+    if at:
+        a2.wait_recv()
+    b2.wait_recv()
+
+    @pl.loop(0, 4)
+    def _(i):
+        if at:
+            line[i, :, :at] = (widen(one1[x, i]) + widen(one2[i])).astype(low)
+        line[i, :, at:] = (widen(two1[i, y]) + widen(two2[i])).astype(low)
+
+    last = [sends.start(line.at[other_z(z, k)], ends.at[k - 1], k) for k in (1, 2, 3)]
+    yield
+    for copy in last:
+        copy.wait_recv()
+    out[:, base : base + wide] = widen(line[z]) + widen(ends[0]) + widen(ends[1]) + widen(ends[2])
+    yield
+
+
+def scatter_bufs(rows, wide):
+    at = cut(wide)
+    shapes = [(2, 4, 2, rows, wide), (2, 4, 2, rows, wide)]
+    if at:
+        shapes += [(2, 4, rows, at), (4, 2, rows, wide - at), (4, rows, at)]
+    else:
+        shapes += [(4, 2, rows, wide)]
+    shapes += [(4, rows, wide - at), (4, rows, wide), (3, rows, wide)]
+    return [pltpu.VMEM(s, jnp.bfloat16) for s in shapes]
+
+
+def total_plan(values, result, bufs, sends):
+    current = values
+    for i, partner in enumerate(("c", "x", "y", 1, 2)):
+        copy = sends.start(current, bufs.at[2 * i], partner)
+        yield
+        copy.wait_recv()
+        target = result if i == 4 else bufs.at[2 * i + 1]
+        target[...] = current[...] + bufs[2 * i]
+        current = target
+    yield
+
+
+def scatter_kernel(plan, count, counts, extra, *refs):
+    grads, refs = refs[:count], refs[count:]
+    if extra:
+        edges, values, refs = refs[0], refs[1], refs[2:]
+    outs, refs = refs[:count], refs[count:]
+    if extra:
+        halo, result, refs = refs[0], refs[1], refs[2:]
+    send_sem, recv_sem, local_sem = refs[:3]
+    bufs = refs[3:]
+    to = partners()
+    sends = Sends(send_sem, recv_sem, to)
+    plans = []
+    if extra:
+        meet_all(to)
+        finish = halo_start(edges, halo, sends, local_sem.at[len(plan)])
+        steps = total_plan(values, result, bufs[-1], sends)
+    else:
+        meet(to)
+    for i, (k, base, wide) in enumerate(plan):
+        first = sum(counts[:i])
+        mine = bufs[first : first + counts[i]]
+        plans.append(scatter_plan(grads[k], outs[k], mine, sends, local_sem.at[i], base, wide))
+    run_staggered(plans)
+    if extra:
+        for _ in steps:
+            pass
+        finish()
+    sends.finish()
+
+
+def scatter_all(grads, parts, collective, extra=()):
+    count = len(grads)
+    grads = [v.reshape(2, 2, 4, 2, v.shape[0] // 32, v.shape[1]) for v in grads]
+    plan = pieces([v.shape[-1] for v in grads], parts)
+    bufs = [scatter_bufs(grads[k].shape[-2], wide) for k, base, wide in plan]
+    counts = [len(b) for b in bufs]
+    bufs = sum(bufs, [])
+    anywhere, vmem = pl.BlockSpec(memory_space=pl.ANY), pl.BlockSpec(memory_space=pltpu.VMEM)
+    shapes = [jax.ShapeDtypeStruct(v.shape[-2:], jnp.float32) for v in grads]
+    in_specs, out_specs = [anywhere] * count, [vmem] * count
+    number = len(plan) * SENDS
+    if extra:
+        in_specs, out_specs = in_specs + [anywhere, vmem], out_specs + [anywhere, vmem]
+        shapes += [jax.ShapeDtypeStruct(v.shape, v.dtype) for v in extra]
+        bufs.append(pltpu.VMEM((10, 8, 128), jnp.float32))
+        number += 7
+    return pl.pallas_call(
+        functools.partial(scatter_kernel, plan, count, counts, bool(extra)),
+        in_specs=in_specs,
+        out_specs=out_specs,
+        out_shape=shapes,
+        scratch_shapes=[
+            pltpu.SemaphoreType.DMA((number,)), pltpu.SemaphoreType.DMA((number,)), pltpu.SemaphoreType.DMA((len(plan) + 1,))
+        ] + bufs,
+        compiler_params=pltpu.CompilerParams(
+            collective_id=collective, has_side_effects=True, vmem_limit_bytes=58 << 20
+        ),
+        name="sum_gradients",
+    )(*grads, *extra)
+
+
 H = 16
 MAXLEN = 512
 TSTEPS = 5000
@@ -260,76 +627,6 @@
 
 def row_dot(left, right):
     return lax.dot_general(left, right, (((0,), (0,)), ((), ())), preferred_element_type=jnp.float32)
-
-
-def place():
-    seq, blk = lax.axis_index("seq"), lax.axis_index("blk")
-    return seq // 2, seq % 2, blk // 2, blk % 2
-
-
-def swap(value, dx=0, dc=0, dz=0, dy=0):
-    pairs = []
-    for i in range(32):
-        seq, blk = i // 8, i % 8
-        seq, blk = seq ^ (2 * dx + dc), blk ^ (2 * dz + dy)
-        pairs.append((i, seq * 8 + blk))
-    return lax.ppermute(value, AXES, pairs)
-
-
-def ordered(bit, own, other, axis):
-    return jnp.where(bit == 0, jnp.stack([own, other], axis), jnp.stack([other, own], axis))
-
-
-def cut(columns):
-    return columns // 256 * 128
-
-
-def gather_rows(shard):
-    x, c, z, y = place()
-    parts = [shard] + [swap(shard, dz=k) for k in (1, 2, 3)]
-    parts = [jnp.where(z % 2 == 0, parts[i], parts[i ^ 1]) for i in range(4)]
-    line = jnp.stack([jnp.where(z < 2, parts[i], parts[i ^ 2]) for i in range(4)])
-    at = cut(shard.shape[1])
-    one, two = line[..., :at], line[..., at:]
-    one = ordered(x, one, swap(one, dx=1), 0)
-    two = ordered(y, two, swap(two, dy=1), 1)
-    one = ordered(y, one, swap(one, dy=1), 2)
-    two = ordered(x, two, swap(two, dx=1), 0)
-    mine = jnp.concatenate([one, two], axis=-1)
-    return mine, swap(mine, dc=1)
-
-
-def gather(shard):
-    mine, other = gather_rows(shard)
-    full = ordered(place()[1], mine, other, 1)
-    return full.reshape(-1, shard.shape[1])
-
-
-def pick(value, index, axis):
-    return lax.dynamic_index_in_dim(value, index, axis, keepdims=False)
-
-
-def scatter_sum(value):
-    x, c, z, y = place()
-    value = value.reshape(2, 2, 4, 2, value.shape[0] // 32, value.shape[1])
-    total = as_float(pick(value, c, 1)) + as_float(swap(pick(value, 1 - c, 1), dc=1))
-    at = cut(value.shape[-1])
-    one, two = low(total[..., :at]), low(total[..., at:])
-    one = low(as_float(pick(one, y, 2)) + as_float(swap(pick(one, 1 - y, 2), dy=1)))
-    two = low(as_float(pick(two, x, 0)) + as_float(swap(pick(two, 1 - x, 0), dx=1)))
-    one = low(as_float(pick(one, x, 0)) + as_float(swap(pick(one, 1 - x, 0), dx=1)))
-    two = low(as_float(pick(two, y, 1)) + as_float(swap(pick(two, 1 - y, 1), dy=1)))
-    line = jnp.concatenate([one, two], axis=-1)
-    total = as_float(pick(line, z, 0))
-    for k in (1, 2, 3):
-        total = total + as_float(swap(pick(line, z ^ k, 0), dz=k))
-    return total
-
-
-def total_of(values):
-    for step in (dict(dc=1), dict(dx=1), dict(dy=1), dict(dz=1), dict(dz=2)):
-        values = values + swap(values, **step)
-    return values
 
 
 def neighbours(low_part, high_part):
@@ -374,22 +671,22 @@
     keep_own = low(padding)
     edge_low = jnp.concatenate([inputs[:half], mark.at[0, :half].set(keep_own[:half])])
     edge_high = jnp.concatenate([inputs[tok - half :], mark.at[0, :half].set(keep_own[tok - half :])])
-    from_low, from_high = neighbours(edge_low, edge_high)
 
     if fast:
         rows = time_weight.shape[0]
         cols = [v[:, None] for v in small] + [upward_bias.reshape(-1, rows).T]
         cols = jnp.concatenate(cols, axis=1)
         cols = jnp.pad(cols, ((0, 0), (0, 128 - cols.shape[1])))
-        first = gather(jnp.concatenate([inproj, cols], axis=1))
-        second = gather(jnp.concatenate([outproj, upward_w], axis=1))
-        downward_f = gather(downward_w)
-        inproj_f = first[:, : 3 * width]
-        small_f = as_float(first[:, 3 * width :].T)
+        *fulls, halo = gather_all(
+            (inproj, cols, outproj, upward_w, downward_w), (1, 1, 1, 2, 2), jnp.stack([edge_low, edge_high]), 0
+        )
+        inproj_f, small_f, outproj_f, upward_f, downward_f = [v.reshape(-1, v.shape[-1]) for v in fulls]
+        small_f = as_float(small_f.T)
+        from_low, from_high = halo[0], halo[1]
         upward_bias_f = small_f[SMALL : SMALL + hidden // width]
         upward_bias_f = upward_bias_f.reshape(-1, width // rows, rows).transpose(1, 0, 2).reshape(hidden)
-        outproj_f, upward_f = second[:, :width], second[:, width:]
     else:
+        from_low, from_high = neighbours(edge_low, edge_high)
         whole = lambda v: lax.all_gather(v, AXES, axis=0, tiled=True)
         inproj_f, outproj_f, upward_f, downward_f = map(whole, (inproj, outproj, upward_w, downward_w))
         small_f = [as_float(whole(v)) for v in small]
@@ -427,8 +724,6 @@
     second_normal, second_inv = norm_forward(first_out + ffn_branch)
     layer_out = low(second_normal * second_gain_f + second_shift_f)
     sums = jnp.stack([jnp.sum(v * v) for v in (start_vec, attn_branch, ffn_branch)])
-    sums = total_of(sums) if fast else lax.psum(sums, AXES)
-    branch_rms = jnp.sqrt(sums / (tok * width * lax.axis_size(AXES)))
 
     grad_second_in, grad_second_gain, grad_second_shift = norm_backward(
         as_float(cotangent), second_normal, second_inv, second_gain_f
@@ -454,7 +749,16 @@
         [query_feat_own[:, lane : lane + 48], delta_features(delta, 0)[:, :48], jnp.zeros((tok, 32), jnp.bfloat16)], axis=1
     )
     packed = jnp.concatenate([grad_attended, stats], axis=1)
-    back_low, back_high = neighbours(packed[:half], packed[tok - half :])
+    if fast:
+        grads = [low(v) for v in (grad_out_weight, grad_up_weight, grad_down_weight)]
+        values = jnp.pad(sums[None], ((0, 7), (0, 125)))
+        edges = jnp.stack([packed[:half], packed[tok - half :]])
+        out_share, up_share, down_share, back, sums = scatter_all(grads, (1, 2, 2), 1, (edges, values))
+        back_low, back_high, sums = back[0], back[1], sums[0, :3]
+    else:
+        back_low, back_high = neighbours(packed[:half], packed[tok - half :])
+        sums = lax.psum(sums, AXES)
+    branch_rms = jnp.sqrt(sums / (tok * width * lax.axis_size(AXES)))
     packed = jnp.concatenate([back_low, packed, back_high])
     grad_ext = packed[:, :width]
     query_feat = jnp.concatenate([query_feat[:, :lane], packed[:, width : width + 48], query_feat[:, lane + 48 :]], axis=1)
@@ -473,16 +777,12 @@
     small_grads = (grad_time_weight, grad_time_bias, grad_query_bias, grad_value_bias, grad_out_bias, grad_first_gain,
                    grad_first_shift, grad_down_bias, grad_second_gain, grad_second_shift)
     if fast:
-        down_share = scatter_sum(low(grad_down_weight))
-        up_share = scatter_sum(low(grad_up_weight))
-        out_share = scatter_sum(low(grad_out_weight))
         cols = grad_up_bias.reshape(width // rows, -1, rows).transpose(1, 0, 2).reshape(-1, width)
         cols = jnp.concatenate([jnp.stack(small_grads), cols]).T
         cols = jnp.pad(cols, ((0, 0), (0, 128 - cols.shape[1])))
-        last = scatter_sum(low(jnp.concatenate([grad_in_weight, cols], axis=1)))
-        in_share = last[:, : 3 * width]
-        small_shares = [last[:, 3 * width + i] for i in range(SMALL)]
-        up_bias_share = last[:, 3 * width + SMALL : 3 * width + SMALL + hidden // width].T.reshape(-1)
+        in_share, last = scatter_all((low(grad_in_weight), low(cols)), (3, 1), 2)
+        small_shares = [last[:, i] for i in range(SMALL)]
+        up_bias_share = last[:, SMALL : SMALL + hidden // width].T.reshape(-1)
     else:
         share = lambda v: lax.psum_scatter(v, AXES, scatter_dimension=0, tiled=True)
         down_share, up_share, out_share, in_share, up_bias_share = map(

time: 981 us -> 864 us (0.88)
  Pallas kernels: 171 us -> 595 us
  waiting for transfers between devices: 232 us -> 0 us
  starting transfers between devices: 179 us -> 0 us
  other arithmetic: 138 us -> 49.6 us
  local copies, waits for them, and re-layouts: 90.9 us -> 56 us
    pallas_call x0 -> x3, Pallas kernels: none -> 398 us  [the longest x2 239 us: scatter_all(): pl.pallas_call(functools.partial(scatter_kernel, plan, count, counts, boo...]
    ppermute x65 -> x0, waiting for transfers between devices: 232 us -> none  [the longest x61 232 us: swap(): return lax.ppermute(value, AXES, pairs)]
    ppermute x65 -> x0, starting transfers between devices: 179 us -> none  [the longest x61 163 us: swap(): return lax.ppermute(value, AXES, pairs)]
    select_n x18 -> x0, other arithmetic: 34.2 us -> none  [ordered(): jnp.where(bit == 0, jnp.stack([own, other], axis), jnp.stack([other, own]...]
    another operation x28 -> x10, other arithmetic: 39.2 us -> 7.66 us
    dynamic_slice x6 -> x0, local copies, waits for them, and re-layouts: 20.3 us -> none  [pick(): return lax.dynamic_index_in_dim(value, index, axis, keepdims=False)]
    pallas_call x1, Pallas kernels: 110 us -> 127 us  [attn_bwd(): pl.pallas_call(functools.partial(bwd_kernel, tiles, lse_lane), grid_spec=...]
    unnamed x116 -> x107, local copies, waits for them, and re-layouts: 25.6 us -> 23.5 us
  transfers between devices with their start and end apart: 65 -> 0, of which waited for: 23 -> 0; matrix products, arithmetic and copies ran while one was open for 25% -> 0% of each run, Pallas kernels for 18% -> 0%
where the time goes in v2:
time: 864 us; the launch traced here: 858 us
  Pallas kernels  595 us (69%)
  matrix products  155 us (18%)
  local copies, waits for them, and re-layouts  56 us (6%)
  other arithmetic  49.6 us (6%)
    pallas_call x2, Pallas kernels, scatter_all(): pl.pallas_call(functools.partial(scatter_kernel, plan, count, counts, boo...  239 us
    pallas_call x1, Pallas kernels, gather_all(): pl.pallas_call(functools.partial(gather_kernel, plan, count), in_specs=[a...  160 us
    pallas_call x1, Pallas kernels, attn_bwd(): pl.pallas_call(functools.partial(bwd_kernel, tiles, lse_lane), grid_spec=...  127 us
    pallas_call x1, Pallas kernels, attn_fwd(): pl.pallas_call(functools.partial(fwd_kernel, tiles, lse_lane), grid_spec=...  69.7 us
    dot_general x4, matrix products, nt(): lax.dot_general(a, b, (((1,), (1,)), ((), ())), preferred_element_type=jn...  47.5 us
    dot_general x4, matrix products, row_dot(): lax.dot_general(left, right, (((0,), (0,)), ((), ())), preferred_element_...  43.2 us
    unnamed x107, local copies, waits for them, and re-layouts  23.5 us
    dot_general x1, matrix products, per_device(): jnp.dot(first_low, upward_f, preferred_element_type=jnp.float32)  20.4 us

profile of v2, /device:TPU:0, one launch (start us, length us, event | category | flops | bytes accessed | tf_op | source)
XLA Modules:
  0.0 857.7 jit_solution(14667028985512222398)
XLA Ops:
  0.8 4.1 copy.178
  6.2 0.6 pad.28.refs_1_
  7.3 1.5 pad_maximum_fusion.5.refs_5_
  8.8 159.9 %gather_weights.1 = (bf16[2,2,4,2,32,3072]{5,4,3,2,1,0:T(8,128)(2,1)}, bf16[2,2,4,2,32,128]{5,4,3,2,1,0:T(8,128)(2,1)}, bf16[2,2,4,2,32,1024]{5,4,3,2,1,0:T(8,12...) custom-call(bf16[32,3072]{1,0:T(8,128)(2,1)} %refs_0_.1, ...), custom_call_target="tpu_custom_call" | custom-call | tf_op jit(solution)/shard_map/gather_weights/pallas_call | solution.py:453
  168.7 1.1 bitcast_convert_fusion
  170.8 4.1 copy.158
  175.8 1.6 fusion.31
  177.3 2.3 copy.173
  179.6 3.5 fusion.23
  183.1 1.3 copy.172
  184.4 19.3 %add_convert_fusion.q_ref.k_ref.v_ref = bf16[2048,3072]{1,0:T(8,128)(2,1)} fusion(bf16[1024,3072]{1,0:T(8,128)(2,1)} %bitcast.143, f32[3072]{0:T(1024)S(1)} %pad_maximum_fusion.9, bf16[512,1024]{0,1:T(8,128)(2,1)} %copy.173, bf16[1024,1024]{0,1:T(8,128)(2,1)} %fusion.23, bf16[512,1024]{0,1:T(8,128)(2,1)} %copy.172), kind=kOutput, calls=%fused_computation.1 | convolution fusion | flops 12910067712 | bytes 23080960 | tf_op jit(solution)/shard_map/dot_general | solution.py:712
  203.9 1.1 convert_convert_fusion.1
  205.3 1.5 multiply_convert_fusion.3
  207.3 1.4 multiply_convert_fusion.1
  208.8 2.8 concatenate.70.qf_ref
  211.8 0.8 copy-done.12
  212.6 3.1 concatenate.74.kf_ref
  215.7 69.7 %attn_fwd.1 = (bf16[1024,1024]{1,0:T(8,128)(2,1)S(1)}, bf16[1024,128]{1,0:T(8,128)(2,1)S(1)}) custom-call(s32[4]{0:T(128)S(1)} %get-tuple-element.190.lo_ref, s32[4]{0:T(128)S(1)} %get-tuple-element.189.n_ref, bf16[2048,3072]{1,0:T(8,128)(2,1)} %add_convert_fusion.q_ref.k_ref.v_ref, bf16[2048,3072]{1,0:T(8,128)(2,1)} %add_convert_fusion.q_ref.k_ref.v_ref, ...), custom_call_target="tpu_custom_call" | custom-call | flops 6442450944 | bytes 8388608 | tf_op jit(solution)/shard_map/attn_fwd/pallas_call | solution.py:86
  285.5 4.6 fusion.63
  290.1 2.1 copy-done.5
  292.6 0.8 slice.237
  293.6 20.4 %multiply_convert_fusion = (bf16[1024,4096]{1,0:T(8,128)(2,1)}, f32[1024,4096]{1,0:T(8,128)}) fusion(f32[4096]{0:T(1024)S(1)} %add.253, bf16[1024,4096]{1,0:T(8,128)(2,1)} %bitcast.139, f32[1024,1024]{0,1:T(8,128)} %copy-done.5, f32[1024]{0:T(1024)S(1)} %bitcast.123, f32[1024]{0:T(1024)S(1)} %bitcast.115, f32[1024]{0:T(1024)S(1)} %add_rsqrt_fusion.1, ...), kind=kOutput, calls=%fused_computation.8 | convolution fusion | flops 8620343296 | bytes 37781504 | tf_op jit(solution)/shard_map/dot_general | solution.py:719
  314.1 17.2 %fusion.62 = (f32[1024]{0:T(1024)S(1)}, f32[1024,1024]{0,1:T(8,128)}, f32[]{:T(128)}) fusion(f32[1024]{0:T(1024)S(1)} %bitcast.126, f32[1024]{0:T(1024)S(1)} %bitcast.124, f32[1024]{0:T(1024)S(1)} %bitcast.116, f32[1024]{0:T(1024)S(1)} %add_rsqrt_fusion.1, f32[1024,1024]{0,1:T(8,128)} %copy-done.5, f32[1024]{0:T(1024)S(1)} %broadcast_multiply_fusion.5, ...), kind=kOutput, calls=%fused_computation.171 | convolution fusion | flops 8599370752 | bytes 25190404 | tf_op jit(solution)/shard_map/dot_general | solution.py:723
  331.3 2.8 multiply_reduce_fusion.5
  334.1 0.6 copy-done
  334.7 5.1 fusion.12
  339.8 3.9 copy.188
  343.8 5.0 fusion.60
  348.8 20.3 %fusion.71 = (bf16[4096]{0:T(1024)(128)(2,1)}, bf16[1024,4096]{1,0:T(8,128)(2,1)}) fusion(f32[1024,4096]{1,0:T(8,128)} %get-tuple-element.235, f32[4096]{0:T(1024)S(1)} %add.253, bf16[1024,1024]{0,1:T(8,128)(2,1)S(1)} %get-tuple-element.182, bf16[4096,1024]{1,0:T(8,128)(2,1)} %bitcast.142), kind=kOutput, calls=%fused_computation.179 | convolution fusion | flops 8640262144 | bytes 35676160 | tf_op jit(solution)/shard_map/dot_general | solution.py:15
  369.1 17.7 %multiply_reduce_fusion = (bf16[1024]{0:T(1024)(128)(2,1)S(1)}, f32[1024]{0:T(1024)S(1)}, f32[1024]{0:T(1024)S(1)}, bf16[1024]{0:T(1024)(128)(2,1)S(1)}, f32[1024,1024]{0,1:T(8,128)}) fusion(f32[1024,1024]{0,1:T(8,128)S(1)} %copy-done.6, f32[1024]{0:T(1024)S(1)} %add_rsqrt_fusion.1, f32[1024]{0:T(1024)S(1)} %broadcast_multiply_fusion.5, ...), kind=kOutput, calls=%fused_computation.29 | convolution fusion | flops 8608804864 | bytes 31502336 | tf_op jit(solution)/shard_map/dot_general | solution.py:15
  386.8 3.8 convert_reduce_fusion.1
  390.6 3.7 convolution_convert_fusion.4
  394.4 0.7 slice-done.3
  395.1 11.7 %convolution_convert_fusion.1 = bf16[1024,4096]{1,0:T(8,128)(2,1)} fusion(bf16[1024,4096]{1,0:T(8,128)(2,1)S(1)} %bitcast.150, f32[1024,1024]{0,1:T(8,128)S(1)} %copy-done.6, f32[1024]{0:T(1024)S(1)} %bitcast.125, f32[1024]{0:T(1024)S(1)} %bitcast.119, f32[1024]{0:T(1024)S(1)} %add_rsqrt_fusion.1, f32[1024]{0:T(1024)S(1)} %broadcast_multiply_fusion.5), kind=kOutput, calls=%fused_computation.11 | convolution fusion | flops 8599371776 | bytes 20987904 | tf_op jit(solution)/shard_map/dot_general | solution.py:629
  406.8 14.8 %convolution_convert_fusion = bf16[4096,1024]{1,0:T(8,128)(2,1)} fusion(bf16[1024,4096]{1,0:T(8,128)(2,1)} %get-tuple-element.234, bf16[1024,1024]{0,1:T(8,128)(2,1)S(1)} %copy-done.19), kind=kOutput, calls=%fused_computation.10 | convolution fusion | flops 8594128896 | bytes 18874368 | tf_op jit(solution)/shard_map/dot_general | solution.py:629
  421.6 2.4 convolution_convert_fusion.3
  424.2 2.4 fusion.70
  427.2 0.9 subtract_convert_fusion
  428.0 0.7 broadcast_in_dim.127
  428.8 4.1 concatenate.75
  433.1 1.6 pad_maximum_fusion.4.refs_3_
  434.7 2.0 maximum_bitcast_fusion
  437.3 168.6 %sum_gradients.2 = (f32[32,1024]{1,0:T(8,128)}, f32[32,4096]{1,0:T(8,128)}, f32[128,1024]{1,0:T(8,128)}, bf16[2,512,1152]{2,1,0:T(8,128)(2,1)}, f32[8,128]{1,0:T(8,128)}) custom-call(bf16[2,2,4,2,32,1024]{5,4,3,2,1,0:T(8,128)(2,1)} %bitcast.98, bf16[2,2,4,2,32,4096]{5,4,3,2,1,0:T(8,128)(2,1)} %bitcast.95, bf16[2,2,4,2,128,1024]{5,4,3,2,1,0:T(8,128)(2,1)} %bitcast.96, ...), custom_call_target="tpu_custom_call" | custom-call | tf_op jit(solution)/shard_map/sum_gradients/pallas_call | solution.py:598
  605.9 1.8 slice_bitcast_fusion.6
  607.8 7.4 pad_maximum_fusion.1
  615.2 2.7 slice.243.d_ref
  617.9 0.8 pad_maximum_fusion.8
  618.7 3.3 concatenate.77.qf_ref
  622.0 1.4 fusion.44.df_ref
  623.5 126.8 %attn_bwd.1 = bf16[3,1024,1024]{2,1,0:T(8,128)(2,1)} custom-call(s32[4]{0:T(128)S(1)} %get-tuple-element.190.lo_ref, s32[4]{0:T(128)S(1)} %get-tuple-element.189.n_ref, bf16[2048,3072]{1,0:T(8,128)(2,1)} %add_convert_fusion.q_ref.k_ref.v_ref, bf16[2048,3072]{1,0:T(8,128)(2,1)} %add_convert_fusion.q_ref.k_ref.v_ref, ...), custom_call_target="tpu_custom_call" | custom-call | flops 12884901888 | bytes 16777216 | tf_op jit(solution)/shard_map/attn_bwd/pallas_call | solution.py:172
  750.4 3.8 slice_reduce_fusion
  754.4 7.1 fusion.65
  761.5 2.6 copy.189
  764.1 12.9 %convolution_convert_fusion.2 = bf16[1024,3072]{1,0:T(8,128)(2,1)} fusion(bf16[1024,1024]{0,1:T(8,128)(2,1)} %fusion.23, bf16[1024,1024]{1,0:T(8,128)(2,1)} %copy-done.20, bf16[1024,1024]{1,0:T(8,128)(2,1)} %copy-done.21, bf16[1024,1024]{1,0:T(8,128)(2,1)} %copy-done.22), kind=kOutput, calls=%fused_computation.13 | convolution fusion | flops 6464471040 | bytes 14680064 | tf_op jit(solution)/shard_map/dot_general | solution.py:629
  778.1 0.8 pad.31.clone
  778.8 70.0 %sum_gradients.3 = (f32[32,3072]{1,0:T(8,128)}, f32[32,128]{1,0:T(8,128)}) custom-call(bf16[2,2,4,2,32,3072]{5,4,3,2,1,0:T(8,128)(2,1)} %bitcast.97, bf16[2,2,4,2,32,128]{5,4,3,2,1,0:T(8,128)(2,1)} %bitcast.99), custom_call_target="tpu_custom_call" | custom-call | tf_op jit(solution)/shard_map/sum_gradients/pallas_call | solution.py:598
  848.8 2.0 slice_reduce_fusion.3
  850.8 0.8 slice_bitcast_fusion.9
  851.6 0.6 reshape.337
  852.2 1.2 sqrt_bitcast_fusion
  853.4 1.8 copy.202
  855.2 0.7 copy.203
  855.9 0.8 copy.204
  856.7 0.8 copy.205
  (180 shorter events, 7.5 us)
Async XLA Ops:
  0.7 4.2 copy-start.31
  0.7 4.3 copy-start.32
  0.7 4.4 copy-start.33
  0.7 4.5 copy-start.34
  0.7 4.6 copy-start.35
  0.7 4.7 copy-start.36
  0.7 4.8 copy-start.37
  0.7 4.9 copy-start.38
  0.7 5.0 copy-start.39
  0.8 5.1 copy-start.40
  0.8 5.2 copy-start.44
  0.8 6.1 copy-start.30
  0.8 6.1 copy-start.8
  8.8 166.1 %copy-start.41 = (s32[1,32]{1,0:T(1,128)S(1)}, s32[1,32]{1,0:T(1,128)}, u32[]{:S(2)}) copy-start(s32[1,32]{1,0:T(1,128)} %param.27) | copy-start | bytes 388
  168.7 7.1 copy-start.7
  170.1 5.7 copy-start.23
  206.8 4.8 copy-start.13
  207.3 4.5 copy-start.14
  208.7 3.0 copy-start.15
  211.8 0.8 copy-start.12
  215.7 69.8 %copy-start.10 = (bf16[1024,1024]{0,1:T(8,128)(2,1)S(1)}, bf16[1024,1024]{0,1:T(8,128)(2,1)}, u32[]{:S(2)}) copy-start(bf16[1024,1024]{0,1:T(8,128)(2,1)} %copy.158) | copy-start | bytes 6291460
  215.7 69.8 %copy-start.42 = (bf16[2,2,4,2,32,1024]{5,4,3,2,1,0:T(8,128)(2,1)S(1)}, bf16[2,2,4,2,32,1024]{5,4,3,2,1,0:T(8,128)(2,1)}, u32[]{:S(2)}) copy-start(bf16[2,2,4,2,32,1024]{5,4,3,2,1,0:T(8,128)(2,1)} %get-tuple-element.61) | copy-start | bytes 6291460
  290.1 2.1 copy-start.5
  331.3 3.4 copy-start
  348.8 20.3 %copy-start.18 = (bf16[1024,1024]{0,1:T(8,128)(2,1)}, bf16[1024,1024]{0,1:T(8,128)(2,1)S(1)}, u32[]{:S(2)}) copy-start(bf16[1024,1024]{0,1:T(8,128)(2,1)S(1)} %get-tuple-element.182) | copy-start | bytes 6291460
  348.8 20.3 %copy-start.1 = (f32[1024,1024]{0,1:T(8,128)S(1)}, f32[1024,1024]{0,1:T(8,128)}, u32[]{:S(2)}) copy-start(f32[1024,1024]{0,1:T(8,128)} %get-tuple-element.186) | copy-start | bytes 12582916
  348.8 20.3 %copy-start.4 = (bf16[1024,1024]{0,1:T(8,128)(2,1)S(1)}, bf16[1024,1024]{0,1:T(8,128)(2,1)}, u32[]{:S(2)}) copy-start(bf16[1024,1024]{0,1:T(8,128)(2,1)} %copy.178) | copy-start | bytes 6291460
  348.8 20.3 %copy-start.6 = (f32[1024,1024]{0,1:T(8,128)S(1)}, f32[1024,1024]{0,1:T(8,128)}, u32[]{:S(2)}) copy-start(f32[1024,1024]{0,1:T(8,128)} %copy-done.5) | copy-start | bytes 12582916
  386.8 7.5 slice-start.2
  390.6 31.0 %copy-start.16 = (f32[1024,1024]{0,1:T(8,128)}, f32[1024,1024]{0,1:T(8,128)S(1)}, u32[]{:S(2)}) copy-start(f32[1024,1024]{0,1:T(8,128)S(1)} %get-tuple-element.184) | copy-start | bytes 12582916
  390.6 4.5 slice-start.3
  395.1 11.7 %copy-start.19 = (bf16[1024,1024]{0,1:T(8,128)(2,1)S(1)}, bf16[1024,1024]{0,1:T(8,128)(2,1)}, u32[]{:S(2)}) copy-start(bf16[1024,1024]{0,1:T(8,128)(2,1)} %copy-done.18) | copy-start | bytes 6291460
  406.8 14.8 %copy-start.43 = (bf16[2,2,4,2,32,1024]{5,4,3,2,1,0:T(8,128)(2,1)S(1)}, bf16[2,2,4,2,32,1024]{5,4,3,2,1,0:T(8,128)(2,1)}, u32[]{:S(2)}) copy-start(bf16[2,2,4,2,32,1024]{5,4,3,2,1,0:T(8,128)(2,1)} %get-tuple-element.61) | copy-start | bytes 6291460
  424.1 2.6 copy-start.11
  607.7 10.1 %copy-start.2 = (bf16[512,1152]{1,0:T(8,128)(2,1)}, bf16[512,1152]{1,0:T(8,128)(2,1)S(1)}, u32[]{:S(2)}) copy-start(bf16[512,1152]{1,0:T(8,128)(2,1)S(1)} %get-tuple-element.199) | copy-start | bytes 3538948
  607.8 10.1 %copy-start.3 = (bf16[512,1152]{1,0:T(8,128)(2,1)}, bf16[512,1152]{1,0:T(8,128)(2,1)S(1)}, u32[]{:S(2)}) copy-start(bf16[512,1152]{1,0:T(8,128)(2,1)S(1)} %get-tuple-element.200) | copy-start | bytes 3538948
  622.0 132.2 %slice-start = ((s8[6291456]{0:T(1024)(128)(4,1)}), s8[4194304]{0:T(1024)(128)(4,1)S(1)}, s32[]{:S(2)}) async-start(s8[6291456]{0:T(1024)(128)(4,1)} %bitcast.144), calls=%async_computation | async-start | bytes 8388608
  623.5 130.7 %slice-start.1 = ((s8[6291456]{0:T(1024)(128)(4,1)}), s8[2097152]{0:T(1024)(128)(4,1)S(1)}, s32[]{:S(2)}) async-start(s8[6291456]{0:T(1024)(128)(4,1)} %bitcast.144), calls=%async_computation.1 | async-start | bytes 4194304
  750.4 4.1 copy-start.17
  754.2 7.3 copy-start.20
  754.2 7.3 copy-start.21
  754.2 7.3 copy-start.22
  764.1 13.0 %copy-start.27 = (bf16[1024]{0:T(1024)(128)(2,1)S(1)}, bf16[1024]{0:T(1024)(128)(2,1)}, u32[]{:S(2)}) copy-start(bf16[1024]{0:T(1024)(128)(2,1)} %get-tuple-element.181) | copy-start | bytes 6148
  764.1 13.1 %copy-start.29 = (bf16[1024]{0:T(1024)(128)(2,1)S(1)}, bf16[1024]{0:T(1024)(128)(2,1)}, u32[]{:S(2)}) copy-start(bf16[1024]{0:T(1024)(128)(2,1)} %get-tuple-element.164) | copy-start | bytes 6148
  764.1 13.1 %copy-start.9 = (bf16[1024,1024]{1,0:T(8,128)(2,1)S(1)}, bf16[1024,1024]{1,0:T(8,128)(2,1)}, u32[]{:S(2)}) copy-start(bf16[1024,1024]{1,0:T(8,128)(2,1)} %param.25) | copy-start | bytes 6291460
  764.1 13.5 %copy-start.28 = (bf16[4096]{0:T(1024)(128)(2,1)S(1)}, bf16[4096]{0:T(1024)(128)(2,1)}, u32[]{:S(2)}) copy-start(bf16[4096]{0:T(1024)(128)(2,1)} %get-tuple-element.240) | copy-start | bytes 24580
  777.9 77.3 %copy-start.26 = (f32[32,1024]{1,0:T(8,128)S(1)}, f32[32,1024]{1,0:T(8,128)}, u32[]{:S(2)}) copy-start(f32[32,1024]{1,0:T(8,128)} %get-tuple-element.271) | copy-start | bytes 393220
  778.1 77.8 %copy-start.25 = (f32[32,4096]{1,0:T(8,128)S(1)}, f32[32,4096]{1,0:T(8,128)}, u32[]{:S(2)}) copy-start(f32[32,4096]{1,0:T(8,128)} %get-tuple-element.275) | copy-start | bytes 1572868
  778.8 77.8 %copy-start.24 = (f32[128,1024]{1,0:T(8,128)S(1)}, f32[128,1024]{1,0:T(8,128)}, u32[]{:S(2)}) copy-start(f32[128,1024]{1,0:T(8,128)} %get-tuple-element.277) | copy-start | bytes 1572868

commit v3 on v2

v3 whole, which is shorter than its diff:
```python
import functools

import jax
import jax.numpy as jnp
from jax import lax
from jax.experimental import pallas as pl
from jax.experimental.pallas import tpu as pltpu
from jax.sharding import PartitionSpec as P

HD = 64
TQ = 256
PAIR = 2 * HD
NEG = -(2.0**100)


def nt(a, b):
    return lax.dot_general(a, b, (((1,), (1,)), ((), ())), preferred_element_type=jnp.float32)


def nn(a, b):
    return jnp.dot(a, b, preferred_element_type=jnp.float32)


def schedule(step, steps, job, length):
    at = [i * steps // length for i in range(length)]
    for s in range(steps):
        count = at.count(s)
        if count or s == steps - 1:

            @pl.when(step == s)
            def _():
                for _ in range(count):
                    next(job)


def fwd_kernel(plan, count, tok, lanes, *refs):
    shards, refs = refs[:count], refs[count:]
    start_ref, wq, wk, wv, bias_ref, qf_ref, kf_ref, refs = *refs[:7], refs[7:]
    fulls, refs = refs[:count], refs[count:]
    proj_ref, o_ref, f_ref, ka, va, qa = refs[:6]
    step = pl.program_id(0)
    ext = start_ref.shape[0]
    half = (ext - tok) // 2
    window = 2 * half + TQ
    if count:
        send_sem, recv_sem, local_sem = refs[6:]
        pos = Place()

        @pl.when(step == 0)
        def _():
            meet(pos, False)

        sends = Sends(send_sem, recv_sem, pos.to)
        schedule(step, FWD_STEPS, gather_job(pos, plan, shards, fulls, sends, local_sem), len(plan) + 4)

    @pl.when(step == 0)
    def _():
        ka[:, PAIR:] = kf_ref[...]
        va[:, PAIR:] = jnp.ones((ext, PAIR), jnp.bfloat16)
        f_ref[...] = qf_ref[half : half + tok, :]

    lane = lax.broadcasted_iota(jnp.int32, (TQ, PAIR), 1)
    left = lane < HD
    for t in range(ext // TQ):
        rows = slice(t * TQ, (t + 1) * TQ)
        start = start_ref[rows, :]
        q = (nn(start, wq[...]) + bias_ref[0:1, :]).astype(jnp.bfloat16)
        k = (nn(start, wk[...]) + bias_ref[1:2, :]).astype(jnp.bfloat16)
        v = (nn(start, wv[...]) + bias_ref[2:3, :]).astype(jnp.bfloat16)
        proj_ref[0, rows, :] = q
        proj_ref[1, rows, :] = k
        proj_ref[2, rows, :] = v
        ka[rows, :PAIR] = k
        va[rows, :PAIR] = v
        if half <= t * TQ < half + tok:
            own = t - half // TQ
            q = q * jnp.bfloat16(HD**-0.5)
            zero = jnp.zeros_like(q)
            qa[2 * own, :, :PAIR] = jnp.where(left, q, zero)
            qa[2 * own + 1, :, :PAIR] = jnp.where(left, zero, q)
            qa[2 * own, :, PAIR:] = qf_ref[rows, :]
            qa[2 * own + 1, :, PAIR:] = qf_ref[rows, :]
    for t in range(tok // TQ):
        win = slice(t * TQ, t * TQ + window)
        own = slice(t * TQ, (t + 1) * TQ)
        feat = f_ref[own, :]
        out = []
        for side in range(2):
            s = nt(qa[2 * t + side], ka[win, :])
            top = jnp.max(s, axis=1, keepdims=True)
            r = nn(jnp.exp(s - top).astype(jnp.bfloat16), va[win, :])
            total = r[:, PAIR:]
            out.append(r[:, :PAIR] / total)
            rest = top + jnp.log(total)
            for part in range(3):
                piece = rest.astype(jnp.bfloat16)
                rest = rest - piece.astype(jnp.float32)
                feat = jnp.where(lane == lanes + part * 16 + 2 * step + side, piece, feat)
        o_ref[own, :] = jnp.where(left, out[0], out[1]).astype(jnp.bfloat16)
        f_ref[own, :] = feat


FWD_STEPS = 8


def attn_fwd(start, inproj, bias, qf, kf, lanes, tok, shards=(), parts=(), share=0.0, collective=None):
    ext, width = start.shape
    pairs = width // PAIR
    count = len(shards)
    plan = pieces([v.shape[1] for v in shards], parts, share)
    anywhere = pl.BlockSpec(memory_space=pl.ANY)
    col = lambda base: pl.BlockSpec((width, PAIR), lambda i: (0, base + i))
    fix = pl.BlockSpec((ext, PAIR), lambda i: (0, 0))
    comm = dict(collective_id=collective, has_side_effects=True) if count else {}
    return pl.pallas_call(
        functools.partial(fwd_kernel, plan, count, tok, lanes),
        grid=(pairs,),
        in_specs=[anywhere] * count
        + [pl.BlockSpec((ext, width), lambda i: (0, 0)), col(0), col(pairs), col(2 * pairs),
           pl.BlockSpec((8, PAIR), lambda i: (0, i)), fix, fix],
        out_specs=[anywhere] * count
        + [pl.BlockSpec((3, ext, PAIR), lambda i: (0, 0, i)), pl.BlockSpec((tok, PAIR), lambda i: (0, i)),
           pl.BlockSpec((tok, PAIR), lambda i: (0, 0))],
        out_shape=full_shapes(shards)
        + [jax.ShapeDtypeStruct((3, ext, width), jnp.bfloat16), jax.ShapeDtypeStruct((tok, width), jnp.bfloat16),
           jax.ShapeDtypeStruct((tok, PAIR), jnp.bfloat16)],
        scratch_shapes=[
            pltpu.VMEM((ext, 2 * PAIR), jnp.bfloat16),
            pltpu.VMEM((ext, 2 * PAIR), jnp.bfloat16),
            pltpu.VMEM((2 * tok // TQ, TQ, 2 * PAIR), jnp.bfloat16),
        ] + (semaphores(len(plan) * SENDS, len(plan)) if count else []),
        compiler_params=pltpu.CompilerParams(
            vmem_limit_bytes=56 << 20, dimension_semantics=("arbitrary",), **comm
        ),
        name="attention",
    )(*shards, start, inproj, inproj, inproj, bias, qf, kf)


def bwd_kernel(plan, count, counts, tok, lanes, *refs):
    grads, refs = refs[:count], refs[count:]
    edges, values, refs = refs[0], refs[1], refs[2:]
    q_ref, k_ref, v_ref, d_ref, qf_ref, own_ref, kf_ref, vf_ref, refs = *refs[:8], refs[8:]
    outs, refs = refs[:count], refs[count:]
    result, gq_ref, gkv_ref, refs = *refs[:3], refs[3:]
    one, two, feats, halo, refs = *refs[:4], refs[4:]
    step = pl.program_id(0)
    ext = k_ref.shape[1]
    half = (ext - tok) // 2
    window = 2 * half + TQ
    pairs = BWD_STEPS // 2
    pair = lax.rem(step, pairs)
    if count:
        send_sem, recv_sem, local_sem, sums, refs = *refs[:4], refs[4:]
        pos = Place()

        @pl.when(step == 0)
        def _():
            meet(pos, True)

        sends = Sends(send_sem, recv_sem, pos.to)

        def work():
            neighbour = halo_plan(pos, edges, halo, sends, local_sem, len(plan))
            total = total_plan(values, result, sums, sends)
            next(neighbour)
            for i, _ in enumerate(scatter_job(pos, plan, counts, grads, outs, refs, sends, local_sem)):
                if i < 6:
                    next(total)
                if i == HALO_TURN:
                    next(neighbour)
                yield

        schedule(step, BWD_STEPS, work(), len(plan) + 4)
    else:

        @pl.when(step == 0)
        def _():
            halo[...] = edges[...]
            result[...] = values[...]

    lane = lax.broadcasted_iota(jnp.int32, (TQ, PAIR), 1)
    left = lane < HD

    @pl.when(step == 0)
    def _():
        one[2, :, PAIR:] = kf_ref[...]
        two[2, :, PAIR:] = vf_ref[...]
        feats[half : half + tok, :] = own_ref[...]

    @pl.when(step == pairs)
    def _():
        for t in range(half // TQ):
            for side, base in ((0, 0), (1, half + tok)):
                rows = slice(base + t * TQ, base + (t + 1) * TQ)
                got = halo[side, t * TQ : (t + 1) * TQ, PAIR * pairs :]
                feats[rows, :] = jnp.where(lane < lanes, qf_ref[rows, :], got)

    def sides(tile, rows, d):
        q = q_ref[0, rows, :] * jnp.bfloat16(HD**-0.5)
        feat = feats[rows, :]
        zero = jnp.zeros_like(q)
        for side in range(2):
            mine = left if side == 0 else ~left
            kept = jnp.where((lane < lanes) | (lax.rem(lane - lanes + 128, 16) == 2 * pair + side), feat, zero)
            one[side, rows, :PAIR] = jnp.where(mine, q, zero)
            one[side, rows, PAIR:] = kept
            two[side, rows, :PAIR] = jnp.where(mine, d, zero)
            two[side, rows, PAIR:] = kept

    one[2, :, :PAIR] = k_ref[0]
    two[2, :, :PAIR] = v_ref[0]
    for t in range(tok // TQ):
        sides(t, slice(half + t * TQ, half + (t + 1) * TQ), d_ref[t * TQ : (t + 1) * TQ, :])

    @pl.when(step < pairs)
    def _():
        for t in range(tok // TQ):
            win = slice(t * TQ, t * TQ + window)
            rows = slice(half + t * TQ, half + (t + 1) * TQ)
            parts = []
            for side in range(2):
                p = jnp.exp(nt(one[side, rows, :], one[2, win, :]))
                g = (p * nt(two[side, rows, :], two[2, win, :])).astype(jnp.bfloat16)
                parts.append(nn(g, k_ref[0, win, :]))
            gq_ref[t * TQ : (t + 1) * TQ, :] = (jnp.where(left, *parts) * HD**-0.5).astype(jnp.bfloat16)

    @pl.when(step >= pairs)
    def _():
        at = pl.ds(pl.multiple_of(pair * PAIR, PAIR), PAIR)
        for t in range(half // TQ):
            for side, base in ((0, 0), (1, half + tok)):
                sides(t, slice(base + t * TQ, base + (t + 1) * TQ), halo[side, t * TQ : (t + 1) * TQ, at])
        for t in range(tok // TQ):
            win = slice(t * TQ, t * TQ + window)
            rows = slice(half + t * TQ, half + (t + 1) * TQ)
            dk, dv = 0.0, 0.0
            for side in range(2):
                p = jnp.exp(nt(one[2, rows, :], one[side, win, :]))
                g = (p * nt(two[2, rows, :], two[side, win, :])).astype(jnp.bfloat16)
                dk = dk + nn(g, one[side, win, :PAIR])
                dv = dv + nn(p.astype(jnp.bfloat16), two[side, win, :PAIR])
            gkv_ref[0, t * TQ : (t + 1) * TQ, :] = dk.astype(jnp.bfloat16)
            gkv_ref[1, t * TQ : (t + 1) * TQ, :] = dv.astype(jnp.bfloat16)


BWD_STEPS = 16
HALO_TURN = 3


def attn_bwd(proj, grad, qf, own_feat, kf, vf, lanes, tok, edges, values, grads=(), parts=(), share=0.0, collective=None):
    _, ext, width = proj.shape
    pairs = width // PAIR
    half = (ext - tok) // 2
    grads, plan, counts, bufs, shapes = scatter_layout(grads, parts, share)
    count = len(grads)
    anywhere, vmem = pl.BlockSpec(memory_space=pl.ANY), pl.BlockSpec(memory_space=pltpu.VMEM)
    third = lambda k: pl.BlockSpec((1, ext, PAIR), lambda i: (k, 0, lax.rem(i, pairs)))
    fix = lambda rows: pl.BlockSpec((rows, PAIR), lambda i: (0, 0))
    comm = dict(collective_id=collective, has_side_effects=True) if count else {}
    scratch = [
        pltpu.VMEM((3, ext, 2 * PAIR), jnp.bfloat16),
        pltpu.VMEM((3, ext, 2 * PAIR), jnp.bfloat16),
        pltpu.VMEM((ext, PAIR), jnp.bfloat16),
        pltpu.VMEM((2, half, width + PAIR), jnp.bfloat16),
    ]
    if count:
        scratch += semaphores(len(plan) * SENDS + 7, len(plan) + 1) + [pltpu.VMEM((10, 8, 128), jnp.float32)] + bufs
    return pl.pallas_call(
        functools.partial(bwd_kernel, plan, count, counts, tok, lanes),
        grid=(2 * pairs,),
        in_specs=[anywhere] * count
        + [anywhere if count else vmem, vmem, third(0), third(1), third(2),
           pl.BlockSpec((tok, PAIR), lambda i: (0, lax.rem(i, pairs))), fix(ext), fix(tok), fix(ext), fix(ext)],
        out_specs=[vmem] * count
        + [vmem, pl.BlockSpec((tok, PAIR), lambda i: (0, lax.min(i, pairs - 1))),
           pl.BlockSpec((2, tok, PAIR), lambda i: (0, 0, lax.max(i - pairs, 0)))],
        out_shape=shapes
        + [jax.ShapeDtypeStruct(values.shape, jnp.float32), jax.ShapeDtypeStruct((tok, width), jnp.bfloat16),
           jax.ShapeDtypeStruct((2, tok, width), jnp.bfloat16)],
        scratch_shapes=scratch,
        compiler_params=pltpu.CompilerParams(
            vmem_limit_bytes=62 << 20, dimension_semantics=("arbitrary",), **comm
        ),
        name="attention_gradients",
    )(*grads, edges, values, proj, proj, proj, grad, qf, own_feat, kf, vf)


def bits(values, count):
    planes = (values[:, None] >> jnp.arange(count, dtype=jnp.int32)[None, :]) & 1
    return planes.astype(jnp.float32)


def features(item, places, keep, n_items):
    ext = item.shape[0]
    nb = (n_items + 1).bit_length()
    pb = (ext - 1).bit_length()
    lanes = 2 * (nb + pb)
    assert lanes + 80 <= PAIR and ext == 1 << pb
    ib = bits(item + 1, nb)
    ps = bits(places, pb)
    kept = keep.astype(jnp.float32)[:, None]
    lost = 1 - kept
    qf = jnp.concatenate([ib, 1 - ib, ps, 1 - ps, jnp.zeros((ext, PAIR - lanes))], axis=1)
    kf = jnp.concatenate([NEG * kept * (1 - ib), NEG * kept * ib, NEG * lost * (1 - ps), NEG * lost * ps,
                          -jnp.ones((ext, 48)), jnp.zeros((ext, PAIR - 48 - lanes))], axis=1)
    return qf.astype(jnp.bfloat16), kf.astype(jnp.bfloat16), lanes


def delta_key(ext, lanes):
    lane = jnp.arange(PAIR)
    vf = jnp.where((lane >= lanes + 48) & (lane < lanes + 80), -1.0, 0.0)
    return jnp.broadcast_to(vf[None], (ext, PAIR)).astype(jnp.bfloat16)


def delta_lanes(delta, lanes):
    first = delta.astype(jnp.bfloat16)
    second = (delta - first.astype(jnp.float32)).astype(jnp.bfloat16)
    return jnp.pad(jnp.concatenate([first, second], axis=1), ((0, 0), (lanes + 48, PAIR - 80 - lanes)))


MESH = pl.DeviceIdType.MESH


class Place:
    def __init__(self):
        seq, blk = lax.axis_index("seq"), lax.axis_index("blk")
        self.seq, self.blk, self.last = seq, blk, lax.axis_size("blk") - 1
        self.x, self.c, self.z, self.y = x, c, z, y = seq // 2, lax.rem(seq, 2), blk // 2, lax.rem(blk, 2)
        self.nx, self.nc, self.ny = nx, nc, ny = 1 - x, 1 - c, 1 - y
        low_bit, high_bit = lax.rem(z, 2), z // 2
        flips = {1: (1 - low_bit, high_bit), 2: (low_bit, 1 - high_bit), 3: (1 - low_bit, 1 - high_bit)}
        self.nz = {k: high * 2 + bit for k, (bit, high) in flips.items()}
        device = lambda x, c, z, y: (x * 2 + c, z * 2 + y)
        self.to = {"x": device(nx, c, z, y), "y": device(x, c, z, ny), "c": device(x, nc, z, y)}
        for k in (1, 2, 3):
            self.to[k] = device(x, c, self.nz[k], y)
        self.below = (seq, lax.max(blk - 1, 0))
        self.above = (seq, lax.min(blk + 1, self.last))


class Copy:
    def __init__(self, make):
        self.make = make

    def start(self):
        self.make().start()
        return self

    def wait(self):
        self.make().wait()

    def wait_send(self):
        self.make().wait_send()

    def wait_recv(self):
        self.make().wait_recv()


def local_copy(src, dst, sems, at):
    return Copy(lambda: pltpu.make_async_copy(src(), dst(), sems.at[at])).start()


class Sends:
    def __init__(self, send_sem, recv_sem, to):
        self.send_sem, self.recv_sem, self.to, self.used, self.live = send_sem, recv_sem, to, 0, []

    def describe(self, src, dst, device):
        at = self.used
        self.used += 1
        return Copy(
            lambda: pltpu.make_async_remote_copy(
                src_ref=src(), dst_ref=dst(), send_sem=self.send_sem.at[at], recv_sem=self.recv_sem.at[at],
                device_id=device, device_id_type=MESH,
            )
        )

    def start(self, src, dst, partner):
        copy = self.describe(src, dst, self.to[partner]).start()
        self.live.append(copy)
        return copy

    def finish(self):
        for copy in self.live:
            copy.wait_send()


def gather_plan(pos, shard, full, sends, local, number, base, wide, at):
    x, c, z, y, nx, nc, ny = pos.x, pos.c, pos.z, pos.y, pos.nx, pos.nc, pos.ny
    every, one, two = pl.ds(base, wide), pl.ds(base, at), pl.ds(base + at, wide - at)

    def send(partner, *index):
        return sends.start(lambda: full.at[index], lambda: full.at[index], partner)

    rows = slice(None)
    source, target = lambda: shard.at[:, every], lambda: full.at[x, c, z, y, :, every]
    own = local_copy(source, target, local, number)
    line = [sends.start(source, target, k) for k in (1, 2, 3)]
    yield
    own.wait()
    for copy in line:
        copy.wait_recv()
    if at:
        a = send("x", x, c, rows, y, rows, one)
    b = send("y", x, c, rows, y, rows, two)
    core = [send("c", x, c, rows, y, rows, every)]
    yield
    if at:
        a.wait_recv()
        a2 = send("y", rows, c, rows, y, rows, one)
        core.append(send("c", nx, c, rows, y, rows, one))
    b.wait_recv()
    b2 = send("x", x, c, rows, rows, rows, two)
    core.append(send("c", x, c, rows, ny, rows, two))
    yield
    if at:
        a2.wait_recv()
        core.append(send("c", rows, c, rows, ny, rows, one))
    b2.wait_recv()
    core.append(send("c", nx, c, rows, rows, rows, two))
    yield
    for copy in core:
        copy.wait_recv()
    yield


SENDS = 12


def turns(plans, last):
    for turn in range(len(plans) + 4):
        for k in reversed(range(len(plans))):
            if 0 <= turn - k <= 4:
                next(plans[k])
        if turn == len(plans) + 3:
            last()
        yield


def pieces(widths, parts, share):
    plan = []
    for k, (whole, count) in enumerate(zip(widths, parts)):
        wide = whole // count
        plan += [(k, p * wide, wide, int(wide * share) // 128 * 128) for p in range(count)]
    return plan


def halo_plan(pos, edges, halo, sends, local, number):
    blk, last = pos.blk, pos.last
    down = sends.describe(lambda: edges.at[0], lambda: halo.at[1], pos.below)
    up = sends.describe(lambda: edges.at[1], lambda: halo.at[0], pos.above)
    fill = [
        Copy(lambda k=k: pltpu.make_async_copy(edges.at[k], halo.at[k], local.at[number])) for k in (0, 1)
    ]

    def where(test, *acts):
        @pl.when(test)
        def _():
            for act in acts:
                act()

    where(blk > 0, down.start)
    where(blk < last, up.start)
    where(blk == 0, fill[0].start)
    where(blk == last, fill[1].start)
    yield
    where(blk > 0, down.wait_send, up.wait_recv)
    where(blk < last, up.wait_send, down.wait_recv)
    where(blk == 0, fill[0].wait)
    where(blk == last, fill[1].wait)
    yield


def meet(pos, halo):
    barrier = pltpu.get_barrier_semaphore()
    for device in pos.to.values():
        pl.semaphore_signal(barrier, inc=1, device_id=device, device_id_type=MESH)
    count = len(pos.to)
    if halo:

        @pl.when(pos.blk > 0)
        def _():
            pl.semaphore_signal(barrier, inc=1, device_id=pos.below, device_id_type=MESH)

        @pl.when(pos.blk < pos.last)
        def _():
            pl.semaphore_signal(barrier, inc=1, device_id=pos.above, device_id_type=MESH)

        count = count + 2 - jnp.where(pos.blk == 0, 1, 0) - jnp.where(pos.blk == pos.last, 1, 0)
    pl.semaphore_wait(barrier, count)


def gather_job(pos, plan, shards, fulls, sends, local):
    yield from turns([
        gather_plan(pos, shards[k], fulls[k], sends, local, i, base, wide, at) for i, (k, base, wide, at) in enumerate(plan)
    ], sends.finish)


def gather_kernel(plan, count, *refs):
    shards, edges, fulls, halo = refs[:count], refs[count], refs[count + 1 : 2 * count + 1], refs[2 * count + 1]
    send_sem, recv_sem, local_sem = refs[2 * count + 2 :]
    pos = Place()
    meet(pos, True)
    sends = Sends(send_sem, recv_sem, pos.to)
    neighbour = halo_plan(pos, edges, halo, sends, local_sem, len(plan))
    next(neighbour)
    for _ in gather_job(pos, plan, shards, fulls, sends, local_sem):
        pass
    next(neighbour)


def semaphores(number, local):
    return [pltpu.SemaphoreType.DMA((number,)), pltpu.SemaphoreType.DMA((number,)), pltpu.SemaphoreType.DMA((local,))]


def full_shapes(shards):
    return [jax.ShapeDtypeStruct((2, 2, 4, 2) + v.shape, jnp.bfloat16) for v in shards]


def gather_all(shards, parts, share, edges, collective):
    count = len(shards)
    plan = pieces([v.shape[1] for v in shards], parts, share)
    anywhere = pl.BlockSpec(memory_space=pl.ANY)
    return pl.pallas_call(
        functools.partial(gather_kernel, plan, count),
        in_specs=[anywhere] * (count + 1),
        out_specs=[anywhere] * (count + 1),
        out_shape=full_shapes(shards) + [jax.ShapeDtypeStruct(edges.shape, edges.dtype)],
        scratch_shapes=semaphores(len(plan) * SENDS + 2, len(plan) + 1),
        compiler_params=pltpu.CompilerParams(collective_id=collective, has_side_effects=True),
        name="gather_weights",
    )(*shards, edges)


def widen(value):
    return value.astype(jnp.float32)


def scatter_plan(pos, grad, out, bufs, sends, local, number, base, wide, at):
    x, c, z, y, nx, nc, ny = pos.x, pos.c, pos.z, pos.y, pos.nx, pos.nc, pos.ny
    own, got, one1, two1, one2, two2, line, ends = bufs if at else bufs[:2] + (None,) + bufs[2:3] + (None,) + bufs[3:]
    every, one, two = pl.ds(base, wide), pl.ds(0, at), pl.ds(at, wide - at)
    low = jnp.bfloat16
    load = local_copy(lambda: grad.at[:, c, :, :, :, every], lambda: own, local, number)
    cross = sends.start(lambda: grad.at[:, nc, :, :, :, every], lambda: got, "c")
    yield
    load.wait()
    cross.wait_recv()

    @pl.loop(0, 8)
    def _(i):
        own[i // 4, lax.rem(i, 4)] = (widen(own[i // 4, lax.rem(i, 4)]) + widen(got[i // 4, lax.rem(i, 4)])).astype(low)

    if at:
        a = sends.start(lambda: own.at[:, :, ny, :, one], lambda: one1, "y")
    b = sends.start(lambda: own.at[nx, :, :, :, two], lambda: two1, "x")
    yield
    if at:
        a.wait_recv()

        @pl.loop(0, 8)
        def _(i):
            one1[i // 4, lax.rem(i, 4)] = (
                widen(own[i // 4, lax.rem(i, 4), y, :, :at]) + widen(one1[i // 4, lax.rem(i, 4)])
            ).astype(low)

        a2 = sends.start(lambda: one1.at[nx], lambda: one2, "x")
    b.wait_recv()

    @pl.loop(0, 4)
    def _(i):
        two1[i] = (widen(own[x, i, :, :, at:]) + widen(two1[i])).astype(low)

    b2 = sends.start(lambda: two1.at[:, ny], lambda: two2, "y")
    yield
    if at:
        a2.wait_recv()
    b2.wait_recv()

    @pl.loop(0, 4)
    def _(i):
        if at:
            line[i, :, :at] = (widen(one1[x, i]) + widen(one2[i])).astype(low)
        line[i, :, at:] = (widen(two1[i, y]) + widen(two2[i])).astype(low)

    last = [
        sends.start(lambda k=k: line.at[pos.nz[k]], lambda k=k: ends.at[k - 1], k) for k in (1, 2, 3)
    ]
    yield
    for copy in last:
        copy.wait_recv()
    out[:, base : base + wide] = widen(line[z]) + widen(ends[0]) + widen(ends[1]) + widen(ends[2])
    yield


def scatter_bufs(rows, wide, at):
    shapes = [(2, 4, 2, rows, wide), (2, 4, 2, rows, wide)]
    if at:
        shapes += [(2, 4, rows, at), (4, 2, rows, wide - at), (4, rows, at)]
    else:
        shapes += [(4, 2, rows, wide)]
    shapes += [(4, rows, wide - at), (4, rows, wide), (3, rows, wide)]
    return [pltpu.VMEM(s, jnp.bfloat16) for s in shapes]


def total_plan(values, result, bufs, sends):
    partners = ("c", "x", "y", 1, 2)
    for i, partner in enumerate(partners):
        source = (lambda i=i: bufs.at[2 * i - 1]) if i else (lambda: values)
        copy = sends.start(source, lambda i=i: bufs.at[2 * i], partner)
        yield
        copy.wait_recv()
        total = source()[...] + bufs[2 * i]
        if i + 1 < len(partners):
            bufs[2 * i + 1] = total
        else:
            result[...] = total
    yield


def scatter_job(pos, plan, counts, grads, outs, bufs, sends, local):
    plans = []
    for i, (k, base, wide, at) in enumerate(plan):
        first = sum(counts[:i])
        mine = bufs[first : first + counts[i]]
        plans.append(scatter_plan(pos, grads[k], outs[k], mine, sends, local, i, base, wide, at))
    yield from turns(plans, sends.finish)


def scatter_layout(grads, parts, share):
    grads = [v.reshape(2, 2, 4, 2, v.shape[0] // 32, v.shape[1]) for v in grads]
    plan = pieces([v.shape[-1] for v in grads], parts, share)
    bufs = [scatter_bufs(grads[k].shape[-2], wide, at) for k, base, wide, at in plan]
    shapes = [jax.ShapeDtypeStruct(v.shape[-2:], jnp.float32) for v in grads]
    return grads, plan, [len(b) for b in bufs], sum(bufs, []), shapes


def scatter_kernel(plan, count, counts, *refs):
    grads, outs, refs = refs[:count], refs[count : 2 * count], refs[2 * count :]
    send_sem, recv_sem, local_sem = refs[:3]
    pos = Place()
    meet(pos, False)
    sends = Sends(send_sem, recv_sem, pos.to)
    for _ in scatter_job(pos, plan, counts, grads, outs, refs[3:], sends, local_sem):
        pass


def scatter_all(grads, parts, share, collective):
    count = len(grads)
    grads, plan, counts, bufs, shapes = scatter_layout(grads, parts, share)
    anywhere, vmem = pl.BlockSpec(memory_space=pl.ANY), pl.BlockSpec(memory_space=pltpu.VMEM)
    return pl.pallas_call(
        functools.partial(scatter_kernel, plan, count, counts),
        in_specs=[anywhere] * count,
        out_specs=[vmem] * count,
        out_shape=shapes,
        scratch_shapes=semaphores(len(plan) * SENDS, len(plan)) + bufs,
        compiler_params=pltpu.CompilerParams(
            collective_id=collective, has_side_effects=True, vmem_limit_bytes=58 << 20
        ),
        name="sum_gradients",
    )(*grads)


H = 16
MAXLEN = 512
TSTEPS = 5000
AXES = ("seq", "blk")
SMALL = 10


def as_float(value):
    return value.astype(jnp.float32)


def low(value):
    return value.astype(jnp.bfloat16)


def row_dot(left, right):
    return lax.dot_general(left, right, (((0,), (0,)), ((), ())), preferred_element_type=jnp.float32)


def neighbours(low_part, high_part):
    count = lax.axis_size("blk")
    up = [(i, i + 1) for i in range(count - 1)]
    down = [(i + 1, i) for i in range(count - 1)]
    return lax.ppermute(high_part, "blk", up), lax.ppermute(low_part, "blk", down)


def norm_forward(values):
    mean_val = jnp.mean(values, axis=-1, keepdims=True)
    centered = values - mean_val
    inv = lax.rsqrt(jnp.mean(centered * centered, axis=-1, keepdims=True) + 1e-05)
    return centered * inv, inv


def norm_backward(grad, normal, inv, gain):
    scaled = grad * gain
    grad_in = inv * (
        scaled
        - jnp.mean(scaled, axis=-1, keepdims=True)
        - normal * jnp.mean(scaled * normal, axis=-1, keepdims=True)
    )
    return grad_in, jnp.sum(grad * normal, axis=0), jnp.sum(grad, axis=0)


def item_of(ends, places):
    return jnp.sum((ends[None, :] <= places[:, None]).astype(jnp.int32), axis=1)


def per_device(fast, inputs, cotangent, timestep, lengths, padding, *shards):
    (time_weight, time_bias, inproj, query_bias, value_bias, outproj, outproj_bias, first_gain, first_shift,
     upward_w, upward_bias, downward_w, downward_bias, second_gain, second_shift) = shards
    small = (time_weight, time_bias, query_bias, value_bias, outproj_bias, first_gain, first_shift,
             downward_bias, second_gain, second_shift)
    tok, width = inputs.shape
    half = MAXLEN
    ext = tok + 2 * half
    hidden = upward_w.shape[1]

    mark = jnp.zeros((16, width), jnp.bfloat16)
    keep_own = low(padding)
    edge_low = jnp.concatenate([inputs[:half], mark.at[0, :half].set(keep_own[:half])])
    edge_high = jnp.concatenate([inputs[tok - half :], mark.at[0, :half].set(keep_own[tok - half :])])

    if fast:
        rows = time_weight.shape[0]
        cols = [v[:, None] for v in small] + [upward_bias.reshape(-1, rows).T]
        cols = jnp.concatenate(cols, axis=1)
        cols = jnp.pad(cols, ((0, 0), (0, 128 - cols.shape[1])))
        *fulls, halo = gather_all(
            (inproj, cols), (1, 1), 0.0, jnp.stack([edge_low, edge_high]), 0
        )
        inproj_f, small_f = [v.reshape(-1, v.shape[-1]) for v in fulls]
        small_f = as_float(small_f.T)
        from_low, from_high = halo[0], halo[1]
        upward_bias_f = small_f[SMALL : SMALL + hidden // width]
        upward_bias_f = upward_bias_f.reshape(-1, width // rows, rows).transpose(1, 0, 2).reshape(hidden)
    else:
        from_low, from_high = neighbours(edge_low, edge_high)
        whole = lambda v: lax.all_gather(v, AXES, axis=0, tiled=True)
        inproj_f, outproj_f, upward_f, downward_f = map(whole, (inproj, outproj, upward_w, downward_w))
        small_f = [as_float(whole(v)) for v in small]
        upward_bias_f = as_float(whole(upward_bias))
    (time_weight_f, time_bias_f, query_bias_f, value_bias_f, outproj_bias_f, first_gain_f, first_shift_f,
     downward_bias_f, second_gain_f, second_shift_f) = [small_f[i] for i in range(SMALL)]

    offset = lax.axis_index("blk") * tok
    ends = jnp.cumsum(lengths[0]).astype(jnp.int32)
    places = offset - half + jnp.arange(ext, dtype=jnp.int32)
    item = jnp.where(places >= 0, item_of(ends, places), -1)
    keep = jnp.concatenate([from_low[half, :half], keep_own, from_high[half, :half]])
    query_feat, key_feat, lane = features(item, places, as_float(keep) > 0.5, lengths.shape[1])

    time_value = as_float(timestep[0]) / TSTEPS
    shift = time_value * time_weight_f + time_bias_f
    start_of = lambda v: as_float(v) + time_value * time_weight_f + time_bias_f
    start_vec = start_of(inputs)
    start_low = low(start_vec)
    start_ext = jnp.concatenate([low(start_of(from_low[:half])), start_low, low(start_of(from_high[:half]))])
    bias = jnp.pad(jnp.stack([query_bias_f, jnp.zeros_like(query_bias_f), value_bias_f]), ((0, 5), (0, 0)))
    if fast:
        *fulls, projected, attended, feat_own = attn_fwd(
            start_ext, inproj_f, bias, query_feat, key_feat, lane, tok, (outproj, upward_w, downward_w), (1, 2, 2), 0.5, 1
        )
        outproj_f, upward_f, downward_f = [v.reshape(-1, v.shape[-1]) for v in fulls]
    else:
        projected, attended, feat_own = attn_fwd(start_ext, inproj_f, bias, query_feat, key_feat, lane, tok)
    attn_branch = jnp.dot(attended, outproj_f, preferred_element_type=jnp.float32) + outproj_bias_f
    first_normal, first_inv = norm_forward(start_vec + attn_branch)
    first_out = first_normal * first_gain_f + first_shift_f
    first_low = low(first_out)
    upward = jnp.dot(first_low, upward_f, preferred_element_type=jnp.float32) + upward_bias_f
    phi = 0.5 * (1.0 + lax.erf(upward * 2.0**-0.5))
    hidden_low = low(upward * phi)
    slope = phi + upward * (jnp.exp(-0.5 * upward * upward) * 0.3989422804014327)
    ffn_branch = jnp.dot(hidden_low, downward_f, preferred_element_type=jnp.float32) + downward_bias_f
    second_normal, second_inv = norm_forward(first_out + ffn_branch)
    layer_out = low(second_normal * second_gain_f + second_shift_f)
    sums = jnp.stack([jnp.sum(v * v) for v in (start_vec, attn_branch, ffn_branch)])

    grad_second_in, grad_second_gain, grad_second_shift = norm_backward(
        as_float(cotangent), second_normal, second_inv, second_gain_f
    )
    grad_ffn_low = low(grad_second_in)
    grad_down_weight = row_dot(hidden_low, grad_ffn_low)
    grad_down_bias = jnp.sum(as_float(grad_ffn_low), axis=0)
    grad_up_low = low(nt(grad_ffn_low, downward_f) * slope)
    grad_up_weight = row_dot(first_low, grad_up_low)
    grad_up_bias = jnp.sum(as_float(grad_up_low), axis=0)
    grad_first = grad_second_in + nt(grad_up_low, upward_f)
    grad_first_in, grad_first_gain, grad_first_shift = norm_backward(grad_first, first_normal, first_inv, first_gain_f)
    grad_branch_low = low(grad_first_in)
    grad_out_weight = row_dot(attended, grad_branch_low)
    grad_out_bias = jnp.sum(as_float(grad_branch_low), axis=0)
    grad_attended = low(nt(grad_branch_low, outproj_f))

    head = jnp.arange(width)[:, None] // HD == jnp.arange(H)[None, :]
    delta = jnp.dot(
        as_float(grad_attended) * as_float(attended), as_float(head), precision=lax.Precision.HIGHEST
    )
    feat_own = jnp.where(jnp.arange(PAIR) < lane + 48, feat_own, delta_lanes(delta, lane))
    packed = jnp.concatenate([grad_attended, feat_own], axis=1)
    values = jnp.pad(sums[None], ((0, 7), (0, 125)))
    backward = functools.partial(
        attn_bwd, projected, grad_attended, query_feat, feat_own, key_feat, delta_key(ext, lane), lane, tok
    )
    if fast:
        grads = [low(v) for v in (grad_out_weight, grad_up_weight, grad_down_weight)]
        edges = jnp.stack([packed[:half], packed[tok - half :]])
        out_share, up_share, down_share, sums, grad_q, grad_kv = backward(edges, values, grads, (1, 2, 2), 0.0, 2)
    else:
        edges = jnp.stack(neighbours(packed[:half], packed[tok - half :]))
        sums, grad_q, grad_kv = backward(edges, lax.psum(values, AXES))
    sums = sums[0, :3]
    branch_rms = jnp.sqrt(sums / (tok * width * lax.axis_size(AXES)))
    grad_proj_low = jnp.concatenate([grad_q, grad_kv[0], grad_kv[1]], axis=1)
    grad_in_weight = row_dot(start_low, grad_proj_low)
    grad_query_bias = jnp.sum(as_float(grad_q), axis=0)
    grad_value_bias = jnp.sum(as_float(grad_kv[1]), axis=0)
    grad_start = grad_first_in + nt(grad_proj_low, inproj_f)
    grad_time_bias = jnp.sum(grad_start, axis=0)
    grad_time_weight = time_value * grad_time_bias
    input_grad = low(grad_start)

    small_grads = (grad_time_weight, grad_time_bias, grad_query_bias, grad_value_bias, grad_out_bias, grad_first_gain,
                   grad_first_shift, grad_down_bias, grad_second_gain, grad_second_shift)
    if fast:
        cols = grad_up_bias.reshape(width // rows, -1, rows).transpose(1, 0, 2).reshape(-1, width)
        cols = jnp.concatenate([jnp.stack(small_grads), cols]).T
        cols = jnp.pad(cols, ((0, 0), (0, 128 - cols.shape[1])))
        in_share, last = scatter_all((low(grad_in_weight), low(cols)), (3, 1), 0.5, 3)
        small_shares = [last[:, i] for i in range(SMALL)]
        up_bias_share = last[:, SMALL : SMALL + hidden // width].T.reshape(-1)
    else:
        share = lambda v: lax.psum_scatter(v, AXES, scatter_dimension=0, tiled=True)
        down_share, up_share, out_share, in_share, up_bias_share = map(
            share, (grad_down_weight, grad_up_weight, grad_out_weight, grad_in_weight, grad_up_bias)
        )
        small_shares = [share(v) for v in small_grads]
    (time_weight_s, time_bias_s, query_bias_s, value_bias_s, out_bias_s, first_gain_s, first_shift_s,
     down_bias_s, second_gain_s, second_shift_s) = small_shares
    return (layer_out, input_grad, time_weight_s, time_bias_s, in_share, query_bias_s, value_bias_s, out_share,
            out_bias_s, first_gain_s, first_shift_s, up_share, up_bias_share, down_share, down_bias_s,
            second_gain_s, second_shift_s, branch_rms)


def solution(mesh):
    both = P(AXES)
    matrix = P(AXES, None)
    in_specs = (matrix, matrix, P("seq"), P("seq", None), both,
                both, both, matrix, both, both, matrix, both, both, both, matrix, both, matrix, both, both, both)
    out_specs = (matrix, matrix, both, both, matrix, both, both, matrix, both, both, both, matrix, both, matrix,
                 both, both, both, P())
    fast = dict(mesh.shape) == {"seq": 4, "blk": 8}
    return jax.shard_map(
        functools.partial(per_device, fast), mesh=mesh, in_specs=in_specs, out_specs=out_specs, check_vma=False
    )
```

time: 864 us -> 643 us (0.74)
  Pallas kernels: 595 us -> 438 us
  matrix products: 155 us -> 130 us
  other arithmetic: 49.6 us -> 31.2 us
  local copies, waits for them, and re-layouts: 56 us -> 38.1 us
    pallas_call x4 -> x3, Pallas kernels: 435 us -> 350 us  [the longest x1 166 us: attn_bwd(): pl.pallas_call(functools.partial(bwd_kernel, plan, count, counts, tok, la...]
    pallas_call x1, Pallas kernels: 160 us -> 87.3 us  [gather_all(): pl.pallas_call(functools.partial(gather_kernel, plan, count), in_specs=[a...]
    dot_general x1 -> x0, matrix products: 19.3 us -> none  [per_device(): jnp.dot(start_ext, inproj_f, preferred_element_type=jnp.float32) + proj_bias]
    unnamed x107 -> x59, local copies, waits for them, and re-layouts: 23.5 us -> 11.7 us
where the time goes in v3:
time: 643 us; the launch traced here: 639 us
  Pallas kernels  438 us (68%)
  matrix products  130 us (20%)
  local copies, waits for them, and re-layouts  38.1 us (6%)
  other arithmetic  31.2 us (5%)
    pallas_call x1, Pallas kernels, attn_bwd(): pl.pallas_call(functools.partial(bwd_kernel, plan, count, counts, tok, la...  166 us
    pallas_call x1, Pallas kernels, attn_fwd(): pl.pallas_call(functools.partial(fwd_kernel, plan, count, tok, lanes), gr...  136 us
    pallas_call x1, Pallas kernels, gather_all(): pl.pallas_call(functools.partial(gather_kernel, plan, count), in_specs=[a...  87.3 us
    dot_general x4, matrix products, nt(): lax.dot_general(a, b, (((1,), (1,)), ((), ())), preferred_element_type=jn...  48.3 us
    pallas_call x1, Pallas kernels, scatter_all(): pl.pallas_call(functools.partial(scatter_kernel, plan, count, counts), in...  47.8 us
    dot_general x4, matrix products, row_dot(): lax.dot_general(left, right, (((0,), (0,)), ((), ())), preferred_element_...  42.8 us
    dot_general x1, matrix products, per_device(): jnp.dot(first_low, upward_f, preferred_element_type=jnp.float32)  18 us
    dot_general x1, matrix products, per_device(): jnp.dot(hidden_low, downward_f, preferred_element_type=jnp.float32)  13 us

profile of v3, /device:TPU:0, one launch (start us, length us, event | category | flops | bytes accessed | tf_op | source)
XLA Modules:
  0.0 639.2 jit_solution(1570543601265397756)
XLA Ops:
  0.7 0.8 copy.147
  1.4 0.8 copy.148
  2.2 0.8 copy.149
  2.9 0.8 copy.150
  3.7 0.8 copy.151
  4.4 0.8 copy.152
  5.2 0.8 copy.153
  5.9 0.8 copy.154
  6.7 0.8 copy.155
  7.4 0.8 copy.156
  8.2 0.7 reshape.327
  9.1 0.6 pad.30.refs_1_
  9.7 0.7 convert_element_type.155
  10.4 1.7 fusion.56
  12.3 1.5 pad_maximum_fusion.5.refs_2_
  13.9 87.3 %gather_weights.1 = (bf16[2,2,4,2,32,3072]{5,4,3,2,1,0:T(8,128)(2,1)}, bf16[2,2,4,2,32,128]{5,4,3,2,1,0:T(8,128)(2,1)}, bf16[2,528,1024]{2,1,0:T(8,128)(2,1)}) custom-call(bf16[32,3072]{1,0:T(8,128)(2,1)} %refs_0_.2, bf16[32,128]{1,0:T(8,128)(2,1)} %pad.30.refs_1_, bf16[2,528,1024]{2,1,0:T(8,128)(2,1)} %pad_maximum_fusion.5.refs_2_), custom_call_target="tpu_custom_call" | custom-call | tf_op jit(solution)/shard_map/gather_weights/pallas_call | solution.py:523
  101.2 1.0 bitcast_convert_fusion
  103.1 2.2 fusion.26
  105.9 2.6 pad_maximum_fusion.1.refs_3_
  108.9 0.6 pad.31.refs_7_
  109.9 1.1 convert_convert_fusion.1
  111.3 0.7 multiply_convert_fusion.3
  112.0 1.1 convert_convert_fusion
  113.1 0.7 multiply_convert_fusion.1
  113.8 0.9 broadcast_in_dim.93
  114.7 3.9 concatenate.55.refs_8_.refs_9_
  118.7 2.3 concatenate.59.refs_9_.refs_11_
  121.1 136.2 %attention.1 = (bf16[2,2,4,2,32,1024]{5,4,3,2,1,0:T(8,128)(2,1)}, bf16[2,2,4,2,32,4096]{5,4,3,2,1,0:T(8,128)(2,1)}, bf16[2,2,4,2,128,1024]{5,4,3,2,1,0:T(8,128)(...) custom-call(bf16[32,1024]{1,0:T(8,128)(2,1)} %refs_0_.3, ...), custom_call_target="tpu_custom_call" | custom-call | tf_op jit(solution)/shard_map/attention/pallas_call | solution.py:115
  257.3 5.9 fusion.53
  263.2 1.9 copy-done.1
  265.8 0.8 slice.194
  266.8 18.0 %multiply_convert_fusion = (bf16[1024,4096]{1,0:T(8,128)(2,1)S(1)}, f32[1024,4096]{1,0:T(8,128)}) fusion(f32[4096]{0:T(1024)S(1)} %add.207, bf16[1024,4096]{1,0:T(8,128)(2,1)} %bitcast.130, f32[1024,1024]{1,0:T(8,128)} %copy-done.1, f32[1024]{0:T(1024)S(1)} %bitcast.114, f32[1024]{0:T(1024)S(1)} %bitcast.108, f32[1024]{0:T(1024)S(1)} %add_rsqrt_fusion.1, ...), kind=kOutput, calls=%fused_computation.7 | convolution fusion | flops 8620343296 | bytes 37781504 | tf_op jit(solution)/shard_map/dot_general | solution.py:773
  284.7 3.3 copy-done.26
  288.0 13.0 %fusion.52 = (f32[1024]{0:T(1024)S(1)}, f32[1024,1024]{1,0:T(8,128)S(1)}, f32[]{:T(128)}) fusion(f32[1024]{0:T(1024)S(1)} %bitcast.117, f32[1024]{0:T(1024)S(1)} %bitcast.115, f32[1024]{0:T(1024)S(1)} %bitcast.109, f32[1024]{0:T(1024)S(1)} %add_rsqrt_fusion.1, f32[1024,1024]{1,0:T(8,128)S(1)} %copy-done.2, f32[1024]{0:T(1024)S(1)} %broadcast_multiply_fusion.5, ...), kind=kOutput, calls=%fused_computation.146 | convolution fusion | flops 8599370752 | bytes 25190404 | tf_op jit(solution)/shard_map/dot_general | solution.py:777
  301.6 1.0 copy-done.8
  302.6 4.3 fusion.12
  306.9 2.5 convert_reduce_fusion.2
  309.4 20.2 %fusion.60 = (bf16[4096]{0:T(1024)(128)(2,1)S(1)}, bf16[1024,4096]{1,0:T(8,128)(2,1)}) fusion(f32[1024,4096]{1,0:T(8,128)} %get-tuple-element.144, f32[4096]{0:T(1024)S(1)} %add.207, bf16[4096,1024]{1,0:T(8,128)(2,1)} %bitcast.133, f32[1024,1024]{1,0:T(8,128)S(1)} %get-tuple-element.94), kind=kOutput, calls=%fused_computation.153 | convolution fusion | flops 8641310720 | bytes 37773312 | tf_op jit(solution)/shard_map/dot_general | solution.py:17
  329.5 14.9 %multiply_reduce_fusion = (bf16[1024]{0:T(1024)(128)(2,1)S(1)}, f32[1024]{0:T(1024)S(1)}, f32[1024]{0:T(1024)S(1)}, bf16[1024]{0:T(1024)(128)(2,1)S(1)}, f32[1024,1024]{1,0:T(8,128)S(1)}) fusion(f32[1024,1024]{1,0:T(8,128)S(1)} %copy-done.2, f32[1024]{0:T(1024)S(1)} %add_rsqrt_fusion.1, f32[1024]{0:T(1024)S(1)} %broadcast_multiply_fusion.5, ...), kind=kOutput, calls=%fused_computation.23 | convolution fusion | flops 8600416256 | bytes 29384704 | tf_op jit(solution)/shard_map/dot_general | solution.py:17
  344.5 1.6 convert_reduce_fusion.1
  346.1 3.8 convolution_convert_fusion.4
  349.9 15.0 %convolution_convert_fusion.1 = bf16[1024,4096]{1,0:T(8,128)(2,1)} fusion(bf16[1024,4096]{1,0:T(8,128)(2,1)} %get-tuple-element.148, f32[1024,1024]{1,0:T(8,128)S(1)} %copy-done.2, f32[1024]{0:T(1024)S(1)} %bitcast.116, f32[1024]{0:T(1024)S(1)} %bitcast.112, f32[1024]{0:T(1024)S(1)} %add_rsqrt_fusion.1, f32[1024]{0:T(1024)S(1)} %broadcast_multiply_fusion.5), kind=kOutput, calls=%fused_computation.10 | convolution fusion | flops 8599371776 | bytes 20987904 | tf_op jit(solution)/shard_map/dot_general | solution.py:680
  364.9 14.7 %convolution_convert_fusion = bf16[4096,1024]{1,0:T(8,128)(2,1)} fusion(bf16[1024,4096]{1,0:T(8,128)(2,1)} %copy-done.26, f32[1024,1024]{1,0:T(8,128)S(1)} %copy-done.12), kind=kOutput, calls=%fused_computation.9 | convolution fusion | flops 8595177472 | bytes 20971520 | tf_op jit(solution)/shard_map/dot_general | solution.py:680
  379.6 2.4 convolution_convert_fusion.3.refs_8_
  382.0 2.4 subtract_convert_fusion
  385.0 1.6 pad_maximum_fusion.4.refs_3_
  386.7 2.0 maximum_bitcast_fusion
  388.7 0.6 pad.33.refs_4_
  389.3 0.9 broadcast_in_dim.99.refs_12_
  390.2 166.4 %attention_gradients.1 = (f32[32,1024]{1,0:T(8,128)}, f32[32,4096]{1,0:T(8,128)}, f32[128,1024]{1,0:T(8,128)}, f32[8,128]{1,0:T(8,128)}, bf16[1024,1024]{1,0:T(8,128)(2,1)}, /*index=5*/bf16[2,1024,1024]{2,1,0:T(8,128)(2,1)}) custom-call(bf16[2,2,4,2,32,1024]{5,4,3,2,1,0:T(8,128)(2,1)} %bitcast.92, bf16[2,2,4,2,32,4096]{5,4,3,2,1,0:T(8,128)(2,1)} %bitcast.89, ...), custom_call_target="tpu_custom_call" | custom-call | tf_op jit(solution)/shard_map/attention_gradients/pallas_call | solution.py:268
  556.6 3.2 slice_reduce_fusion
  560.0 0.7 copy-done.15
  560.7 10.8 %fusion.55 = (f32[1024]{0:T(1024)S(1)}, bf16[1024,1024]{1,0:T(8,128)(2,1)}) fusion(f32[1024,1024]{1,0:T(8,128)S(1)} %copy-done.10, bf16[1024,3072]{1,0:T(8,128)(2,1)} %bitcast.88, bf16[1024,1024]{1,0:T(8,128)(2,1)S(1)} %get-tuple-element.107, bf16[1024,1024]{1,0:T(8,128)(2,1)S(1)} %get-tuple-element.108, bf16[1024,1024]{1,0:T(8,128)(2,1)S(1)} %copy-done.15), kind=kOutput, calls=%fused_computation.148 | convolution fusion | flops 6464470016 | bytes 18878464 | tf_op jit(solution)/shard_map/dot_general | solution.py:17
  571.5 9.2 %convolution_convert_fusion.2 = bf16[1024,3072]{1,0:T(8,128)(2,1)} fusion(bf16[1024,1024]{1,0:T(8,128)(2,1)S(1)} %copy-done.7, bf16[1024,1024]{1,0:T(8,128)(2,1)S(1)} %get-tuple-element.107, bf16[1024,1024]{1,0:T(8,128)(2,1)S(1)} %get-tuple-element.108, bf16[1024,1024]{1,0:T(8,128)(2,1)S(1)} %copy-done.15), kind=kOutput, calls=%fused_computation.12 | convolution fusion | flops 6464471040 | bytes 14680064 | tf_op jit(solution)/shard_map/dot_general | solution.py:680
  581.8 0.8 pad.34.clone
  582.6 47.8 %sum_gradients.1 = (f32[32,3072]{1,0:T(8,128)}, f32[32,128]{1,0:T(8,128)}) custom-call(bf16[2,2,4,2,32,3072]{5,4,3,2,1,0:T(8,128)(2,1)} %bitcast.91, bf16[2,2,4,2,32,128]{5,4,3,2,1,0:T(8,128)(2,1)} %bitcast.93), custom_call_target="tpu_custom_call" | custom-call | tf_op jit(solution)/shard_map/sum_gradients/pallas_call | solution.py:651
  630.4 2.0 slice_reduce_fusion.1
  632.4 0.8 slice_bitcast_fusion.4
  633.2 0.6 reshape.344
  633.8 1.2 sqrt_bitcast_fusion
  635.0 1.8 copy.179
  636.8 0.7 copy.180
  637.5 0.8 copy.181
  638.2 0.8 copy.182
  (111 shorter events, 5.6 us)
Async XLA Ops:
  13.9 91.4 %copy-start.4 = (bf16[1024,1024]{1,0:T(8,128)(2,1)S(1)}, bf16[1024,1024]{1,0:T(8,128)(2,1)}, u32[]{:S(2)}) copy-start(bf16[1024,1024]{1,0:T(8,128)(2,1)} %param.24) | copy-start | bytes 6291460
  102.4 3.5 copy-start.16
  105.9 2.8 copy-start.6
  105.9 3.6 copy-start.24
  105.9 5.1 copy-start.3
  121.1 136.2 %copy-start.5 = (bf16[1024,1024]{1,0:T(8,128)(2,1)S(1)}, bf16[1024,1024]{1,0:T(8,128)(2,1)}, u32[]{:S(2)}) copy-start(bf16[1024,1024]{1,0:T(8,128)(2,1)} %param.24) | copy-start | bytes 6291460
  263.2 2.0 copy-start.1
  266.8 21.3 %copy-start.2 = (f32[1024,1024]{1,0:T(8,128)S(1)}, f32[1024,1024]{1,0:T(8,128)}, u32[]{:S(2)}) copy-start(f32[1024,1024]{1,0:T(8,128)} %copy-done.1) | copy-start | bytes 12582916
  284.7 3.3 copy-start.26
  301.0 1.6 copy-start.8
  309.4 20.2 %copy-start.11 = (f32[1024,1024]{1,0:T(8,128)}, f32[1024,1024]{1,0:T(8,128)S(1)}, u32[]{:S(2)}) copy-start(f32[1024,1024]{1,0:T(8,128)S(1)} %get-tuple-element.94) | copy-start | bytes 12582916
  344.5 1.6 copy-start.14
  346.1 33.6 %copy-start.9 = (f32[1024,1024]{1,0:T(8,128)}, f32[1024,1024]{1,0:T(8,128)S(1)}, u32[]{:S(2)}) copy-start(f32[1024,1024]{1,0:T(8,128)S(1)} %get-tuple-element.96) | copy-start | bytes 12582916
  349.9 15.0 %copy-start.12 = (f32[1024,1024]{1,0:T(8,128)S(1)}, f32[1024,1024]{1,0:T(8,128)}, u32[]{:S(2)}) copy-start(f32[1024,1024]{1,0:T(8,128)} %copy-done.11) | copy-start | bytes 12582916
  364.9 14.7 %copy-start.25 = (bf16[2,2,4,2,32,1024]{5,4,3,2,1,0:T(8,128)(2,1)S(1)}, bf16[2,2,4,2,32,1024]{5,4,3,2,1,0:T(8,128)(2,1)}, u32[]{:S(2)}) copy-start(bf16[2,2,4,2,32,1024]{5,4,3,2,1,0:T(8,128)(2,1)} %get-tuple-element.63) | copy-start | bytes 6291460
  382.0 3.0 copy-start
  382.0 2.6 copy-start.19
  384.8 1.9 copy-start.13
  556.6 3.5 copy-start.10
  556.6 4.1 copy-start.15
  560.7 10.8 %copy-start.7 = (bf16[1024,1024]{1,0:T(8,128)(2,1)S(1)}, bf16[1024,1024]{1,0:T(8,128)(2,1)}, u32[]{:S(2)}) copy-start(bf16[1024,1024]{1,0:T(8,128)(2,1)} %copy-done.6) | copy-start | bytes 6291460
  571.5 9.7 %copy-start.22 = (bf16[1024]{0:T(1024)(128)(2,1)S(1)}, bf16[1024]{0:T(1024)(128)(2,1)}, u32[]{:S(2)}) copy-start(bf16[1024]{0:T(1024)(128)(2,1)} %get-tuple-element.93) | copy-start | bytes 6148
  571.5 9.7 %copy-start.23 = (bf16[1024]{0:T(1024)(128)(2,1)S(1)}, bf16[1024]{0:T(1024)(128)(2,1)}, u32[]{:S(2)}) copy-start(bf16[1024]{0:T(1024)(128)(2,1)} %get-tuple-element.78) | copy-start | bytes 6148
  571.5 9.7 %copy-start.21 = (bf16[1024]{0:T(1024)(128)(2,1)S(1)}, bf16[1024]{0:T(1024)(128)(2,1)}, u32[]{:S(2)}) copy-start(bf16[1024]{0:T(1024)(128)(2,1)} %get-tuple-element.118) | copy-start | bytes 6148
  581.6 55.2 %copy-start.20 = (f32[32,1024]{1,0:T(8,128)S(1)}, f32[32,1024]{1,0:T(8,128)}, u32[]{:S(2)}) copy-start(f32[32,1024]{1,0:T(8,128)} %get-tuple-element.176) | copy-start | bytes 393220
  581.8 55.7 %copy-start.18 = (f32[32,4096]{1,0:T(8,128)S(1)}, f32[32,4096]{1,0:T(8,128)}, u32[]{:S(2)}) copy-start(f32[32,4096]{1,0:T(8,128)} %get-tuple-element.180) | copy-start | bytes 1572868
  582.6 55.7 %copy-start.17 = (f32[128,1024]{1,0:T(8,128)S(1)}, f32[128,1024]{1,0:T(8,128)}, u32[]{:S(2)}) copy-start(f32[128,1024]{1,0:T(8,128)} %get-tuple-element.182) | copy-start | bytes 1572868

commit v4 on v3

--- a/solution.py
+++ b/solution.py
@@ -21,11 +21,11 @@
     return jnp.dot(a, b, preferred_element_type=jnp.float32)
 
 
-def schedule(step, steps, job, length):
-    at = [i * steps // length for i in range(length)]
-    for s in range(steps):
+def schedule(step, first, last, job, length):
+    at = [first + (2 * i * (last - first) + length - 1) // (2 * (length - 1)) for i in range(length)]
+    for s in range(last + 1):
         count = at.count(s)
-        if count or s == steps - 1:
+        if count:
 
             @pl.when(step == s)
             def _():
@@ -35,15 +35,15 @@
 
 def fwd_kernel(plan, count, tok, lanes, *refs):
     shards, refs = refs[:count], refs[count:]
-    start_ref, wq, wk, wv, bias_ref, qf_ref, kf_ref, refs = *refs[:7], refs[7:]
+    edges, shift_ref, start_ref, wq, wk, wv, bias_ref, qf_ref, kf_ref, refs = *refs[:9], refs[9:]
     fulls, refs = refs[:count], refs[count:]
-    proj_ref, o_ref, f_ref, ka, va, qa = refs[:6]
+    proj_ref, o_ref, f_ref, ka, va, qa, halo = refs[:7]
     step = pl.program_id(0)
-    ext = start_ref.shape[0]
-    half = (ext - tok) // 2
+    half = halo.shape[1]
+    ext = tok + 2 * half
     window = 2 * half + TQ
     if count:
-        send_sem, recv_sem, local_sem = refs[6:]
+        send_sem, recv_sem, local_sem = refs[7:]
         pos = Place()
 
         @pl.when(step == 0)
@@ -51,10 +51,15 @@
             meet(pos, False)
 
         sends = Sends(send_sem, recv_sem, pos.to)
-        schedule(step, FWD_STEPS, gather_job(pos, plan, shards, fulls, sends, local_sem), len(plan) + 4)
+        schedule(step, 0, FWD_STEPS - 1, gather_job(pos, plan, shards, fulls, sends, local_sem), len(plan) + 4)
 
     @pl.when(step == 0)
     def _():
+        for side in range(2):
+            for t in range(half // TQ):
+                rows = slice(t * TQ, (t + 1) * TQ)
+                moved = edges[side, rows, :].astype(jnp.float32) + shift_ref[0:1, :] + shift_ref[1:2, :]
+                halo[side, rows, :] = moved.astype(jnp.bfloat16)
         ka[:, PAIR:] = kf_ref[...]
         va[:, PAIR:] = jnp.ones((ext, PAIR), jnp.bfloat16)
         f_ref[...] = qf_ref[half : half + tok, :]
@@ -63,7 +68,12 @@
     left = lane < HD
     for t in range(ext // TQ):
         rows = slice(t * TQ, (t + 1) * TQ)
-        start = start_ref[rows, :]
+        if t * TQ < half:
+            start = halo[0, rows, :]
+        elif t * TQ < half + tok:
+            start = start_ref[t * TQ - half : (t + 1) * TQ - half, :]
+        else:
+            start = halo[1, t * TQ - half - tok : (t + 1) * TQ - half - tok, :]
         q = (nn(start, wq[...]) + bias_ref[0:1, :]).astype(jnp.bfloat16)
         k = (nn(start, wk[...]) + bias_ref[1:2, :]).astype(jnp.bfloat16)
         v = (nn(start, wv[...]) + bias_ref[2:3, :]).astype(jnp.bfloat16)
@@ -103,12 +113,14 @@
 FWD_STEPS = 8
 
 
-def attn_fwd(start, inproj, bias, qf, kf, lanes, tok, shards=(), parts=(), share=0.0, collective=None):
-    ext, width = start.shape
+def attn_fwd(edges, shift, start, inproj, bias, qf, kf, lanes, shards=(), parts=(), share=0.0, collective=None):
+    tok, width = start.shape
+    half = edges.shape[1]
+    ext = tok + 2 * half
     pairs = width // PAIR
     count = len(shards)
     plan = pieces([v.shape[1] for v in shards], parts, share)
-    anywhere = pl.BlockSpec(memory_space=pl.ANY)
+    anywhere, vmem = pl.BlockSpec(memory_space=pl.ANY), pl.BlockSpec(memory_space=pltpu.VMEM)
     col = lambda base: pl.BlockSpec((width, PAIR), lambda i: (0, base + i))
     fix = pl.BlockSpec((ext, PAIR), lambda i: (0, 0))
     comm = dict(collective_id=collective, has_side_effects=True) if count else {}
@@ -116,7 +128,7 @@
         functools.partial(fwd_kernel, plan, count, tok, lanes),
         grid=(pairs,),
         in_specs=[anywhere] * count
-        + [pl.BlockSpec((ext, width), lambda i: (0, 0)), col(0), col(pairs), col(2 * pairs),
+        + [vmem, vmem, vmem, col(0), col(pairs), col(2 * pairs),
            pl.BlockSpec((8, PAIR), lambda i: (0, i)), fix, fix],
         out_specs=[anywhere] * count
         + [pl.BlockSpec((3, ext, PAIR), lambda i: (0, 0, i)), pl.BlockSpec((tok, PAIR), lambda i: (0, i)),
@@ -128,12 +140,13 @@
             pltpu.VMEM((ext, 2 * PAIR), jnp.bfloat16),
             pltpu.VMEM((ext, 2 * PAIR), jnp.bfloat16),
             pltpu.VMEM((2 * tok // TQ, TQ, 2 * PAIR), jnp.bfloat16),
+            pltpu.VMEM((2, half, width), jnp.bfloat16),
         ] + (semaphores(len(plan) * SENDS, len(plan)) if count else []),
         compiler_params=pltpu.CompilerParams(
             vmem_limit_bytes=56 << 20, dimension_semantics=("arbitrary",), **comm
         ),
         name="attention",
-    )(*shards, start, inproj, inproj, inproj, bias, qf, kf)
+    )(*shards, edges, shift, start, inproj, inproj, inproj, bias, qf, kf)
 
 
 def bwd_kernel(plan, count, counts, tok, lanes, *refs):
@@ -170,7 +183,7 @@
                     next(neighbour)
                 yield
 
-        schedule(step, BWD_STEPS, work(), len(plan) + 4)
+        schedule(step, 0, BWD_STEPS - 1, work(), len(plan) + 4)
     else:
 
         @pl.when(step == 0)
@@ -312,12 +325,6 @@
     return jnp.broadcast_to(vf[None], (ext, PAIR)).astype(jnp.bfloat16)
 
 
-def delta_lanes(delta, lanes):
-    first = delta.astype(jnp.bfloat16)
-    second = (delta - first.astype(jnp.float32)).astype(jnp.bfloat16)
-    return jnp.pad(jnp.concatenate([first, second], axis=1), ((0, 0), (lanes + 48, PAIR - 80 - lanes)))
-
-
 MESH = pl.DeviceIdType.MESH
 
 
@@ -535,24 +542,31 @@
     return value.astype(jnp.float32)
 
 
-def scatter_plan(pos, grad, out, bufs, sends, local, number, base, wide, at):
+def scatter_plan(pos, grad, out, bufs, sends, local, number, base, wide, at, held=False):
     x, c, z, y, nx, nc, ny = pos.x, pos.c, pos.z, pos.y, pos.nx, pos.nc, pos.ny
-    own, got, one1, two1, one2, two2, line, ends = bufs if at else bufs[:2] + (None,) + bufs[2:3] + (None,) + bufs[3:]
     every, one, two = pl.ds(base, wide), pl.ds(0, at), pl.ds(at, wide - at)
+    if held:
+        own, bufs = lambda: grad.at[:, c, :, :, :, every], (None,) + tuple(bufs)
+    else:
+        own = lambda: bufs[0]
+    got, one1, two1, one2, two2, line, ends = bufs[1:] if at else bufs[1:2] + (None,) + bufs[2:3] + (None,) + bufs[3:]
     low = jnp.bfloat16
-    load = local_copy(lambda: grad.at[:, c, :, :, :, every], lambda: own, local, number)
+    if not held:
+        load = local_copy(lambda: grad.at[:, c, :, :, :, every], own, local, number)
     cross = sends.start(lambda: grad.at[:, nc, :, :, :, every], lambda: got, "c")
     yield
-    load.wait()
+    if not held:
+        load.wait()
     cross.wait_recv()
 
     @pl.loop(0, 8)
     def _(i):
-        own[i // 4, lax.rem(i, 4)] = (widen(own[i // 4, lax.rem(i, 4)]) + widen(got[i // 4, lax.rem(i, 4)])).astype(low)
+        mine = own().at[i // 4, lax.rem(i, 4)]
+        mine[...] = (widen(mine[...]) + widen(got[i // 4, lax.rem(i, 4)])).astype(low)
 
     if at:
-        a = sends.start(lambda: own.at[:, :, ny, :, one], lambda: one1, "y")
-    b = sends.start(lambda: own.at[nx, :, :, :, two], lambda: two1, "x")
+        a = sends.start(lambda: own().at[:, :, ny, :, one], lambda: one1, "y")
+    b = sends.start(lambda: own().at[nx, :, :, :, two], lambda: two1, "x")
     yield
     if at:
         a.wait_recv()
@@ -560,7 +574,7 @@
         @pl.loop(0, 8)
         def _(i):
             one1[i // 4, lax.rem(i, 4)] = (
-                widen(own[i // 4, lax.rem(i, 4), y, :, :at]) + widen(one1[i // 4, lax.rem(i, 4)])
+                widen(own().at[i // 4, lax.rem(i, 4), y, :, one][...]) + widen(one1[i // 4, lax.rem(i, 4)])
             ).astype(low)
 
         a2 = sends.start(lambda: one1.at[nx], lambda: one2, "x")
@@ -568,7 +582,7 @@
 
     @pl.loop(0, 4)
     def _(i):
-        two1[i] = (widen(own[x, i, :, :, at:]) + widen(two1[i])).astype(low)
+        two1[i] = (widen(own().at[x, i, :, :, two][...]) + widen(two1[i])).astype(low)
 
     b2 = sends.start(lambda: two1.at[:, ny], lambda: two2, "y")
     yield
@@ -592,8 +606,8 @@
     yield
 
 
-def scatter_bufs(rows, wide, at):
-    shapes = [(2, 4, 2, rows, wide), (2, 4, 2, rows, wide)]
+def scatter_bufs(rows, wide, at, held=False):
+    shapes = [(2, 4, 2, rows, wide)] * (1 if held else 2)
     if at:
         shapes += [(2, 4, rows, at), (4, 2, rows, wide - at), (4, rows, at)]
     else:
@@ -617,12 +631,12 @@
     yield
 
 
-def scatter_job(pos, plan, counts, grads, outs, bufs, sends, local):
+def scatter_job(pos, plan, counts, grads, outs, bufs, sends, local, held=False):
     plans = []
     for i, (k, base, wide, at) in enumerate(plan):
         first = sum(counts[:i])
         mine = bufs[first : first + counts[i]]
-        plans.append(scatter_plan(pos, grads[k], outs[k], mine, sends, local, i, base, wide, at))
+        plans.append(scatter_plan(pos, grads[k], outs[k], mine, sends, local, i, base, wide, at, held))
     yield from turns(plans, sends.finish)
 
 
@@ -661,6 +675,259 @@
     )(*grads)
 
 
+FT = 512
+ROWS = 256
+
+
+def normalize(values):
+    centered = values - jnp.mean(values, axis=1, keepdims=True)
+    inv = lax.rsqrt(jnp.mean(centered * centered, axis=1, keepdims=True) + 1e-05)
+    return centered * inv, inv
+
+
+def normalize_back(grad, normal, inv):
+    return inv * (
+        grad - jnp.mean(grad, axis=1, keepdims=True) - normal * jnp.mean(grad * normal, axis=1, keepdims=True)
+    )
+
+
+def column_sum(values):
+    return jnp.sum(values, axis=0, keepdims=True)
+
+
+def ffn_kernel(plan, count, ups, *refs):
+    source, att, inp, wo, wu, vec, ub, cot = refs[:8]
+    if count:
+        full, refs = refs[8], refs[9:]
+    else:
+        full, refs = source, refs[8:]
+    hid, slope, normal_ref, inv_ref, low_ref, out_ref, grad_ref, grad_low_ref, sums, keep, wd, load = refs[:12]
+    step = pl.program_id(0)
+    tok = att.shape[0]
+    if count:
+        send_sem, recv_sem, local_sem = refs[12:]
+        pos = Place()
+
+        @pl.when(step == 0)
+        def _():
+            meet(pos, False)
+
+        sends = Sends(send_sem, recv_sem, pos.to)
+        schedule(step, 0, ups, gather_job(pos, plan, [source], [full], sends, local_sem), len(plan) + 4)
+    @pl.when(step == 0)
+    def _():
+        sums[...] = jnp.zeros_like(sums)
+        for r in range(tok // ROWS):
+            rows = slice(r * ROWS, (r + 1) * ROWS)
+            branch = nn(att[rows, :], wo[...]) + vec[2:3, :]
+            start = inp[rows, :].astype(jnp.float32) + vec[0:1, :] + vec[1:2, :]
+            normal, inv = normalize(start + branch)
+            normal_ref[rows, :] = normal
+            inv_ref[rows, :] = jnp.broadcast_to(inv, (ROWS, 128))
+            low_ref[rows, :] = (normal * vec[3:4, :] + vec[4:5, :]).astype(jnp.bfloat16)
+            sums[3:4, :] += column_sum(start * start)
+            sums[4:5, :] += column_sum(branch * branch)
+
+    @pl.when(step < ups)
+    def _():
+        at = pl.ds(pl.multiple_of(step * FT, FT), FT)
+        for r in range(tok // ROWS):
+            rows = slice(r * ROWS, (r + 1) * ROWS)
+            up = nn(low_ref[rows, :], wu[...]) + ub[0:1, :]
+            phi = 0.5 * (1.0 + lax.erf(up * 2.0**-0.5))
+            h = (up * phi).astype(jnp.bfloat16)
+            hid[rows, :] = h
+            keep[rows, at] = h
+            slope[rows, :] = (phi + up * (jnp.exp(-0.5 * up * up) * 0.3989422804014327)).astype(jnp.bfloat16)
+
+    @pl.when(step == ups)
+    def _():
+        copy = pltpu.make_async_copy(full, wd, load)
+        copy.start()
+        copy.wait()
+
+    @pl.when(step >= ups)
+    def _():
+        rows = pl.ds(pl.multiple_of((step - ups) * ROWS, ROWS), ROWS)
+        weight = wd[...].reshape(-1, wd.shape[-1])
+        branch = nn(keep[rows, :], weight) + vec[5:6, :]
+        first = normal_ref[rows, :] * vec[3:4, :] + vec[4:5, :]
+        normal, inv = normalize(first + branch)
+        out_ref[...] = (normal * vec[6:7, :] + vec[7:8, :]).astype(jnp.bfloat16)
+        g = cot[...].astype(jnp.float32)
+        grad = normalize_back(g * vec[6:7, :], normal, inv)
+        grad_ref[...] = grad
+        low_grad = grad.astype(jnp.bfloat16)
+        grad_low_ref[...] = low_grad
+        sums[0:1, :] += column_sum(g * normal)
+        sums[1:2, :] += column_sum(g)
+        sums[2:3, :] += column_sum(low_grad.astype(jnp.float32))
+        sums[5:6, :] += column_sum(branch * branch)
+
+
+def ffn_forward(source, att, inp, wo, wu, vec, ub, cot, parts=(), share=0.0, collective=None):
+    tok, width = att.shape
+    wide = wu.shape[1]
+    ups, downs = wide // FT, tok // ROWS
+    count = 1 if parts else 0
+    plan = pieces([source.shape[1]], parts, share) if count else []
+    anywhere, vmem = pl.BlockSpec(memory_space=pl.ANY), pl.BlockSpec(memory_space=pltpu.VMEM)
+    tile = pl.BlockSpec((tok, FT), lambda i: (0, lax.min(i, ups - 1)))
+    row = pl.BlockSpec((ROWS, width), lambda i: (lax.max(i - ups, 0), 0))
+    comm = dict(collective_id=collective, has_side_effects=True) if count else {}
+    f32, low = jnp.float32, jnp.bfloat16
+    shape = jax.ShapeDtypeStruct
+    wd_shape = (2, 2, 4, 2) + source.shape if count else source.shape
+    return pl.pallas_call(
+        functools.partial(ffn_kernel, plan, count, ups),
+        grid=(ups + downs,),
+        in_specs=[anywhere, vmem, vmem, vmem, pl.BlockSpec((width, FT), lambda i: (0, lax.min(i, ups - 1))), vmem,
+                  pl.BlockSpec((8, FT), lambda i: (0, lax.min(i, ups - 1))), row],
+        out_specs=[anywhere] * count + [tile, tile, vmem, vmem, vmem, row, row, row, vmem],
+        out_shape=(full_shapes([source]) if count else [])
+        + [shape((tok, wide), low), shape((tok, wide), low), shape((tok, width), f32), shape((tok, 128), f32),
+           shape((tok, width), low), shape((tok, width), low), shape((tok, width), f32), shape((tok, width), low),
+           shape((8, width), f32)],
+        scratch_shapes=[pltpu.VMEM((tok, wide), low), pltpu.VMEM(wd_shape, low), pltpu.SemaphoreType.DMA]
+        + (semaphores(len(plan) * SENDS, len(plan)) if count else []),
+        compiler_params=pltpu.CompilerParams(vmem_limit_bytes=62 << 20, dimension_semantics=("arbitrary",), **comm),
+        name="feed_forward",
+    )(source, att, inp, wo, wu, vec, ub, cot)
+
+
+def tn(a, b):
+    return lax.dot_general(a, b, (((0,), (0,)), ((), ())), preferred_element_type=jnp.float32)
+
+
+def back_kernel(plan, count, counts, ups, lanes, *refs):
+    hid, gffn, wd, slope, wu, first_low, gsecond, normal_ref, inv_ref, vec, att, wo, feat_ref = refs[:13]
+    down, up_grad, out_grad, up_sum, sums, gin_ref, gatt_ref, feat_out, acc, piece, low_grad = refs[13:24]
+    refs = refs[24:]
+    step = pl.program_id(0)
+    tok, width = gffn.shape
+    last = 2 * ups + tok // ROWS - 1
+    if count:
+        dwd, send_sem, recv_sem, local_sem, bufs = *refs[:4], refs[4:]
+        pos = Place()
+
+        @pl.when(step == ups)
+        def _():
+            meet(pos, False)
+
+        sends = Sends(send_sem, recv_sem, pos.to)
+        job = scatter_job(pos, plan, counts, [dwd], [down], bufs, sends, local_sem, True)
+        schedule(step, ups, last, job, len(plan) + 4)
+
+    @pl.when(step < ups)
+    def _():
+        grad = tn(hid[...], gffn[...]).astype(jnp.bfloat16)
+        if count:
+            each = dwd.shape[4]
+            for k in range(FT // each):
+                at = step * (FT // each) + k
+                dwd[at // 16, lax.rem(at // 8, 2), lax.rem(at // 2, 4), lax.rem(at, 2)] = grad[k * each : (k + 1) * each]
+        else:
+            down[pl.ds(pl.multiple_of(step * FT, FT), FT), :] = grad
+
+    @pl.when((step >= ups) & (step < 2 * ups))
+    def _():
+        total = jnp.zeros((1, FT), jnp.float32)
+        for r in range(tok // ROWS):
+            rows = slice(r * ROWS, (r + 1) * ROWS)
+            g = (nt(gffn[rows, :], wd[...]) * slope[rows, :].astype(jnp.float32)).astype(jnp.bfloat16)
+            piece[rows, :] = g
+            total += column_sum(g.astype(jnp.float32))
+            more = nt(g, wu[...])
+
+            @pl.when(step == ups)
+            def _():
+                acc[rows, :] = more
+
+            @pl.when(step > ups)
+            def _():
+                acc[rows, :] += more
+
+        up_sum[...] = jnp.broadcast_to(total, (8, FT))
+        up_grad[...] = tn(first_low[...], piece[...]).astype(jnp.bfloat16)
+
+    @pl.when(step == 2 * ups)
+    def _():
+        sums[...] = jnp.zeros_like(sums)
+
+    @pl.when(step >= 2 * ups)
+    def _():
+        rows = pl.ds(pl.multiple_of((step - 2 * ups) * ROWS, ROWS), ROWS)
+        g = gsecond[...] + acc[rows, :]
+        normal = normal_ref[...]
+        grad = normalize_back(g * vec[3:4, :], normal, inv_ref[:, :1])
+        gin_ref[...] = grad
+        low = grad.astype(jnp.bfloat16)
+        low_grad[rows, :] = low
+        sums[0:1, :] += column_sum(g * normal)
+        sums[1:2, :] += column_sum(g)
+        sums[2:3, :] += column_sum(low.astype(jnp.float32))
+        gatt = nt(low, wo[...]).astype(jnp.bfloat16)
+        gatt_ref[...] = gatt
+        both = gatt.astype(jnp.float32) * att[rows, :].astype(jnp.float32)
+        lane = lax.broadcasted_iota(jnp.int32, (width, PAIR), 1)
+        head = lax.broadcasted_iota(jnp.int32, (width, PAIR), 0) // HD
+        pick = (lane >= lanes + 48) & (lane < lanes + 80) & (lax.rem(lane - lanes + 128, 16) == head)
+        pick = jnp.where(pick, 1.0, 0.0).astype(jnp.bfloat16)
+        high = both.astype(jnp.bfloat16)
+        delta = nn(high, pick) + nn((both - high.astype(jnp.float32)).astype(jnp.bfloat16), pick)
+        first = delta.astype(jnp.bfloat16)
+        second = (delta - first.astype(jnp.float32)).astype(jnp.bfloat16)
+        lane = lax.broadcasted_iota(jnp.int32, (ROWS, PAIR), 1)
+        feat = feat_ref[...]
+        feat = jnp.where((lane >= lanes + 48) & (lane < lanes + 64), first, feat)
+        feat_out[...] = jnp.where((lane >= lanes + 64) & (lane < lanes + 80), second, feat)
+
+    @pl.when(step == last)
+    def _():
+        for k in range(2):
+            cols = slice(k * width // 2, (k + 1) * width // 2)
+            out_grad[cols, :] = tn(att[:, cols], low_grad[...]).astype(jnp.bfloat16)
+
+
+def ffn_backward(hid, gffn, wd, slope, wu, first_low, gsecond, normal, inv, vec, att, wo, feat, lanes, parts=(), share=0.0,
+                 collective=None):
+    tok, wide = hid.shape
+    width = gffn.shape[1]
+    ups, downs = wide // FT, tok // ROWS
+    count = 1 if parts else 0
+    f32, low = jnp.float32, jnp.bfloat16
+    shape = jax.ShapeDtypeStruct
+    vmem = pl.BlockSpec(memory_space=pltpu.VMEM)
+    whole = lambda r, c: pl.BlockSpec((r, c), lambda i: (0, 0), pipeline_mode=pl.Buffered(1))
+    middle = lambda i: lax.max(lax.min(i - ups, ups - 1), 0)
+    tile = pl.BlockSpec((tok, FT), lambda i: (0, middle(i)))
+    row = lambda c: pl.BlockSpec((ROWS, c), lambda i: (lax.max(i - 2 * ups, 0), 0))
+    scratch = [pltpu.VMEM((tok, width), f32), pltpu.VMEM((tok, FT), low), pltpu.VMEM((tok, width), low)]
+    plan, counts, down, comm = [], [], shape((wide, width), low), {}
+    if count:
+        rows = wide // 32
+        plan = pieces([width], parts, share)
+        bufs = [scatter_bufs(rows, w, at, True) for _, _, w, at in plan]
+        counts = [len(b) for b in bufs]
+        scratch += [pltpu.VMEM((2, 2, 4, 2, rows, width), low)] + semaphores(len(plan) * SENDS, len(plan)) + sum(bufs, [])
+        down, comm = shape((rows, width), f32), dict(collective_id=collective, has_side_effects=True)
+    return pl.pallas_call(
+        functools.partial(back_kernel, plan, count, counts, ups, lanes),
+        grid=(2 * ups + downs,),
+        in_specs=[pl.BlockSpec((tok, FT), lambda i: (0, lax.min(i, ups - 1))), whole(tok, width),
+                  pl.BlockSpec((FT, width), lambda i: (middle(i), 0)), tile,
+                  pl.BlockSpec((width, FT), lambda i: (0, middle(i))), whole(tok, width), row(width), row(width), row(128),
+                  whole(8, width), whole(tok, width), whole(width, width), row(PAIR)],
+        out_specs=[vmem, pl.BlockSpec((width, FT), lambda i: (0, middle(i))), whole(width, width),
+                   pl.BlockSpec((8, FT), lambda i: (0, middle(i))), whole(8, width), row(width), row(width), row(PAIR)],
+        out_shape=[down, shape((width, wide), low), shape((width, width), low), shape((8, wide), f32),
+                   shape((8, width), f32), shape((tok, width), f32), shape((tok, width), low), shape((tok, PAIR), low)],
+        scratch_shapes=scratch,
+        compiler_params=pltpu.CompilerParams(vmem_limit_bytes=62 << 20, dimension_semantics=("arbitrary",), **comm),
+        name="feed_forward_gradients",
+    )(hid, gffn, wd, slope, wu, first_low, gsecond, normal, inv, vec, att, wo, feat)
+
+
 H = 16
 MAXLEN = 512
 TSTEPS = 5000
@@ -685,23 +952,6 @@
     up = [(i, i + 1) for i in range(count - 1)]
     down = [(i + 1, i) for i in range(count - 1)]
     return lax.ppermute(high_part, "blk", up), lax.ppermute(low_part, "blk", down)
-
-
-def norm_forward(values):
-    mean_val = jnp.mean(values, axis=-1, keepdims=True)
-    centered = values - mean_val
-    inv = lax.rsqrt(jnp.mean(centered * centered, axis=-1, keepdims=True) + 1e-05)
-    return centered * inv, inv
-
-
-def norm_backward(grad, normal, inv, gain):
-    scaled = grad * gain
-    grad_in = inv * (
-        scaled
-        - jnp.mean(scaled, axis=-1, keepdims=True)
-        - normal * jnp.mean(scaled * normal, axis=-1, keepdims=True)
-    )
-    return grad_in, jnp.sum(grad * normal, axis=0), jnp.sum(grad, axis=0)
 
 
 def item_of(ends, places):
@@ -718,10 +968,9 @@
     ext = tok + 2 * half
     hidden = upward_w.shape[1]
 
-    mark = jnp.zeros((16, width), jnp.bfloat16)
     keep_own = low(padding)
-    edge_low = jnp.concatenate([inputs[:half], mark.at[0, :half].set(keep_own[:half])])
-    edge_high = jnp.concatenate([inputs[tok - half :], mark.at[0, :half].set(keep_own[tok - half :])])
+    mark = jnp.pad(keep_own.reshape(1, tok), ((0, 15), (0, width - tok)))
+    edges = jnp.stack([jnp.concatenate([inputs[:half], mark]), jnp.concatenate([inputs[tok - half :], mark])])
 
     if fast:
         rows = time_weight.shape[0]
@@ -729,15 +978,15 @@
         cols = jnp.concatenate(cols, axis=1)
         cols = jnp.pad(cols, ((0, 0), (0, 128 - cols.shape[1])))
         *fulls, halo = gather_all(
-            (inproj, cols), (1, 1), 0.0, jnp.stack([edge_low, edge_high]), 0
+            (inproj, cols), (1, 1), 0.5, edges, 0
         )
         inproj_f, small_f = [v.reshape(-1, v.shape[-1]) for v in fulls]
         small_f = as_float(small_f.T)
-        from_low, from_high = halo[0], halo[1]
+        edges = halo
         upward_bias_f = small_f[SMALL : SMALL + hidden // width]
         upward_bias_f = upward_bias_f.reshape(-1, width // rows, rows).transpose(1, 0, 2).reshape(hidden)
     else:
-        from_low, from_high = neighbours(edge_low, edge_high)
+        edges = jnp.stack(neighbours(*edges))
         whole = lambda v: lax.all_gather(v, AXES, axis=0, tiled=True)
         inproj_f, outproj_f, upward_f, downward_f = map(whole, (inproj, outproj, upward_w, downward_w))
         small_f = [as_float(whole(v)) for v in small]
@@ -749,66 +998,57 @@
     ends = jnp.cumsum(lengths[0]).astype(jnp.int32)
     places = offset - half + jnp.arange(ext, dtype=jnp.int32)
     item = jnp.where(places >= 0, item_of(ends, places), -1)
-    keep = jnp.concatenate([from_low[half, :half], keep_own, from_high[half, :half]])
+    keep = jnp.concatenate([edges[0, half, tok - half :], keep_own, edges[1, half, :half]])
+    edges = edges[:, :half]
     query_feat, key_feat, lane = features(item, places, as_float(keep) > 0.5, lengths.shape[1])
 
     time_value = as_float(timestep[0]) / TSTEPS
-    shift = time_value * time_weight_f + time_bias_f
-    start_of = lambda v: as_float(v) + time_value * time_weight_f + time_bias_f
-    start_vec = start_of(inputs)
+    move = time_value * time_weight_f
+    start_vec = as_float(inputs) + move + time_bias_f
     start_low = low(start_vec)
-    start_ext = jnp.concatenate([low(start_of(from_low[:half])), start_low, low(start_of(from_high[:half]))])
+    shift = jnp.pad(jnp.stack([move, time_bias_f]), ((0, 6), (0, 0)))
     bias = jnp.pad(jnp.stack([query_bias_f, jnp.zeros_like(query_bias_f), value_bias_f]), ((0, 5), (0, 0)))
     if fast:
         *fulls, projected, attended, feat_own = attn_fwd(
-            start_ext, inproj_f, bias, query_feat, key_feat, lane, tok, (outproj, upward_w, downward_w), (1, 2, 2), 0.5, 1
+            edges, shift, start_low, inproj_f, bias, query_feat, key_feat, lane, (outproj, upward_w), (1, 4),
+            0.5, 1,
         )
-        outproj_f, upward_f, downward_f = [v.reshape(-1, v.shape[-1]) for v in fulls]
+        outproj_f, upward_f = [v.reshape(-1, v.shape[-1]) for v in fulls]
     else:
-        projected, attended, feat_own = attn_fwd(start_ext, inproj_f, bias, query_feat, key_feat, lane, tok)
-    attn_branch = jnp.dot(attended, outproj_f, preferred_element_type=jnp.float32) + outproj_bias_f
-    first_normal, first_inv = norm_forward(start_vec + attn_branch)
-    first_out = first_normal * first_gain_f + first_shift_f
-    first_low = low(first_out)
-    upward = jnp.dot(first_low, upward_f, preferred_element_type=jnp.float32) + upward_bias_f
-    phi = 0.5 * (1.0 + lax.erf(upward * 2.0**-0.5))
-    hidden_low = low(upward * phi)
-    slope = phi + upward * (jnp.exp(-0.5 * upward * upward) * 0.3989422804014327)
-    ffn_branch = jnp.dot(hidden_low, downward_f, preferred_element_type=jnp.float32) + downward_bias_f
-    second_normal, second_inv = norm_forward(first_out + ffn_branch)
-    layer_out = low(second_normal * second_gain_f + second_shift_f)
-    sums = jnp.stack([jnp.sum(v * v) for v in (start_vec, attn_branch, ffn_branch)])
-
-    grad_second_in, grad_second_gain, grad_second_shift = norm_backward(
-        as_float(cotangent), second_normal, second_inv, second_gain_f
+        projected, attended, feat_own = attn_fwd(
+            edges, shift, start_low, inproj_f, bias, query_feat, key_feat, lane
+        )
+    vec = jnp.stack([move, time_bias_f, outproj_bias_f, first_gain_f, first_shift_f, downward_bias_f, second_gain_f,
+                     second_shift_f])
+    up_bias = jnp.broadcast_to(upward_bias_f, (8, hidden))
+    forward = (attended, inputs, outproj_f, upward_f, vec, up_bias, cotangent)
+    if fast:
+        downward_f, *results = ffn_forward(downward_w, *forward, (4,), 0.5, 2)
+        downward_f = downward_f.reshape(-1, width)
+    else:
+        results = ffn_forward(downward_f, *forward)
+    hidden_low, slope, first_normal, first_inv, first_low, layer_out, grad_second_in, grad_ffn_low, sums = results
+    grad_second_gain, grad_second_shift, grad_down_bias = sums[0], sums[1], sums[2]
+    sums = jnp.sum(sums[3:6], axis=1)
+    backward = functools.partial(
+        ffn_backward, hidden_low, grad_ffn_low, downward_f, slope, upward_f, first_low, grad_second_in, first_normal,
+        first_inv, vec, attended, outproj_f, feat_own, lane
     )
-    grad_ffn_low = low(grad_second_in)
-    grad_down_weight = row_dot(hidden_low, grad_ffn_low)
-    grad_down_bias = jnp.sum(as_float(grad_ffn_low), axis=0)
-    grad_up_low = low(nt(grad_ffn_low, downward_f) * slope)
-    grad_up_weight = row_dot(first_low, grad_up_low)
-    grad_up_bias = jnp.sum(as_float(grad_up_low), axis=0)
-    grad_first = grad_second_in + nt(grad_up_low, upward_f)
-    grad_first_in, grad_first_gain, grad_first_shift = norm_backward(grad_first, first_normal, first_inv, first_gain_f)
-    grad_branch_low = low(grad_first_in)
-    grad_out_weight = row_dot(attended, grad_branch_low)
-    grad_out_bias = jnp.sum(as_float(grad_branch_low), axis=0)
-    grad_attended = low(nt(grad_branch_low, outproj_f))
-
-    head = jnp.arange(width)[:, None] // HD == jnp.arange(H)[None, :]
-    delta = jnp.dot(
-        as_float(grad_attended) * as_float(attended), as_float(head), precision=lax.Precision.HIGHEST
-    )
-    feat_own = jnp.where(jnp.arange(PAIR) < lane + 48, feat_own, delta_lanes(delta, lane))
+    (grad_down, grad_up_weight, grad_out_weight, grad_up_bias, sums_back, grad_first_in, grad_attended,
+     feat_own) = backward((4,), 0.5, 3) if fast else backward()
+    grad_up_bias = grad_up_bias[0]
+    grad_first_gain, grad_first_shift, grad_out_bias = sums_back[0], sums_back[1], sums_back[2]
     packed = jnp.concatenate([grad_attended, feat_own], axis=1)
     values = jnp.pad(sums[None], ((0, 7), (0, 125)))
     backward = functools.partial(
         attn_bwd, projected, grad_attended, query_feat, feat_own, key_feat, delta_key(ext, lane), lane, tok
     )
     if fast:
-        grads = [low(v) for v in (grad_out_weight, grad_up_weight, grad_down_weight)]
         edges = jnp.stack([packed[:half], packed[tok - half :]])
-        out_share, up_share, down_share, sums, grad_q, grad_kv = backward(edges, values, grads, (1, 2, 2), 0.0, 2)
+        down_share = grad_down
+        out_share, up_share, sums, grad_q, grad_kv = backward(
+            edges, values, (grad_out_weight, grad_up_weight), (1, 4), 0.0, 4
+        )
     else:
         edges = jnp.stack(neighbours(packed[:half], packed[tok - half :]))
         sums, grad_q, grad_kv = backward(edges, lax.psum(values, AXES))
@@ -829,13 +1069,13 @@
         cols = grad_up_bias.reshape(width // rows, -1, rows).transpose(1, 0, 2).reshape(-1, width)
         cols = jnp.concatenate([jnp.stack(small_grads), cols]).T
         cols = jnp.pad(cols, ((0, 0), (0, 128 - cols.shape[1])))
-        in_share, last = scatter_all((low(grad_in_weight), low(cols)), (3, 1), 0.5, 3)
+        in_share, last = scatter_all((low(grad_in_weight), low(cols)), (3, 1), 0.5, 5)
         small_shares = [last[:, i] for i in range(SMALL)]
         up_bias_share = last[:, SMALL : SMALL + hidden // width].T.reshape(-1)
     else:
         share = lambda v: lax.psum_scatter(v, AXES, scatter_dimension=0, tiled=True)
         down_share, up_share, out_share, in_share, up_bias_share = map(
-            share, (grad_down_weight, grad_up_weight, grad_out_weight, grad_in_weight, grad_up_bias)
+            share, map(as_float, (grad_down, grad_up_weight, grad_out_weight, grad_in_weight, grad_up_bias))
         )
         small_shares = [share(v) for v in small_grads]
     (time_weight_s, time_bias_s, query_bias_s, value_bias_s, out_bias_s, first_gain_s, first_shift_s,

time: 643 us -> 591 us (0.919)
  matrix products: 130 us -> 22.9 us
  Pallas kernels: 438 us -> 510 us
  other arithmetic: 31.2 us -> 16.6 us
  local copies, waits for them, and re-layouts: 38.1 us -> 29.6 us
    pallas_call x0 -> x2, Pallas kernels: none -> 163 us  [the longest x1 89.4 us: ffn_backward(): pl.pallas_call(functools.partial(back_kernel, plan, count, counts, ups, l...]
    pallas_call x1, Pallas kernels: 136 us -> 86.7 us  [attn_fwd(): pl.pallas_call(functools.partial(fwd_kernel, plan, count, tok, lanes), gr...]
    dot_general x4 -> x0, matrix products: 39.3 us -> none  [the longest x1 18 us: per_device(): jnp.dot(first_low, upward_f, preferred_element_type=jnp.float32)]
    dot_general x4 -> x1, matrix products: 48.3 us -> 11.3 us  [nt(): lax.dot_general(a, b, (((1,), (1,)), ((), ())), preferred_element_type=jn...]
    pallas_call x1, Pallas kernels: 166 us -> 131 us  [attn_bwd(): pl.pallas_call(functools.partial(bwd_kernel, plan, count, counts, tok, la...]
    dot_general x4 -> x1, matrix products: 42.8 us -> 11.6 us  [row_dot(): lax.dot_general(left, right, (((0,), (0,)), ((), ())), preferred_element_...]
    reduce_sum x5 -> x1, other arithmetic: 9.46 us -> 0.12 us  [per_device(): sums = jnp.sum(sums[3:6], axis=1)]
    pallas_call x1, Pallas kernels: 87.3 us -> 78.2 us  [gather_all(): pl.pallas_call(functools.partial(gather_kernel, plan, count), in_specs=[a...]
where the time goes in v4:
time: 591 us; the launch traced here: 581 us
  Pallas kernels  510 us (86%)
  local copies, waits for them, and re-layouts  29.6 us (5%)
  matrix products  22.9 us (4%)
  other arithmetic  16.6 us (3%)
    pallas_call x1, Pallas kernels, attn_bwd(): pl.pallas_call(functools.partial(bwd_kernel, plan, count, counts, tok, la...  131 us
    pallas_call x1, Pallas kernels, ffn_backward(): pl.pallas_call(functools.partial(back_kernel, plan, count, counts, ups, l...  89.4 us
    pallas_call x1, Pallas kernels, attn_fwd(): pl.pallas_call(functools.partial(fwd_kernel, plan, count, tok, lanes), gr...  86.7 us
    pallas_call x1, Pallas kernels, gather_all(): pl.pallas_call(functools.partial(gather_kernel, plan, count), in_specs=[a...  78.2 us
    pallas_call x1, Pallas kernels, ffn_forward(): pl.pallas_call(functools.partial(ffn_kernel, plan, count, ups), grid=(ups...  74 us
    pallas_call x1, Pallas kernels, scatter_all(): pl.pallas_call(functools.partial(scatter_kernel, plan, count, counts), in...  50.6 us

profile of v4, /device:TPU:0, one launch (start us, length us, event | category | flops | bytes accessed | tf_op | source)
XLA Modules:
  0.0 581.1 jit_solution(14848661908768911864)
XLA Ops:
  0.7 1.7 fusion.16
  2.4 0.2 fusion.6
  2.8 1.5 pad_maximum_fusion.4.refs_2_
  4.4 0.1 copy.115
  4.5 0.1 copy.116
  4.6 0.1 copy.117
  4.7 0.1 copy.118
  4.8 0.1 copy.119
  4.9 0.1 copy.120
  5.0 0.1 copy.121
  5.1 0.1 copy.122
  5.2 0.1 copy.123
  5.3 0.1 copy.124
  5.4 0.1 copy.125
  5.5 0.1 concatenate.42
  5.6 0.6 pad.25.refs_1_
  6.3 78.2 %gather_weights.1 = (bf16[2,2,4,2,32,3072]{5,4,3,2,1,0:T(8,128)(2,1)}, bf16[2,2,4,2,32,128]{5,4,3,2,1,0:T(8,128)(2,1)}, bf16[2,528,1024]{2,1,0:T(8,128)(2,1)}) custom-call(bf16[32,3072]{1,0:T(8,128)(2,1)} %refs_0_.3, bf16[32,128]{1,0:T(8,128)(2,1)} %pad.25.refs_1_, bf16[2,528,1024]{2,1,0:T(8,128)(2,1)} %pad_maximum_fusion.4.refs_2_), custom_call_target="tpu_custom_call" | custom-call | tf_op jit(solution)/shard_map/gather_weights/pallas_call | solution.py:530
  84.4 0.7 slice_reduce_fusion.13
  85.2 0.1 copy.127
  85.3 0.1 reduce.3
  85.5 0.1 convert_reduce_fusion
  85.6 1.4 multiply_convert_fusion.2
  87.0 1.4 multiply_convert_fusion
  88.5 2.3 concatenate.49.refs_10_
  90.9 0.3 convert_convert_fusion.1
  91.2 0.3 convert_convert_fusion
  91.6 0.9 broadcast_in_dim.79
  92.4 4.0 concatenate.45.refs_9_.refs_8_
  96.5 0.2 copy.126
  97.4 0.6 fusion.10
  98.1 1.9 add_convert_fusion.refs_4_
  100.1 0.6 pad.28.refs_8_
  100.8 1.5 slice.117.refs_2_
  102.2 86.7 %attention.1 = (bf16[2,2,4,2,32,1024]{5,4,3,2,1,0:T(8,128)(2,1)}, bf16[2,2,4,2,32,4096]{5,4,3,2,1,0:T(8,128)(2,1)}, bf16[3,2048,1024]{2,1,0:T(8,128)(2,1)}, bf16[1024,1024]{1,0:T(8,128)(2,1)}, bf16[1024,128]{1,0:T(8,128)(2,1)}) custom-call(bf16[32,1024]{1,0:T(8,128)(2,1)} %refs_0_.4, bf16[32,4096]{1,0:T(8,128)(2,1)} %refs_1_.1, ...), custom_call_target="tpu_custom_call" | custom-call | tf_op jit(solution)/shard_map/attention/pallas_call | solution.py:127
  189.1 0.1 reshape.194
  189.2 0.7 broadcast_in_dim.81.refs_6_
  189.9 74.0 %feed_forward.1 = (bf16[2,2,4,2,128,1024]{5,4,3,2,1,0:T(8,128)(2,1)}, bf16[1024,4096]{1,0:T(8,128)(2,1)}, bf16[1024,4096]{1,0:T(8,128)(2,1)}, f32[1024,1024]{1,0...) custom-call(bf16[128,1024]{1,0:T(8,128)(2,1)} %refs_0_.5, ...), custom_call_target="tpu_custom_call" | custom-call | tf_op jit(solution)/shard_map/feed_forward/pallas_call | solution.py:781
  263.9 89.4 %feed_forward_gradients.1 = (f32[128,1024]{1,0:T(8,128)}, bf16[1024,4096]{1,0:T(8,128)(2,1)}, bf16[1024,1024]{1,0:T(8,128)(2,1)}, f32[8,4096]{1,0:T(8,128)}, f32...) custom-call(bf16[1024,4096]{1,0:T(8,128)(2,1)} %get-tuple-element.58.refs_0_, ...), custom_call_target="tpu_custom_call" | custom-call | tf_op jit(solution)/shard_map/feed_forward_gradients/pallas_call | solution.py:914
  353.3 1.8 constant_dynamic-update-slice_fusion.1
  355.2 0.2 slice_bitcast_fusion.3
  355.4 1.7 pad_maximum_fusion.3.refs_2_
  357.1 0.1 slice_reduce_fusion.11
  357.3 0.6 pad.29.refs_3_
  357.9 0.9 broadcast_in_dim.85.refs_11_
  358.7 131.0 %attention_gradients.1 = (f32[32,1024]{1,0:T(8,128)}, f32[32,4096]{1,0:T(8,128)}, f32[8,128]{1,0:T(8,128)}, bf16[1024,1024]{1,0:T(8,128)(2,1)}, bf16[2,1024,1024]{2,1,0:T(8,128)(2,1)}) custom-call(bf16[2,2,4,2,32,1024]{5,4,3,2,1,0:T(8,128)(2,1)} %bitcast.63, bf16[2,2,4,2,32,4096]{5,4,3,2,1,0:T(8,128)(2,1)} %bitcast.58, ...), custom_call_target="tpu_custom_call" | custom-call | tf_op jit(solution)/shard_map/attention_gradients/pallas_call | solution.py:281
  489.7 3.2 slice_reduce_fusion
  493.0 0.8 copy-done.27
  493.8 11.3 %fusion.15 = (f32[1024]{0:T(1024)S(1)}, bf16[1024,1024]{1,0:T(8,128)(2,1)}) fusion(f32[1024,1024]{1,0:T(8,128)S(1)} %copy-done.27, bf16[1024,3072]{1,0:T(8,128)(2,1)} %bitcast.55, bf16[1024,1024]{1,0:T(8,128)(2,1)S(1)} %get-tuple-element.97, bf16[1024,1024]{1,0:T(8,128)(2,1)S(1)} %get-tuple-element.98, bf16[1024,1024]{1,0:T(8,128)(2,1)S(1)} %copy-done.5), kind=kOutput, calls=%fused_computation.70 | convolution fusion | flops 6464470016 | bytes 18878464 | tf_op jit(solution)/shard_map/dot_general | solution.py:17
  505.2 2.1 reduce
  507.3 0.9 fusion.11
  508.3 0.1 reshape.199
  508.6 0.2 copy.135
  508.8 0.8 pad.30.clone
  509.6 11.6 %convolution_convert_fusion = bf16[1024,3072]{1,0:T(8,128)(2,1)} fusion(bf16[1024,1024]{1,0:T(8,128)(2,1)S(1)} %copy-done.1, bf16[1024,1024]{1,0:T(8,128)(2,1)} %copy-done.2, bf16[1024,1024]{1,0:T(8,128)(2,1)} %copy-done.3, bf16[1024,1024]{1,0:T(8,128)(2,1)} %get-tuple-element.74), kind=kOutput, calls=%fused_computation.1 | convolution fusion | flops 6464471040 | bytes 14680064 | tf_op jit(solution)/shard_map/dot_general | solution.py:947
  521.1 50.6 %sum_gradients.1 = (f32[32,3072]{1,0:T(8,128)}, f32[32,128]{1,0:T(8,128)}) custom-call(bf16[2,2,4,2,32,3072]{5,4,3,2,1,0:T(8,128)(2,1)} %bitcast.62, bf16[2,2,4,2,32,128]{5,4,3,2,1,0:T(8,128)(2,1)} %bitcast.64), custom_call_target="tpu_custom_call" | custom-call | tf_op jit(solution)/shard_map/sum_gradients/pallas_call | solution.py:665
  571.7 0.8 slice_bitcast_fusion.4
  572.6 0.6 reshape.201
  573.2 2.0 slice_reduce_fusion.1
  575.1 1.2 sqrt_bitcast_fusion
  576.4 1.3 copy.145
  577.7 0.7 copy.146
  578.4 0.7 copy.147
  579.1 0.8 copy.148
  579.9 0.8 copy.149
  (91 shorter events, 1.2 us)
Async XLA Ops:
  0.7 1.7 copy-start.15
  2.6 1.7 copy-start.28
  2.6 1.8 copy-start.16
  2.7 1.9 copy-start.17
  2.7 2.0 copy-start.18
  2.7 2.1 copy-start.19
  2.7 2.2 copy-start.20
  2.7 2.3 copy-start.21
  2.7 2.4 copy-start.22
  2.7 2.5 copy-start.23
  2.7 2.6 copy-start.24
  2.7 2.7 copy-start.25
  4.3 80.9 %copy-start.26 = (s32[1,32]{1,0:T(1,128)S(1)}, s32[1,32]{1,0:T(1,128)}, u32[]{:S(2)}) copy-start(s32[1,32]{1,0:T(1,128)} %param.23) | copy-start | bytes 388
  91.2 5.3 copy-start.11
  92.4 5.6 copy-start
  98.1 2.7 copy-start.6
  353.3 1.8 copy-start.7
  355.4 1.7 copy-start.13
  489.7 3.3 copy-start.5
  489.7 4.1 copy-start.27
  493.0 12.1 %copy-start.2 = (bf16[1024,1024]{1,0:T(8,128)(2,1)}, bf16[1024,1024]{1,0:T(8,128)(2,1)S(1)}, u32[]{:S(2)}) copy-start(bf16[1024,1024]{1,0:T(8,128)(2,1)S(1)} %get-tuple-element.97) | copy-start | bytes 6291460
  493.0 12.1 %copy-start.3 = (bf16[1024,1024]{1,0:T(8,128)(2,1)}, bf16[1024,1024]{1,0:T(8,128)(2,1)S(1)}, u32[]{:S(2)}) copy-start(bf16[1024,1024]{1,0:T(8,128)(2,1)S(1)} %get-tuple-element.98) | copy-start | bytes 6291460
  505.1 3.3 copy-start.14
  505.1 4.5 copy-start.1
  521.1 55.2 %copy-start.4 = (bf16[1024,1024]{1,0:T(8,128)(2,1)S(1)}, bf16[1024,1024]{1,0:T(8,128)(2,1)}, u32[]{:S(2)}) copy-start(bf16[1024,1024]{1,0:T(8,128)(2,1)} %get-tuple-element.142) | copy-start | bytes 6291460
  573.2 4.5 copy-start.10
  576.3 2.1 copy-start.12
  576.3 2.7 copy-start.9
  576.3 3.5 copy-start.8

commit v5 on v4

--- a/solution.py
+++ b/solution.py
@@ -21,9 +21,12 @@
     return jnp.dot(a, b, preferred_element_type=jnp.float32)
 
 
-def schedule(step, first, last, job, length):
-    at = [first + (2 * i * (last - first) + length - 1) // (2 * (length - 1)) for i in range(length)]
-    for s in range(last + 1):
+def spread(first, last, length):
+    return [first + (2 * i * (last - first) + length - 1) // (2 * (length - 1)) for i in range(length)]
+
+
+def place(step, at, job):
+    for s in range(at[-1] + 1):
         count = at.count(s)
         if count:
 
@@ -33,25 +36,12 @@
                     next(job)
 
 
-def fwd_kernel(plan, count, tok, lanes, *refs):
-    shards, refs = refs[:count], refs[count:]
-    edges, shift_ref, start_ref, wq, wk, wv, bias_ref, qf_ref, kf_ref, refs = *refs[:9], refs[9:]
-    fulls, refs = refs[:count], refs[count:]
-    proj_ref, o_ref, f_ref, ka, va, qa, halo = refs[:7]
-    step = pl.program_id(0)
+def attention_body(step, tok, lanes, edges, shift_ref, start_ref, wq, wk, wv, bias_ref, qf_ref, kf_ref,
+                   proj_ref, o_ref, f_ref, ka, va, qa, halo):
     half = halo.shape[1]
     ext = tok + 2 * half
     window = 2 * half + TQ
-    if count:
-        send_sem, recv_sem, local_sem = refs[7:]
-        pos = Place()
-
-        @pl.when(step == 0)
-        def _():
-            meet(pos, False)
-
-        sends = Sends(send_sem, recv_sem, pos.to)
-        schedule(step, 0, FWD_STEPS - 1, gather_job(pos, plan, shards, fulls, sends, local_sem), len(plan) + 4)
+    columns = pl.ds(pl.multiple_of(step * PAIR, PAIR), PAIR)
 
     @pl.when(step == 0)
     def _():
@@ -106,47 +96,40 @@
                 piece = rest.astype(jnp.bfloat16)
                 rest = rest - piece.astype(jnp.float32)
                 feat = jnp.where(lane == lanes + part * 16 + 2 * step + side, piece, feat)
-        o_ref[own, :] = jnp.where(left, out[0], out[1]).astype(jnp.bfloat16)
+        o_ref[own, columns] = jnp.where(left, out[0], out[1]).astype(jnp.bfloat16)
         f_ref[own, :] = feat
 
 
-FWD_STEPS = 8
-
-
-def attn_fwd(edges, shift, start, inproj, bias, qf, kf, lanes, shards=(), parts=(), share=0.0, collective=None):
+def fwd_kernel(tok, lanes, *refs):
+    attention_body(pl.program_id(0), tok, lanes, *refs)
+
+
+def fixed(*shape):
+    return pl.BlockSpec(shape, lambda i: (0,) * len(shape), pipeline_mode=pl.Buffered(1))
+
+
+def attention_specs(tok, ext, width):
+    half, last = (ext - tok) // 2, width // PAIR - 1
+    col = lambda base: pl.BlockSpec((width, PAIR), lambda i: (0, base * (last + 1) + lax.min(i, last)))
+    ins = [fixed(2, half, width), fixed(8, width), fixed(tok, width), col(0), col(1), col(2),
+           pl.BlockSpec((8, PAIR), lambda i: (0, lax.min(i, last))), fixed(ext, PAIR), fixed(ext, PAIR)]
+    outs = [pl.BlockSpec((3, ext, PAIR), lambda i: (0, 0, lax.min(i, last))), fixed(tok, width), fixed(tok, PAIR)]
+    shape, low = jax.ShapeDtypeStruct, jnp.bfloat16
+    shapes = [shape((3, ext, width), low), shape((tok, width), low), shape((tok, PAIR), low)]
+    scratch = [pltpu.VMEM((ext, 2 * PAIR), low), pltpu.VMEM((ext, 2 * PAIR), low),
+               pltpu.VMEM((2 * tok // TQ, TQ, 2 * PAIR), low), pltpu.VMEM((2, half, width), low)]
+    return ins, outs, shapes, scratch
+
+
+def attn_fwd(edges, shift, start, inproj, bias, qf, kf, lanes):
     tok, width = start.shape
-    half = edges.shape[1]
-    ext = tok + 2 * half
-    pairs = width // PAIR
-    count = len(shards)
-    plan = pieces([v.shape[1] for v in shards], parts, share)
-    anywhere, vmem = pl.BlockSpec(memory_space=pl.ANY), pl.BlockSpec(memory_space=pltpu.VMEM)
-    col = lambda base: pl.BlockSpec((width, PAIR), lambda i: (0, base + i))
-    fix = pl.BlockSpec((ext, PAIR), lambda i: (0, 0))
-    comm = dict(collective_id=collective, has_side_effects=True) if count else {}
+    ins, outs, shapes, scratch = attention_specs(tok, tok + 2 * (edges.shape[1] - 16), width)
     return pl.pallas_call(
-        functools.partial(fwd_kernel, plan, count, tok, lanes),
-        grid=(pairs,),
-        in_specs=[anywhere] * count
-        + [vmem, vmem, vmem, col(0), col(pairs), col(2 * pairs),
-           pl.BlockSpec((8, PAIR), lambda i: (0, i)), fix, fix],
-        out_specs=[anywhere] * count
-        + [pl.BlockSpec((3, ext, PAIR), lambda i: (0, 0, i)), pl.BlockSpec((tok, PAIR), lambda i: (0, i)),
-           pl.BlockSpec((tok, PAIR), lambda i: (0, 0))],
-        out_shape=full_shapes(shards)
-        + [jax.ShapeDtypeStruct((3, ext, width), jnp.bfloat16), jax.ShapeDtypeStruct((tok, width), jnp.bfloat16),
-           jax.ShapeDtypeStruct((tok, PAIR), jnp.bfloat16)],
-        scratch_shapes=[
-            pltpu.VMEM((ext, 2 * PAIR), jnp.bfloat16),
-            pltpu.VMEM((ext, 2 * PAIR), jnp.bfloat16),
-            pltpu.VMEM((2 * tok // TQ, TQ, 2 * PAIR), jnp.bfloat16),
-            pltpu.VMEM((2, half, width), jnp.bfloat16),
-        ] + (semaphores(len(plan) * SENDS, len(plan)) if count else []),
-        compiler_params=pltpu.CompilerParams(
-            vmem_limit_bytes=56 << 20, dimension_semantics=("arbitrary",), **comm
-        ),
+        functools.partial(fwd_kernel, tok, lanes),
+        grid=(width // PAIR,), in_specs=ins, out_specs=outs, out_shape=shapes, scratch_shapes=scratch,
+        compiler_params=pltpu.CompilerParams(vmem_limit_bytes=56 << 20, dimension_semantics=("arbitrary",)),
         name="attention",
-    )(*shards, edges, shift, start, inproj, inproj, inproj, bias, qf, kf)
+    )(edges, shift, start, inproj, inproj, inproj, bias, qf, kf)
 
 
 def bwd_kernel(plan, count, counts, tok, lanes, *refs):
@@ -172,6 +155,9 @@
 
         sends = Sends(send_sem, recv_sem, pos.to)
 
+        at = spread(0, BWD_STEPS - 1, len(plan) + 4)
+        ready = max(i for i, s in enumerate(at) if s <= pairs)
+
         def work():
             neighbour = halo_plan(pos, edges, halo, sends, local_sem, len(plan))
             total = total_plan(values, result, sums, sends)
@@ -179,11 +165,11 @@
             for i, _ in enumerate(scatter_job(pos, plan, counts, grads, outs, refs, sends, local_sem)):
                 if i < 6:
                     next(total)
-                if i == HALO_TURN:
+                if i == ready:
                     next(neighbour)
                 yield
 
-        schedule(step, 0, BWD_STEPS - 1, work(), len(plan) + 4)
+        place(step, at, work())
     else:
 
         @pl.when(step == 0)
@@ -257,10 +243,9 @@
 
 
 BWD_STEPS = 16
-HALO_TURN = 3
-
-
-def attn_bwd(proj, grad, qf, own_feat, kf, vf, lanes, tok, edges, values, grads=(), parts=(), share=0.0, collective=None):
+
+
+def attn_bwd(proj, packed, qf, kf, vf, lanes, tok, edges, values, grads=(), parts=(), share=0.0, collective=None):
     _, ext, width = proj.shape
     pairs = width // PAIR
     half = (ext - tok) // 2
@@ -283,7 +268,8 @@
         grid=(2 * pairs,),
         in_specs=[anywhere] * count
         + [anywhere if count else vmem, vmem, third(0), third(1), third(2),
-           pl.BlockSpec((tok, PAIR), lambda i: (0, lax.rem(i, pairs))), fix(ext), fix(tok), fix(ext), fix(ext)],
+           pl.BlockSpec((tok, PAIR), lambda i: (0, lax.rem(i, pairs))), fix(ext),
+           pl.BlockSpec((tok, PAIR), lambda i: (0, pairs)), fix(ext), fix(ext)],
         out_specs=[vmem] * count
         + [vmem, pl.BlockSpec((tok, PAIR), lambda i: (0, lax.min(i, pairs - 1))),
            pl.BlockSpec((2, tok, PAIR), lambda i: (0, 0, lax.max(i - pairs, 0)))],
@@ -295,12 +281,7 @@
             vmem_limit_bytes=62 << 20, dimension_semantics=("arbitrary",), **comm
         ),
         name="attention_gradients",
-    )(*grads, edges, values, proj, proj, proj, grad, qf, own_feat, kf, vf)
-
-
-def bits(values, count):
-    planes = (values[:, None] >> jnp.arange(count, dtype=jnp.int32)[None, :]) & 1
-    return planes.astype(jnp.float32)
+    )(*grads, edges, values, proj, proj, proj, packed, qf, packed, kf, vf)
 
 
 def features(item, places, keep, n_items):
@@ -309,13 +290,15 @@
     pb = (ext - 1).bit_length()
     lanes = 2 * (nb + pb)
     assert lanes + 80 <= PAIR and ext == 1 << pb
-    ib = bits(item + 1, nb)
-    ps = bits(places, pb)
-    kept = keep.astype(jnp.float32)[:, None]
-    lost = 1 - kept
-    qf = jnp.concatenate([ib, 1 - ib, ps, 1 - ps, jnp.zeros((ext, PAIR - lanes))], axis=1)
-    kf = jnp.concatenate([NEG * kept * (1 - ib), NEG * kept * ib, NEG * lost * (1 - ps), NEG * lost * ps,
-                          -jnp.ones((ext, 48)), jnp.zeros((ext, PAIR - 48 - lanes))], axis=1)
+    lane = jnp.arange(PAIR, dtype=jnp.int32)
+    of_item = lane < 2 * nb
+    shift = jnp.where(of_item, lane % nb, (lane - 2 * nb) % pb)
+    turned = jnp.where(of_item, lane // nb, (lane - 2 * nb) // pb)
+    bit = ((jnp.where(of_item, (item + 1)[:, None], places[:, None]) >> shift) ^ turned) & 1
+    used = lane < lanes
+    active = of_item == keep[:, None]
+    qf = jnp.where(used, bit, 0)
+    kf = jnp.where(used, jnp.where(active & (bit == 0), NEG, 0.0), jnp.where(lane < lanes + 48, -1.0, 0.0))
     return qf.astype(jnp.bfloat16), kf.astype(jnp.bfloat16), lanes
 
 
@@ -433,12 +416,13 @@
 SENDS = 12
 
 
-def turns(plans, last):
-    for turn in range(len(plans) + 4):
+def turns(plans, last, begin=None):
+    begin = begin or list(range(len(plans)))
+    for turn in range(begin[-1] + 5):
         for k in reversed(range(len(plans))):
-            if 0 <= turn - k <= 4:
+            if 0 <= turn - begin[k] <= 4:
                 next(plans[k])
-        if turn == len(plans) + 3:
+        if turn == begin[-1] + 4:
             last()
         yield
 
@@ -550,7 +534,6 @@
     else:
         own = lambda: bufs[0]
     got, one1, two1, one2, two2, line, ends = bufs[1:] if at else bufs[1:2] + (None,) + bufs[2:3] + (None,) + bufs[3:]
-    low = jnp.bfloat16
     if not held:
         load = local_copy(lambda: grad.at[:, c, :, :, :, every], own, local, number)
     cross = sends.start(lambda: grad.at[:, nc, :, :, :, every], lambda: got, "c")
@@ -562,7 +545,7 @@
     @pl.loop(0, 8)
     def _(i):
         mine = own().at[i // 4, lax.rem(i, 4)]
-        mine[...] = (widen(mine[...]) + widen(got[i // 4, lax.rem(i, 4)])).astype(low)
+        mine[...] = mine[...] + got[i // 4, lax.rem(i, 4)]
 
     if at:
         a = sends.start(lambda: own().at[:, :, ny, :, one], lambda: one1, "y")
@@ -573,16 +556,14 @@
 
         @pl.loop(0, 8)
         def _(i):
-            one1[i // 4, lax.rem(i, 4)] = (
-                widen(own().at[i // 4, lax.rem(i, 4), y, :, one][...]) + widen(one1[i // 4, lax.rem(i, 4)])
-            ).astype(low)
+            one1[i // 4, lax.rem(i, 4)] = own().at[i // 4, lax.rem(i, 4), y, :, one][...] + one1[i // 4, lax.rem(i, 4)]
 
         a2 = sends.start(lambda: one1.at[nx], lambda: one2, "x")
     b.wait_recv()
 
     @pl.loop(0, 4)
     def _(i):
-        two1[i] = (widen(own().at[x, i, :, :, two][...]) + widen(two1[i])).astype(low)
+        two1[i] = own().at[x, i, :, :, two][...] + two1[i]
 
     b2 = sends.start(lambda: two1.at[:, ny], lambda: two2, "y")
     yield
@@ -593,8 +574,8 @@
     @pl.loop(0, 4)
     def _(i):
         if at:
-            line[i, :, :at] = (widen(one1[x, i]) + widen(one2[i])).astype(low)
-        line[i, :, at:] = (widen(two1[i, y]) + widen(two2[i])).astype(low)
+            line[i, :, :at] = one1[x, i] + one2[i]
+        line[i, :, at:] = two1[i, y] + two2[i]
 
     last = [
         sends.start(lambda k=k: line.at[pos.nz[k]], lambda k=k: ends.at[k - 1], k) for k in (1, 2, 3)
@@ -631,13 +612,13 @@
     yield
 
 
-def scatter_job(pos, plan, counts, grads, outs, bufs, sends, local, held=False):
+def scatter_job(pos, plan, counts, grads, outs, bufs, sends, local, held=False, begin=None):
     plans = []
     for i, (k, base, wide, at) in enumerate(plan):
         first = sum(counts[:i])
         mine = bufs[first : first + counts[i]]
         plans.append(scatter_plan(pos, grads[k], outs[k], mine, sends, local, i, base, wide, at, held))
-    yield from turns(plans, sends.finish)
+    yield from turns(plans, sends.finish, begin)
 
 
 def scatter_layout(grads, parts, share):
@@ -695,56 +676,41 @@
     return jnp.sum(values, axis=0, keepdims=True)
 
 
-def ffn_kernel(plan, count, ups, *refs):
-    source, att, inp, wo, wu, vec, ub, cot = refs[:8]
-    if count:
-        full, refs = refs[8], refs[9:]
-    else:
-        full, refs = source, refs[8:]
-    hid, slope, normal_ref, inv_ref, low_ref, out_ref, grad_ref, grad_low_ref, sums, keep, wd, load = refs[:12]
-    step = pl.program_id(0)
+def ffn_body(step, ups, whole_weight, up_weight, att, inp, wo, vec, ub, cot, hid, slope, normal_ref, inv_ref, low_ref,
+             out_ref, grad_ref, grad_low_ref, sums, keep, wd, low):
     tok = att.shape[0]
-    if count:
-        send_sem, recv_sem, local_sem = refs[12:]
-        pos = Place()
-
-        @pl.when(step == 0)
-        def _():
-            meet(pos, False)
-
-        sends = Sends(send_sem, recv_sem, pos.to)
-        schedule(step, 0, ups, gather_job(pos, plan, [source], [full], sends, local_sem), len(plan) + 4)
+
     @pl.when(step == 0)
     def _():
         sums[...] = jnp.zeros_like(sums)
         for r in range(tok // ROWS):
             rows = slice(r * ROWS, (r + 1) * ROWS)
-            branch = nn(att[rows, :], wo[...]) + vec[2:3, :]
+            branch = nn(att[rows, :], wo().reshape(-1, att.shape[1])) + vec[2:3, :]
             start = inp[rows, :].astype(jnp.float32) + vec[0:1, :] + vec[1:2, :]
             normal, inv = normalize(start + branch)
             normal_ref[rows, :] = normal
             inv_ref[rows, :] = jnp.broadcast_to(inv, (ROWS, 128))
-            low_ref[rows, :] = (normal * vec[3:4, :] + vec[4:5, :]).astype(jnp.bfloat16)
+            first = (normal * vec[3:4, :] + vec[4:5, :]).astype(jnp.bfloat16)
+            low[rows, :] = first
+            low_ref[:, rows] = first.T
             sums[3:4, :] += column_sum(start * start)
             sums[4:5, :] += column_sum(branch * branch)
 
-    @pl.when(step < ups)
+    @pl.when((step >= 0) & (step < ups))
     def _():
         at = pl.ds(pl.multiple_of(step * FT, FT), FT)
         for r in range(tok // ROWS):
             rows = slice(r * ROWS, (r + 1) * ROWS)
-            up = nn(low_ref[rows, :], wu[...]) + ub[0:1, :]
+            up = nn(low[rows, :], up_weight()) + ub[0:1, at]
             phi = 0.5 * (1.0 + lax.erf(up * 2.0**-0.5))
             h = (up * phi).astype(jnp.bfloat16)
-            hid[rows, :] = h
+            hid[:, rows] = h.T
             keep[rows, at] = h
             slope[rows, :] = (phi + up * (jnp.exp(-0.5 * up * up) * 0.3989422804014327)).astype(jnp.bfloat16)
 
     @pl.when(step == ups)
     def _():
-        copy = pltpu.make_async_copy(full, wd, load)
-        copy.start()
-        copy.wait()
+        whole_weight()
 
     @pl.when(step >= ups)
     def _():
@@ -765,34 +731,126 @@
         sums[5:6, :] += column_sum(branch * branch)
 
 
-def ffn_forward(source, att, inp, wo, wu, vec, ub, cot, parts=(), share=0.0, collective=None):
+def ffn_specs(tok, width, wide, wd_shape, begin):
+    ups = wide // FT
+    f32, low, shape = jnp.float32, jnp.bfloat16, jax.ShapeDtypeStruct
+    now = lambda i: lax.max(lax.min(i - begin, ups - 1), 0)
+    row = pl.BlockSpec((ROWS, width), lambda i: (lax.max(i - begin - ups, 0), 0))
+    ins = [fixed(8, width), fixed(8, wide), row]
+    outs = [pl.BlockSpec((FT, tok), lambda i: (now(i), 0)), pl.BlockSpec((tok, FT), lambda i: (0, now(i))),
+            fixed(tok, width), fixed(tok, 128), fixed(width, tok), row, row, row, fixed(8, width)]
+    shapes = [shape((wide, tok), low), shape((tok, wide), low), shape((tok, width), f32), shape((tok, 128), f32),
+              shape((width, tok), low), shape((tok, width), low), shape((tok, width), f32), shape((tok, width), low),
+              shape((8, width), f32)]
+    scratch = [pltpu.VMEM((tok, wide), low), pltpu.VMEM(wd_shape, low), pltpu.VMEM((tok, width), low)]
+    return ins, outs, shapes, scratch
+
+
+def ffn_kernel(ups, *refs):
+    down, att, inp, wo, wu, refs = *refs[:5], refs[5:]
+    load, wd = refs[-1], refs[-3]
+
+    def whole_weight():
+        copy = pltpu.make_async_copy(down, wd, load)
+        copy.start()
+        copy.wait()
+
+    ffn_body(pl.program_id(0), ups, whole_weight, lambda: wu[...], att, inp, lambda: wo[...], *refs[:-1])
+
+
+def ffn_forward(down, att, inp, wo, wu, vec, ub, cot):
     tok, width = att.shape
     wide = wu.shape[1]
-    ups, downs = wide // FT, tok // ROWS
-    count = 1 if parts else 0
-    plan = pieces([source.shape[1]], parts, share) if count else []
-    anywhere, vmem = pl.BlockSpec(memory_space=pl.ANY), pl.BlockSpec(memory_space=pltpu.VMEM)
-    tile = pl.BlockSpec((tok, FT), lambda i: (0, lax.min(i, ups - 1)))
-    row = pl.BlockSpec((ROWS, width), lambda i: (lax.max(i - ups, 0), 0))
-    comm = dict(collective_id=collective, has_side_effects=True) if count else {}
-    f32, low = jnp.float32, jnp.bfloat16
-    shape = jax.ShapeDtypeStruct
-    wd_shape = (2, 2, 4, 2) + source.shape if count else source.shape
+    ups = wide // FT
+    ins, outs, shapes, scratch = ffn_specs(tok, width, wide, down.shape, 0)
     return pl.pallas_call(
-        functools.partial(ffn_kernel, plan, count, ups),
-        grid=(ups + downs,),
-        in_specs=[anywhere, vmem, vmem, vmem, pl.BlockSpec((width, FT), lambda i: (0, lax.min(i, ups - 1))), vmem,
-                  pl.BlockSpec((8, FT), lambda i: (0, lax.min(i, ups - 1))), row],
-        out_specs=[anywhere] * count + [tile, tile, vmem, vmem, vmem, row, row, row, vmem],
-        out_shape=(full_shapes([source]) if count else [])
-        + [shape((tok, wide), low), shape((tok, wide), low), shape((tok, width), f32), shape((tok, 128), f32),
-           shape((tok, width), low), shape((tok, width), low), shape((tok, width), f32), shape((tok, width), low),
-           shape((8, width), f32)],
-        scratch_shapes=[pltpu.VMEM((tok, wide), low), pltpu.VMEM(wd_shape, low), pltpu.SemaphoreType.DMA]
-        + (semaphores(len(plan) * SENDS, len(plan)) if count else []),
-        compiler_params=pltpu.CompilerParams(vmem_limit_bytes=62 << 20, dimension_semantics=("arbitrary",), **comm),
+        functools.partial(ffn_kernel, ups),
+        grid=(ups + tok // ROWS,),
+        in_specs=[pl.BlockSpec(memory_space=pl.ANY), fixed(tok, width), fixed(tok, width), fixed(width, width),
+                  pl.BlockSpec((width, FT), lambda i: (0, lax.min(i, ups - 1)))] + ins,
+        out_specs=outs, out_shape=shapes, scratch_shapes=scratch + [pltpu.SemaphoreType.DMA],
+        compiler_params=pltpu.CompilerParams(vmem_limit_bytes=62 << 20, dimension_semantics=("arbitrary",)),
         name="feed_forward",
-    )(source, att, inp, wo, wu, vec, ub, cot)
+    )(down, att, inp, wo, wu, vec, ub, cot)
+
+
+def layer_kernel(plan, at, ups, tok, lanes, *refs):
+    shards, refs = refs[:3], refs[3:]
+    attention_in, refs = refs[:9], refs[9:]
+    inp, ffn_in, refs = refs[0], refs[1:4], refs[4:]
+    fulls, refs = refs[:3], refs[3:]
+    attention_out, ffn_out, refs = refs[:3], refs[3:12], refs[12:]
+    attention_scratch, ffn_scratch, refs = refs[:4], refs[4:7], refs[7:]
+    wo, wu, load, send_sem, recv_sem, local_sem = refs
+    step = pl.program_id(0)
+    begin = attention_out[1].shape[1] // PAIR
+    pos = Place()
+
+    @pl.when(step == 0)
+    def _():
+        meet(pos, False)
+
+    sends = Sends(send_sem, recv_sem, pos.to)
+    place(step, at, gather_job(pos, plan, shards, fulls, sends, local_sem))
+
+    @pl.when(step < begin)
+    def _():
+        attention_body(step, tok, lanes, *attention_in, *attention_out, *attention_scratch)
+
+    turn = step - begin
+    wo_load = Copy(lambda: pltpu.make_async_copy(fulls[0], wo, load.at[2]))
+    wd_load = Copy(lambda: pltpu.make_async_copy(fulls[2], ffn_scratch[1], load.at[2]))
+
+    def wu_load(k):
+        slot = lax.rem(k, 2)
+        columns = pl.ds(pl.multiple_of(k * FT, FT), FT)
+        return pltpu.make_async_copy(fulls[1].at[:, :, :, :, :, columns], wu.at[slot], load.at[slot])
+
+    @pl.when(turn == 0)
+    def _():
+        wo_load.start()
+        wu_load(0).start()
+        wo_load.wait()
+
+    @pl.when((turn >= 0) & (turn < ups - 1))
+    def _():
+        wu_load(turn + 1).start()
+
+    @pl.when((turn >= 0) & (turn < ups))
+    def _():
+        wu_load(turn).wait()
+
+    def whole_weight():
+        wd_load.start()
+        wd_load.wait()
+
+    ffn_body(turn, ups, whole_weight, lambda: wu[lax.rem(turn, 2)].reshape(-1, FT), attention_out[1], inp,
+             lambda: wo[...], *ffn_in, *ffn_out, *ffn_scratch)
+
+
+def layer_forward(shards, plan, at, edges, shift, start, inproj, bias, qf, kf, lanes, inp, vec, ub, cot, collective):
+    tok, width = start.shape
+    wide = ub.shape[1]
+    ups, begin = wide // FT, width // PAIR
+    low = jnp.bfloat16
+    ins, outs, shapes, scratch = attention_specs(tok, tok + 2 * (edges.shape[1] - 16), width)
+    ffn_ins, ffn_outs, ffn_shapes, ffn_scratch = ffn_specs(tok, width, wide, (2, 2, 4, 2) + shards[2].shape, begin)
+    anywhere = pl.BlockSpec(memory_space=pl.ANY)
+    rows = shards[0].shape[0]
+    return pl.pallas_call(
+        functools.partial(layer_kernel, plan, at, ups, tok, lanes),
+        grid=(begin + ups + tok // ROWS,),
+        in_specs=[anywhere] * 3 + ins + [fixed(tok, width)] + ffn_ins,
+        out_specs=[anywhere] * 3 + outs + ffn_outs,
+        out_shape=full_shapes(shards) + shapes + ffn_shapes,
+        scratch_shapes=scratch + ffn_scratch
+        + [pltpu.VMEM((2, 2, 4, 2, rows, width), low), pltpu.VMEM((2, 2, 2, 4, 2, rows, FT), low),
+           pltpu.SemaphoreType.DMA((3,))] + semaphores(len(plan) * SENDS, len(plan)),
+        compiler_params=pltpu.CompilerParams(
+            vmem_limit_bytes=63 << 20, dimension_semantics=("arbitrary",), collective_id=collective, has_side_effects=True
+        ),
+        name="layer_forward",
+    )(*shards, edges, shift, start, inproj, inproj, inproj, bias, qf, kf, inp, vec, ub, cot)
 
 
 def tn(a, b):
@@ -801,8 +859,8 @@
 
 def back_kernel(plan, count, counts, ups, lanes, *refs):
     hid, gffn, wd, slope, wu, first_low, gsecond, normal_ref, inv_ref, vec, att, wo, feat_ref = refs[:13]
-    down, up_grad, out_grad, up_sum, sums, gin_ref, gatt_ref, feat_out, acc, piece, low_grad = refs[13:24]
-    refs = refs[24:]
+    down, up_grad, out_grad, up_sum, sums, gin_ref, packed, acc, piece, low_grad = refs[13:23]
+    refs = refs[23:]
     step = pl.program_id(0)
     tok, width = gffn.shape
     last = 2 * ups + tok // ROWS - 1
@@ -816,11 +874,11 @@
 
         sends = Sends(send_sem, recv_sem, pos.to)
         job = scatter_job(pos, plan, counts, [dwd], [down], bufs, sends, local_sem, True)
-        schedule(step, ups, last, job, len(plan) + 4)
+        place(step, spread(ups, last, len(plan) + 4), job)
 
     @pl.when(step < ups)
     def _():
-        grad = tn(hid[...], gffn[...]).astype(jnp.bfloat16)
+        grad = nn(hid[...], gffn[...]).astype(jnp.bfloat16)
         if count:
             each = dwd.shape[4]
             for k in range(FT // each):
@@ -848,7 +906,7 @@
                 acc[rows, :] += more
 
         up_sum[...] = jnp.broadcast_to(total, (8, FT))
-        up_grad[...] = tn(first_low[...], piece[...]).astype(jnp.bfloat16)
+        up_grad[...] = nn(first_low[...], piece[...]).astype(jnp.bfloat16)
 
     @pl.when(step == 2 * ups)
     def _():
@@ -867,7 +925,7 @@
         sums[1:2, :] += column_sum(g)
         sums[2:3, :] += column_sum(low.astype(jnp.float32))
         gatt = nt(low, wo[...]).astype(jnp.bfloat16)
-        gatt_ref[...] = gatt
+        packed[:, :width] = gatt
         both = gatt.astype(jnp.float32) * att[rows, :].astype(jnp.float32)
         lane = lax.broadcasted_iota(jnp.int32, (width, PAIR), 1)
         head = lax.broadcasted_iota(jnp.int32, (width, PAIR), 0) // HD
@@ -880,7 +938,7 @@
         lane = lax.broadcasted_iota(jnp.int32, (ROWS, PAIR), 1)
         feat = feat_ref[...]
         feat = jnp.where((lane >= lanes + 48) & (lane < lanes + 64), first, feat)
-        feat_out[...] = jnp.where((lane >= lanes + 64) & (lane < lanes + 80), second, feat)
+        packed[:, width:] = jnp.where((lane >= lanes + 64) & (lane < lanes + 80), second, feat)
 
     @pl.when(step == last)
     def _():
@@ -891,7 +949,7 @@
 
 def ffn_backward(hid, gffn, wd, slope, wu, first_low, gsecond, normal, inv, vec, att, wo, feat, lanes, parts=(), share=0.0,
                  collective=None):
-    tok, wide = hid.shape
+    wide, tok = hid.shape
     width = gffn.shape[1]
     ups, downs = wide // FT, tok // ROWS
     count = 1 if parts else 0
@@ -914,18 +972,101 @@
     return pl.pallas_call(
         functools.partial(back_kernel, plan, count, counts, ups, lanes),
         grid=(2 * ups + downs,),
-        in_specs=[pl.BlockSpec((tok, FT), lambda i: (0, lax.min(i, ups - 1))), whole(tok, width),
+        in_specs=[pl.BlockSpec((FT, tok), lambda i: (lax.min(i, ups - 1), 0)), whole(tok, width),
                   pl.BlockSpec((FT, width), lambda i: (middle(i), 0)), tile,
-                  pl.BlockSpec((width, FT), lambda i: (0, middle(i))), whole(tok, width), row(width), row(width), row(128),
+                  pl.BlockSpec((width, FT), lambda i: (0, middle(i))), whole(width, tok), row(width), row(width), row(128),
                   whole(8, width), whole(tok, width), whole(width, width), row(PAIR)],
         out_specs=[vmem, pl.BlockSpec((width, FT), lambda i: (0, middle(i))), whole(width, width),
-                   pl.BlockSpec((8, FT), lambda i: (0, middle(i))), whole(8, width), row(width), row(width), row(PAIR)],
+                   pl.BlockSpec((8, FT), lambda i: (0, middle(i))), whole(8, width), row(width), row(width + PAIR)],
         out_shape=[down, shape((width, wide), low), shape((width, width), low), shape((8, wide), f32),
-                   shape((8, width), f32), shape((tok, width), f32), shape((tok, width), low), shape((tok, PAIR), low)],
+                   shape((8, width), f32), shape((tok, width), f32), shape((tok, width + PAIR), low)],
         scratch_shapes=scratch,
         compiler_params=pltpu.CompilerParams(vmem_limit_bytes=62 << 20, dimension_semantics=("arbitrary",), **comm),
         name="feed_forward_gradients",
     )(hid, gffn, wd, slope, wu, first_low, gsecond, normal, inv, vec, att, wo, feat)
+
+
+def tail_kernel(plan, counts, *refs):
+    gq, gkv, start, wt, gin, near, far, other, out_ref, in_share, small_share, sums = refs[:12]
+    held, held_small, send_sem, recv_sem, local_sem, bufs = *refs[12:17], refs[17:]
+    step = pl.program_id(0)
+    width = start.shape[1]
+    pos = Place()
+
+    @pl.when(step == 0)
+    def _():
+        meet(pos, False)
+        sums[...] = jnp.zeros_like(sums)
+
+    sends = Sends(send_sem, recv_sem, pos.to)
+    last = 3 + gq.shape[0] // ROWS
+    job = scatter_job(pos, plan, counts, [held, held_small], [in_share, small_share], bufs, sends, local_sem, True, [0, 1, 2, 2])
+
+    def keep(k, grad):
+        for half in range(2):
+            cols = slice(half * width // 2, (half + 1) * width // 2)
+            part = tn(start[...], grad[:, cols]).astype(jnp.bfloat16).reshape(held.shape[:5] + (width // 2,))
+            held[:, :, :, :, :, k * width + half * width // 2 : k * width + (half + 1) * width // 2] = part
+
+    @pl.when(step == last)
+    def _():
+        lines = [other[4:5, :] * sums[1:2, :], sums[1:2, :], sums[2:3, :], sums[3:4, :], near[2:3, :], near[0:1, :],
+                 near[1:2, :], far[2:3, :], far[0:1, :], far[1:2, :]] + [other[k : k + 1, :] for k in range(4)]
+        row = lax.broadcasted_iota(jnp.int32, (128, width), 0)
+        total = jnp.zeros((128, width), jnp.float32)
+        for k, line in enumerate(lines):
+            total = jnp.where(row == k, line, total)
+        held_small[...] = total.T.astype(jnp.bfloat16).reshape(held_small.shape)
+
+    place(step, [1, 2] + [last] * 5, job)
+
+    @pl.when(step == 0)
+    def _():
+        keep(0, gq)
+
+    @pl.when(step == 1)
+    def _():
+        keep(1, gkv.at[0])
+
+    @pl.when(step == last - 1)
+    def _():
+        keep(2, gkv.at[1])
+
+    @pl.when((step >= 2) & (step < last - 1))
+    def _():
+        rows = pl.ds(pl.multiple_of((step - 2) * ROWS, ROWS), ROWS)
+        q, k, v = gq[rows, :], gkv[0, rows, :], gkv[1, rows, :]
+        total = gin[...] + nt(q, wt[:, :width]) + nt(k, wt[:, width : 2 * width]) + nt(v, wt[:, 2 * width :])
+        out_ref[...] = total.astype(jnp.bfloat16)
+        sums[1:2, :] += column_sum(total)
+        sums[2:3, :] += column_sum(q.astype(jnp.float32))
+        sums[3:4, :] += column_sum(v.astype(jnp.float32))
+
+
+def input_gradients(gq, gkv, start, wt, gin, near, far, other, share, collective):
+    tok, width = start.shape
+    rows = width // 32
+    plan = pieces([3 * width, 128], (3, 1), share)
+    bufs = [scatter_bufs(rows, w, at, True) for _, _, w, at in plan]
+    f32, low = jnp.float32, jnp.bfloat16
+    shape = jax.ShapeDtypeStruct
+    vmem = pl.BlockSpec(memory_space=pltpu.VMEM)
+    row = pl.BlockSpec((ROWS, width), lambda i: (lax.max(lax.min(i - 2, tok // ROWS - 1), 0), 0))
+    fix = lambda *s: pl.BlockSpec(s, lambda i: (0,) * len(s), pipeline_mode=pl.Buffered(1))
+    return pl.pallas_call(
+        functools.partial(tail_kernel, plan, [len(b) for b in bufs]),
+        grid=(4 + tok // ROWS,),
+        in_specs=[fix(tok, width), fix(2, tok, width), fix(tok, width), fix(width, 3 * width), row] + [fix(8, width)] * 3,
+        out_specs=[row, vmem, vmem],
+        out_shape=[shape((tok, width), low), shape((rows, 3 * width), f32), shape((rows, 128), f32)],
+        scratch_shapes=[pltpu.VMEM((8, width), f32), pltpu.VMEM((2, 2, 4, 2, rows, 3 * width), low),
+                        pltpu.VMEM((2, 2, 4, 2, rows, 128), low)]
+        + semaphores(len(plan) * SENDS, len(plan)) + sum(bufs, []),
+        compiler_params=pltpu.CompilerParams(
+            vmem_limit_bytes=62 << 20, dimension_semantics=("arbitrary",), collective_id=collective, has_side_effects=True
+        ),
+        name="input_gradients",
+    )(gq, gkv, start, wt, gin, near, far, other)
 
 
 H = 16
@@ -999,7 +1140,6 @@
     places = offset - half + jnp.arange(ext, dtype=jnp.int32)
     item = jnp.where(places >= 0, item_of(ends, places), -1)
     keep = jnp.concatenate([edges[0, half, tok - half :], keep_own, edges[1, half, :half]])
-    edges = edges[:, :half]
     query_feat, key_feat, lane = features(item, places, as_float(keep) > 0.5, lengths.shape[1])
 
     time_value = as_float(timestep[0]) / TSTEPS
@@ -1008,71 +1148,67 @@
     start_low = low(start_vec)
     shift = jnp.pad(jnp.stack([move, time_bias_f]), ((0, 6), (0, 0)))
     bias = jnp.pad(jnp.stack([query_bias_f, jnp.zeros_like(query_bias_f), value_bias_f]), ((0, 5), (0, 0)))
-    if fast:
-        *fulls, projected, attended, feat_own = attn_fwd(
-            edges, shift, start_low, inproj_f, bias, query_feat, key_feat, lane, (outproj, upward_w), (1, 4),
-            0.5, 1,
-        )
-        outproj_f, upward_f = [v.reshape(-1, v.shape[-1]) for v in fulls]
-    else:
-        projected, attended, feat_own = attn_fwd(
-            edges, shift, start_low, inproj_f, bias, query_feat, key_feat, lane
-        )
     vec = jnp.stack([move, time_bias_f, outproj_bias_f, first_gain_f, first_shift_f, downward_bias_f, second_gain_f,
                      second_shift_f])
     up_bias = jnp.broadcast_to(upward_bias_f, (8, hidden))
-    forward = (attended, inputs, outproj_f, upward_f, vec, up_bias, cotangent)
+    attention = (edges, shift, start_low, inproj_f, bias, query_feat, key_feat, lane)
     if fast:
-        downward_f, *results = ffn_forward(downward_w, *forward, (4,), 0.5, 2)
-        downward_f = downward_f.reshape(-1, width)
+        plan = pieces((width, hidden, width), (1, 4, 4), 0.5)
+        at = [0, 1, 2, 3, 4, 5, 6, 7, 9, 11, 13, 15, 16]
+        results = layer_forward(
+            (outproj, upward_w, downward_w), plan, at, *attention, inputs, vec, up_bias, cotangent, 1
+        )
+        outproj_f, upward_f, downward_f = [v.reshape(-1, v.shape[-1]) for v in results[:3]]
+        projected, attended, feat_own, *results = results[3:]
     else:
-        results = ffn_forward(downward_f, *forward)
+        projected, attended, feat_own = attn_fwd(*attention)
+        results = ffn_forward(downward_f, attended, inputs, outproj_f, upward_f, vec, up_bias, cotangent)
     hidden_low, slope, first_normal, first_inv, first_low, layer_out, grad_second_in, grad_ffn_low, sums = results
     grad_second_gain, grad_second_shift, grad_down_bias = sums[0], sums[1], sums[2]
-    sums = jnp.sum(sums[3:6], axis=1)
+    sums_forward, sums = sums, jnp.sum(sums[3:6], axis=1)
     backward = functools.partial(
         ffn_backward, hidden_low, grad_ffn_low, downward_f, slope, upward_f, first_low, grad_second_in, first_normal,
         first_inv, vec, attended, outproj_f, feat_own, lane
     )
-    (grad_down, grad_up_weight, grad_out_weight, grad_up_bias, sums_back, grad_first_in, grad_attended,
-     feat_own) = backward((4,), 0.5, 3) if fast else backward()
+    grad_down, grad_up_weight, grad_out_weight, grad_up_bias, sums_back, grad_first_in, packed = (
+        backward((4,), 0.5, 3) if fast else backward()
+    )
     grad_up_bias = grad_up_bias[0]
     grad_first_gain, grad_first_shift, grad_out_bias = sums_back[0], sums_back[1], sums_back[2]
-    packed = jnp.concatenate([grad_attended, feat_own], axis=1)
     values = jnp.pad(sums[None], ((0, 7), (0, 125)))
     backward = functools.partial(
-        attn_bwd, projected, grad_attended, query_feat, feat_own, key_feat, delta_key(ext, lane), lane, tok
+        attn_bwd, projected, packed, query_feat, key_feat, delta_key(ext, lane), lane, tok
     )
     if fast:
-        edges = jnp.stack([packed[:half], packed[tok - half :]])
+        edges = packed.reshape(2, half, width + PAIR)
         down_share = grad_down
         out_share, up_share, sums, grad_q, grad_kv = backward(
-            edges, values, (grad_out_weight, grad_up_weight), (1, 4), 0.0, 4
+            edges, values, (grad_out_weight, grad_up_weight), (1, 2), 0.0, 4
         )
     else:
         edges = jnp.stack(neighbours(packed[:half], packed[tok - half :]))
         sums, grad_q, grad_kv = backward(edges, lax.psum(values, AXES))
     sums = sums[0, :3]
     branch_rms = jnp.sqrt(sums / (tok * width * lax.axis_size(AXES)))
-    grad_proj_low = jnp.concatenate([grad_q, grad_kv[0], grad_kv[1]], axis=1)
-    grad_in_weight = row_dot(start_low, grad_proj_low)
-    grad_query_bias = jnp.sum(as_float(grad_q), axis=0)
-    grad_value_bias = jnp.sum(as_float(grad_kv[1]), axis=0)
-    grad_start = grad_first_in + nt(grad_proj_low, inproj_f)
-    grad_time_bias = jnp.sum(grad_start, axis=0)
-    grad_time_weight = time_value * grad_time_bias
-    input_grad = low(grad_start)
-
-    small_grads = (grad_time_weight, grad_time_bias, grad_query_bias, grad_value_bias, grad_out_bias, grad_first_gain,
-                   grad_first_shift, grad_down_bias, grad_second_gain, grad_second_shift)
     if fast:
         cols = grad_up_bias.reshape(width // rows, -1, rows).transpose(1, 0, 2).reshape(-1, width)
-        cols = jnp.concatenate([jnp.stack(small_grads), cols]).T
-        cols = jnp.pad(cols, ((0, 0), (0, 128 - cols.shape[1])))
-        in_share, last = scatter_all((low(grad_in_weight), low(cols)), (3, 1), 0.5, 5)
+        other = jnp.concatenate([cols, jnp.broadcast_to(time_value, (4, width))])
+        input_grad, in_share, last = input_gradients(
+            grad_q, grad_kv, start_low, inproj_f, grad_first_in, sums_back, sums_forward, other, 0.5, 5
+        )
         small_shares = [last[:, i] for i in range(SMALL)]
         up_bias_share = last[:, SMALL : SMALL + hidden // width].T.reshape(-1)
     else:
+        grad_proj_low = jnp.concatenate([grad_q, grad_kv[0], grad_kv[1]], axis=1)
+        grad_in_weight = row_dot(start_low, grad_proj_low)
+        grad_query_bias = jnp.sum(as_float(grad_q), axis=0)
+        grad_value_bias = jnp.sum(as_float(grad_kv[1]), axis=0)
+        grad_start = grad_first_in + nt(grad_proj_low, inproj_f)
+        grad_time_bias = jnp.sum(grad_start, axis=0)
+        grad_time_weight = time_value * grad_time_bias
+        input_grad = low(grad_start)
+        small_grads = (grad_time_weight, grad_time_bias, grad_query_bias, grad_value_bias, grad_out_bias, grad_first_gain,
+                       grad_first_shift, grad_down_bias, grad_second_gain, grad_second_shift)
         share = lambda v: lax.psum_scatter(v, AXES, scatter_dimension=0, tiled=True)
         down_share, up_share, out_share, in_share, up_bias_share = map(
             share, map(as_float, (grad_down, grad_up_weight, grad_out_weight, grad_in_weight, grad_up_bias))

time: 591 us -> 523 us (0.88); the launches traced: 581 us -> 519 us
  Pallas kernels: 510 us -> 485 us
  matrix products: 22.9 us -> 0 us
  local copies, waits for them, and re-layouts: 29.6 us -> 20.4 us
    dot_general x2 -> x0, matrix products: 22.9 us -> none  [the longest x1 11.6 us: row_dot(): lax.dot_general(left, right, (((0,), (0,)), ((), ())), preferred_element_...]
    pallas_call x3 -> x2, Pallas kernels: 211 us -> 200 us  [the longest x1 141 us: layer_forward(): pl.pallas_call(functools.partial(layer_kernel, plan, at, ups, tok, lanes)...]
    pallas_call x1, Pallas kernels: 131 us -> 121 us  [attn_bwd(): pl.pallas_call(functools.partial(bwd_kernel, plan, count, counts, tok, la...]
where the time goes in v5:
time: 523 us; the launch traced here: 519 us
  Pallas kernels  485 us (93%)
  local copies, waits for them, and re-layouts  20.4 us (4%)
  other arithmetic  11.7 us (2%)
    pallas_call x1, Pallas kernels, layer_forward(): pl.pallas_call(functools.partial(layer_kernel, plan, at, ups, tok, lanes)...  141 us
    pallas_call x1, Pallas kernels, attn_bwd(): pl.pallas_call(functools.partial(bwd_kernel, plan, count, counts, tok, la...  121 us
    pallas_call x1, Pallas kernels, ffn_backward(): pl.pallas_call(functools.partial(back_kernel, plan, count, counts, ups, l...  86.3 us
    pallas_call x1, Pallas kernels, gather_all(): pl.pallas_call(functools.partial(gather_kernel, plan, count), in_specs=[a...  78.2 us
    pallas_call x1, Pallas kernels, input_gradients(): pl.pallas_call(functools.partial(tail_kernel, plan, [len(b) for b in bufs...  58.7 us

profile of v5, /device:TPU:0, one launch (start us, length us, event | category | flops | bytes accessed | tf_op | source)
XLA Modules:
  0.0 519.1 jit_solution(12147937618879800313)
XLA Ops:
  0.7 1.7 fusion.15
  2.4 0.2 fusion.4
  2.6 0.0 copy-start.19
  2.7 0.0 copy-start.9
  2.7 0.0 copy-start.10
  2.7 0.0 copy-start.13
  2.7 0.0 copy-start.14
  2.7 0.0 copy-start.16
  2.7 0.0 copy-start.17
  2.8 1.5 pad_maximum_fusion.refs_2_
  4.3 0.1 reshape.192
  4.4 0.1 copy.69
  4.5 0.1 copy.70
  4.6 0.1 copy.71
  4.7 0.1 copy.72
  4.8 0.1 copy.73
  4.9 0.1 copy.74
  5.0 0.1 copy.75
  5.1 0.1 copy.76
  5.2 0.1 copy.77
  5.3 0.1 copy.78
  5.4 0.1 copy.79
  5.5 0.1 concatenate.23
  5.7 0.6 pad.21.refs_1_
  6.3 78.2 %gather_weights.1 = (bf16[2,2,4,2,32,3072]{5,4,3,2,1,0:T(8,128)(2,1)}, bf16[2,2,4,2,32,128]{5,4,3,2,1,0:T(8,128)(2,1)}, bf16[2,528,1024]{2,1,0:T(8,128)(2,1)}) custom-call(bf16[32,3072]{1,0:T(8,128)(2,1)} %refs_0_.2, bf16[32,128]{1,0:T(8,128)(2,1)} %pad.21.refs_1_, bf16[2,528,1024]{2,1,0:T(8,128)(2,1)} %pad_maximum_fusion.refs_2_), custom_call_target="tpu_custom_call" | custom-call | tf_op jit(solution)/shard_map/gather_weights/pallas_call | solution.py:514
  84.4 1.0 bitcast_convert_fusion
  85.4 0.2 copy.80
  86.3 0.6 fusion.8
  87.0 0.7 slice_reduce_fusion.13
  87.8 0.1 copy.81
  87.8 0.1 reduce-window.8
  87.9 0.1 reduce
  88.0 0.1 convert_reduce_fusion
  88.2 2.6 select_convert_fusion.refs_11_.refs_10_
  90.8 1.9 add_convert_fusion.refs_5_.refs_2_
  92.7 0.1 pad.33.clone
  92.8 0.1 pad_maximum_fusion.2
  92.9 0.6 pad.24.refs_9_
  93.5 2.1 select_convert_fusion.1.refs_10_.refs_8_
  95.6 0.1 reshape.197
  95.7 0.1 reshape.198
  95.8 0.7 broadcast_in_dim.133.refs_14_
  96.5 141.4 %layer_forward.1 = (bf16[2,2,4,2,32,1024]{5,4,3,2,1,0:T(8,128)(2,1)}, bf16[2,2,4,2,32,4096]{5,4,3,2,1,0:T(8,128)(2,1)}, bf16[2,2,4,2,128,1024]{5,4,3,2,1,0:T(8,1...) custom-call(bf16[32,1024]{1,0:T(8,128)(2,1)} %refs_0_.3, ...), custom_call_target="tpu_custom_call" | custom-call | tf_op jit(solution)/shard_map/layer_forward/pallas_call | solution.py:840
  237.9 86.3 %feed_forward_gradients.1 = (f32[128,1024]{1,0:T(8,128)}, bf16[1024,4096]{1,0:T(8,128)(2,1)}, bf16[1024,1024]{1,0:T(8,128)(2,1)}, f32[8,4096]{1,0:T(8,128)}, f32...) custom-call(bf16[4096,1024]{1,0:T(8,128)(2,1)} %get-tuple-element.55.refs_0_, ...), custom_call_target="tpu_custom_call" | custom-call | tf_op jit(solution)/shard_map/feed_forward_gradients/pallas_call | solution.py:972
  324.2 0.1 slice_reduce_fusion.11
  324.3 0.6 pad.25.refs_3_
  324.9 0.9 broadcast_in_dim.135.refs_11_
  325.8 120.6 %attention_gradients.1 = (f32[32,1024]{1,0:T(8,128)}, f32[32,4096]{1,0:T(8,128)}, f32[8,128]{1,0:T(8,128)}, bf16[1024,1024]{1,0:T(8,128)(2,1)}, bf16[2,1024,1024]{2,1,0:T(8,128)(2,1)}) custom-call(bf16[2,2,4,2,32,1024]{5,4,3,2,1,0:T(8,128)(2,1)} %bitcast.50, bf16[2,2,4,2,32,4096]{5,4,3,2,1,0:T(8,128)(2,1)} %bitcast.47, bf16[2,512,1152]{2,1,0:T(8,128)(2,1)} %bitcast.46, ...), custom_call_target="tpu_custom_call" | custom-call | tf_op jit(solution)/shard_map/attention_gradients/pallas_call | solution.py:266
  446.4 0.9 slice_reduce_fusion.10
  447.3 0.1 reshape_squeeze.3
  447.4 0.1 reshape.205
  447.5 0.6 concatenate.29.refs_7_
  448.1 58.7 %input_gradients.1 = (bf16[1024,1024]{1,0:T(8,128)(2,1)}, f32[32,3072]{1,0:T(8,128)}, f32[32,128]{1,0:T(8,128)}) custom-call(bf16[1024,1024]{1,0:T(8,128)(2,1)} %get-tuple-element.72.refs_0_, bf16[2,1024,1024]{2,1,0:T(8,128)(2,1)} %get-tuple-element.73.refs_1_, bf16[1024,1024]{1,0:T(8,128)(2,1)} %add_convert_fusion.refs_5_.refs_2_, ...), custom_call_target="tpu_custom_call" | custom-call | tf_op jit(solution)/shard_map/input_gradients/pallas_call | solution.py:1056
  506.8 0.8 slice_bitcast_fusion
  507.6 0.1 copy.84
  507.7 0.6 reshape.206
  508.3 2.0 slice_reduce_fusion
  510.3 1.2 sqrt_bitcast_fusion
  511.5 3.1 copy.96
  514.6 1.3 copy.97
  515.9 0.7 copy.98
  516.6 0.7 copy.99
  517.3 0.8 copy.100
  518.1 0.8 copy.101
  (47 shorter events, 0.2 us)
Async XLA Ops:
  0.7 1.7 copy-start.7
  2.6 1.7 copy-start.19
  2.6 1.9 copy-start.8
  2.7 1.9 copy-start.9
  2.7 2.0 copy-start.10
  2.7 2.1 copy-start.11
  2.7 2.2 copy-start.12
  2.7 2.3 copy-start.13
  2.7 2.4 copy-start.14
  2.7 2.5 copy-start.15
  2.7 2.6 copy-start.16
  2.7 2.7 copy-start.17
  6.3 81.5 %copy-start.18 = (s32[1,32]{1,0:T(1,128)S(1)}, s32[1,32]{1,0:T(1,128)}, u32[]{:S(2)}) copy-start(s32[1,32]{1,0:T(1,128)} %param.23) | copy-start | bytes 388
  6.3 84.5 %copy-start = (bf16[1024,1024]{1,0:T(8,128)(2,1)S(1)}, bf16[1024,1024]{1,0:T(8,128)(2,1)}, u32[]{:S(2)}) copy-start(bf16[1024,1024]{1,0:T(8,128)(2,1)} %refs_12_.1) | copy-start | bytes 6291460
  237.9 86.3 %copy-start.6 = (f32[8,1024]{1,0:T(8,128)S(1)}, f32[8,1024]{1,0:T(8,128)}, u32[]{:S(2)}) copy-start(f32[8,1024]{1,0:T(8,128)} %get-tuple-element.70.refs_6_) | copy-start | bytes 98308
  508.3 6.2 %copy-start.1 = (bf16[1024,1024]{1,0:T(8,128)(2,1)S(1)}, bf16[1024,1024]{1,0:T(8,128)(2,1)}, u32[]{:S(2)}) copy-start(bf16[1024,1024]{1,0:T(8,128)(2,1)} %get-tuple-element.129) | copy-start | bytes 6291460
  514.6 1.3 copy-start.4
  514.6 2.1 copy-start.5
  514.6 2.7 copy-start.3
  514.6 3.5 copy-start.2

commit v6 on v5

--- a/solution.py
+++ b/solution.py
@@ -155,7 +155,7 @@
 
         sends = Sends(send_sem, recv_sem, pos.to)
 
-        at = spread(0, BWD_STEPS - 1, len(plan) + 4)
+        at = [0, 3, 6, 8, 11, 13, 15]
         ready = max(i for i, s in enumerate(at) if s <= pairs)
 
         def work():
@@ -1000,7 +1000,7 @@
 
     sends = Sends(send_sem, recv_sem, pos.to)
     last = 3 + gq.shape[0] // ROWS
-    job = scatter_job(pos, plan, counts, [held, held_small], [in_share, small_share], bufs, sends, local_sem, True, [0, 1, 2, 2])
+    job = scatter_job(pos, plan, counts, [held, held_small], [in_share, small_share], bufs, sends, local_sem, True, [0, 1, 3, 3])
 
     def keep(k, grad):
         for half in range(2):
@@ -1018,7 +1018,7 @@
             total = jnp.where(row == k, line, total)
         held_small[...] = total.T.astype(jnp.bfloat16).reshape(held_small.shape)
 
-    place(step, [1, 2] + [last] * 5, job)
+    place(step, [1, 2, 4] + [last] * 5, job)
 
     @pl.when(step == 0)
     def _():
@@ -1154,7 +1154,7 @@
     attention = (edges, shift, start_low, inproj_f, bias, query_feat, key_feat, lane)
     if fast:
         plan = pieces((width, hidden, width), (1, 4, 4), 0.5)
-        at = [0, 1, 2, 3, 4, 5, 6, 7, 9, 11, 13, 15, 16]
+        at = [0, 1, 2, 3, 4, 5, 7, 8, 9, 11, 13, 15, 16]
         results = layer_forward(
             (outproj, upward_w, downward_w), plan, at, *attention, inputs, vec, up_bias, cotangent, 1
         )

time: 523 us -> 513 us (0.981)
  Pallas kernels: 485 us -> 475 us
    pallas_call x1, Pallas kernels: 58.7 us -> 51.4 us  [input_gradients(): pl.pallas_call(functools.partial(tail_kernel, plan, [len(b) for b in bufs...]
where the time goes in v6:
time: 513 us; the launch traced here: 510 us
  Pallas kernels  475 us (93%)
  local copies, waits for them, and re-layouts  20.4 us (4%)
  other arithmetic  11.7 us (2%)
    pallas_call x1, Pallas kernels, layer_forward(): pl.pallas_call(functools.partial(layer_kernel, plan, at, ups, tok, lanes)...  140 us
    pallas_call x1, Pallas kernels, attn_bwd(): pl.pallas_call(functools.partial(bwd_kernel, plan, count, counts, tok, la...  119 us
    pallas_call x1, Pallas kernels, ffn_backward(): pl.pallas_call(functools.partial(back_kernel, plan, count, counts, ups, l...  86.6 us
    pallas_call x1, Pallas kernels, gather_all(): pl.pallas_call(functools.partial(gather_kernel, plan, count), in_specs=[a...  78.2 us
    pallas_call x1, Pallas kernels, input_gradients(): pl.pallas_call(functools.partial(tail_kernel, plan, [len(b) for b in bufs...  51.4 us

profile of v6, /device:TPU:0, one launch (start us, length us, event | category | flops | bytes accessed | tf_op | source)
XLA Modules:
  0.0 509.5 jit_solution(17756035849615262922)
XLA Ops:
  0.7 1.7 fusion.15
  2.4 0.2 fusion.4
  2.6 0.0 copy-start.19
  2.6 0.0 copy-start.8
  2.7 0.0 copy-start.9
  2.7 0.0 copy-start.10
  2.7 0.0 copy-start.11
  2.7 0.0 copy-start.14
  2.7 0.0 copy-start.15
  2.8 1.5 pad_maximum_fusion.refs_2_
  4.3 0.1 reshape.192
  4.4 0.1 copy.69
  4.5 0.1 copy.70
  4.6 0.1 copy.71
  4.7 0.1 copy.72
  4.8 0.1 copy.73
  4.9 0.1 copy.74
  5.0 0.1 copy.75
  5.1 0.1 copy.76
  5.2 0.1 copy.77
  5.3 0.1 copy.78
  5.4 0.1 copy.79
  5.5 0.1 concatenate.23
  5.7 0.6 pad.21.refs_1_
  6.3 78.2 %gather_weights.1 = (bf16[2,2,4,2,32,3072]{5,4,3,2,1,0:T(8,128)(2,1)}, bf16[2,2,4,2,32,128]{5,4,3,2,1,0:T(8,128)(2,1)}, bf16[2,528,1024]{2,1,0:T(8,128)(2,1)}) custom-call(bf16[32,3072]{1,0:T(8,128)(2,1)} %refs_0_.2, bf16[32,128]{1,0:T(8,128)(2,1)} %pad.21.refs_1_, bf16[2,528,1024]{2,1,0:T(8,128)(2,1)} %pad_maximum_fusion.refs_2_), custom_call_target="tpu_custom_call" | custom-call | tf_op jit(solution)/shard_map/gather_weights/pallas_call | solution.py:514
  84.4 1.0 bitcast_convert_fusion
  85.4 0.2 copy.80
  86.3 0.6 fusion.8
  87.0 0.7 slice_reduce_fusion.13
  87.8 0.1 copy.81
  87.8 0.1 reduce-window.8
  87.9 0.1 reduce
  88.0 0.1 convert_reduce_fusion
  88.2 2.6 select_convert_fusion.refs_11_.refs_10_
  90.8 1.9 add_convert_fusion.refs_5_.refs_2_
  92.7 0.1 pad.33.clone
  92.8 0.1 pad_maximum_fusion.2
  92.9 0.6 pad.24.refs_9_
  93.5 2.1 select_convert_fusion.1.refs_10_.refs_8_
  95.6 0.1 reshape.197
  95.7 0.1 reshape.198
  95.8 0.7 broadcast_in_dim.133.refs_14_
  96.5 140.1 %layer_forward.1 = (bf16[2,2,4,2,32,1024]{5,4,3,2,1,0:T(8,128)(2,1)}, bf16[2,2,4,2,32,4096]{5,4,3,2,1,0:T(8,128)(2,1)}, bf16[2,2,4,2,128,1024]{5,4,3,2,1,0:T(8,1...) custom-call(bf16[32,1024]{1,0:T(8,128)(2,1)} %refs_0_.3, ...), custom_call_target="tpu_custom_call" | custom-call | tf_op jit(solution)/shard_map/layer_forward/pallas_call | solution.py:840
  236.6 86.6 %feed_forward_gradients.1 = (f32[128,1024]{1,0:T(8,128)}, bf16[1024,4096]{1,0:T(8,128)(2,1)}, bf16[1024,1024]{1,0:T(8,128)(2,1)}, f32[8,4096]{1,0:T(8,128)}, f32...) custom-call(bf16[4096,1024]{1,0:T(8,128)(2,1)} %get-tuple-element.55.refs_0_, ...), custom_call_target="tpu_custom_call" | custom-call | tf_op jit(solution)/shard_map/feed_forward_gradients/pallas_call | solution.py:972
  323.1 0.1 slice_reduce_fusion.11
  323.3 0.6 pad.25.refs_3_
  323.9 0.9 broadcast_in_dim.135.refs_11_
  324.7 119.3 %attention_gradients.1 = (f32[32,1024]{1,0:T(8,128)}, f32[32,4096]{1,0:T(8,128)}, f32[8,128]{1,0:T(8,128)}, bf16[1024,1024]{1,0:T(8,128)(2,1)}, bf16[2,1024,1024]{2,1,0:T(8,128)(2,1)}) custom-call(bf16[2,2,4,2,32,1024]{5,4,3,2,1,0:T(8,128)(2,1)} %bitcast.50, bf16[2,2,4,2,32,4096]{5,4,3,2,1,0:T(8,128)(2,1)} %bitcast.47, bf16[2,512,1152]{2,1,0:T(8,128)(2,1)} %bitcast.46, ...), custom_call_target="tpu_custom_call" | custom-call | tf_op jit(solution)/shard_map/attention_gradients/pallas_call | solution.py:266
  444.0 0.9 slice_reduce_fusion.10
  445.0 0.1 reshape_squeeze.3
  445.1 0.1 reshape.205
  445.2 0.6 concatenate.29.refs_7_
  445.8 51.4 %input_gradients.1 = (bf16[1024,1024]{1,0:T(8,128)(2,1)}, f32[32,3072]{1,0:T(8,128)}, f32[32,128]{1,0:T(8,128)}) custom-call(bf16[1024,1024]{1,0:T(8,128)(2,1)} %get-tuple-element.72.refs_0_, bf16[2,1024,1024]{2,1,0:T(8,128)(2,1)} %get-tuple-element.73.refs_1_, bf16[1024,1024]{1,0:T(8,128)(2,1)} %add_convert_fusion.refs_5_.refs_2_, ...), custom_call_target="tpu_custom_call" | custom-call | tf_op jit(solution)/shard_map/input_gradients/pallas_call | solution.py:1056
  497.2 0.8 slice_bitcast_fusion
  498.0 0.1 copy.84
  498.1 0.6 reshape.206
  498.7 2.0 slice_reduce_fusion
  500.7 1.2 sqrt_bitcast_fusion
  501.9 3.1 copy.96
  505.0 1.3 copy.97
  506.3 0.7 copy.98
  507.1 0.7 copy.99
  507.7 0.8 copy.100
  508.5 0.8 copy.101
  (47 shorter events, 0.2 us)
Async XLA Ops:
  0.7 1.7 copy-start.7
  2.6 1.7 copy-start.19
  2.6 1.9 copy-start.8
  2.7 1.9 copy-start.9
  2.7 2.0 copy-start.10
  2.7 2.1 copy-start.11
  2.7 2.2 copy-start.12
  2.7 2.3 copy-start.13
  2.7 2.4 copy-start.14
  2.7 2.5 copy-start.15
  2.7 2.6 copy-start.16
  2.7 2.7 copy-start.17
  6.3 81.5 %copy-start.18 = (s32[1,32]{1,0:T(1,128)S(1)}, s32[1,32]{1,0:T(1,128)}, u32[]{:S(2)}) copy-start(s32[1,32]{1,0:T(1,128)} %param.23) | copy-start | bytes 388
  6.3 84.5 %copy-start = (bf16[1024,1024]{1,0:T(8,128)(2,1)S(1)}, bf16[1024,1024]{1,0:T(8,128)(2,1)}, u32[]{:S(2)}) copy-start(bf16[1024,1024]{1,0:T(8,128)(2,1)} %refs_12_.1) | copy-start | bytes 6291460
  236.6 86.6 %copy-start.6 = (f32[8,1024]{1,0:T(8,128)S(1)}, f32[8,1024]{1,0:T(8,128)}, u32[]{:S(2)}) copy-start(f32[8,1024]{1,0:T(8,128)} %get-tuple-element.70.refs_6_) | copy-start | bytes 98308
  498.7 6.2 %copy-start.1 = (bf16[1024,1024]{1,0:T(8,128)(2,1)S(1)}, bf16[1024,1024]{1,0:T(8,128)(2,1)}, u32[]{:S(2)}) copy-start(bf16[1024,1024]{1,0:T(8,128)(2,1)} %get-tuple-element.129) | copy-start | bytes 6291460
  505.0 1.3 copy-start.4
  505.0 2.1 copy-start.5
  505.0 2.7 copy-start.3
  505.0 3.5 copy-start.2
